TPU v7x, 32 devices: a whole 2x2x4 slice. The times are simulated.
32 devices in a mesh: dp: 8 (over y, x, core), expert: 4 (over z).
Axes of the slice: x: 2, y: 2, z: 4, core: 2. Of those that a mesh axis runs over, the one named last changes fastest.
Arguments:
- tokens: bfloat16 [32768, 768], P(('dp', 'expert')), may hold values from -6 to 6
- bucket: int32 [128], P(('dp', 'expert')), may hold values from 0 to 49, as said below
- image_length: int32 [128], P(('dp', 'expert')), may hold values from 256 to 1024, as said below
- routes: int32 [32768, 2], P(('dp', 'expert')), may hold values from 0 to 7, all different within a row; in each aligned block of 1024 rows (0 to 1023, 1024 to 2047, ...) at most 288 rows name the same one
- cotangent: bfloat16 [32768, 768], P(('dp', 'expert')), may hold values from -6 to 6
- w_qkv: bfloat16 [768, 2304], P(('dp', 'expert')), may hold values from -0.21875 to 0.21875
- w_out: bfloat16 [768, 768], P(('dp', 'expert')), may hold values from -0.875 to 0.875
- w_ada: bfloat16 [768, 4608], P(('dp', 'expert')), may hold values from -0.21875 to 0.21875
- b_ada: bfloat16 [4608], P(('dp', 'expert')), may hold values from -3 to 3
- w_router: bfloat16 [768, 8], P(('dp', 'expert')), may hold values from -0.15625 to 0.15625
- w_shared_in: bfloat16 [768, 3072], P(('dp', 'expert')), may hold values from -0.21875 to 0.21875
- w_shared_out: bfloat16 [3072, 768], P(('dp', 'expert')), may hold values from -0.109375 to 0.109375
- w_expert_in: bfloat16 [8, 768, 3072], P('expert'), may hold values from -0.21875 to 0.21875
- w_expert_out: bfloat16 [8, 3072, 768], P('expert'), may hold values from -0.109375 to 0.109375
Outputs:
- block_out: bfloat16 [32768, 768], P(('dp', 'expert'))
- grad_tokens: bfloat16 [32768, 768], P(('dp', 'expert'))
- grad_w_qkv: float32 [768, 2304], P('dp', 'expert')
- grad_w_out: float32 [768, 768], P('dp', 'expert')
- grad_w_ada: float32 [768, 4608], P('dp', 'expert')
- grad_b_ada: float32 [4608], P(('dp', 'expert'))
- grad_w_router: float32 [768, 8], P('dp', 'expert')
- grad_w_shared_in: float32 [768, 3072], P('dp', 'expert')
- grad_w_shared_out: float32 [3072, 768], P('dp', 'expert')
- grad_w_expert_in: float32 [8, 768, 3072], P('expert', 'dp')
- grad_w_expert_out: float32 [8, 3072, 768], P('expert', 'dp')
Inputs may be any that keep to these rules, and one draw needn't show every extreme that they name: `image_length`: each group of four consecutive blocks (one device's patches) carries one value: 1024 where it is one image, 256 where it is four; both kinds occur in every draw. The four blocks of one 1024-patch image carry the same bucket. `routes`: the two experts of a patch differ; within the 1024 patches of one device no expert is named more than 288 times.
All inputs are finite; a program needn't handle non-finite values.
Results may differ from a plain program's by a relative error of at most 0.02.
Values may be sent and summed in bfloat16 or wider, within the bound.
A program may use at most 384 MiB of HBM per device.

v0:
```python
import math

import jax
import jax.numpy as jnp
from jax import lax
from jax.sharding import PartitionSpec as P

D = 768
HEADS = 12
HEAD_DIM = 64
EXPERTS = 8
LONG = 1024
SHORT = 256
CAP = 288
BUCKETS = 50


HIGHEST = lax.Precision.HIGHEST


def product(left_side, right_side):
    return jnp.dot(left_side, right_side, preferred_element_type=jnp.float32)


def embed(bucket):
    time_values = bucket.astype(jnp.float32) * (1000.0 / BUCKETS)
    half_width = D // 2
    frequency = jnp.exp(-math.log(10000.0) * jnp.arange(half_width, dtype=jnp.float32) / half_width)
    angles = time_values[:, None] * frequency[None, :]
    return jnp.concatenate([jnp.cos(angles), jnp.sin(angles)], axis=1)


def normalize(values):
    center = values - jnp.mean(values, axis=-1, keepdims=True)
    variance = jnp.mean(center * center, axis=-1, keepdims=True)
    inverse = lax.rsqrt(variance + 1e-06)
    return (center * inverse, inverse)


def norm_back(grad_hat, hat_values, inverse):
    return inverse * (
        grad_hat
        - jnp.mean(grad_hat, axis=-1, keepdims=True)
        - hat_values * jnp.mean(grad_hat * hat_values, axis=-1, keepdims=True)
    )


def expand(block_rows):
    return jnp.repeat(block_rows, SHORT, axis=0)


def block_sums(values):
    return jnp.sum(values.reshape(LONG // SHORT, SHORT, D), axis=1)


def dispatch_slots(routes):
    flat_routes = routes.reshape(-1)
    chosen_hot = (flat_routes[:, None] == jnp.arange(EXPERTS, dtype=jnp.int32)[None, :]).astype(
        jnp.int32
    )
    before = jnp.cumsum(chosen_hot, axis=0) - chosen_hot
    slot_index = flat_routes * CAP + jnp.sum(before * chosen_hot, axis=1)
    slot_owner = (
        jnp.full((EXPERTS * CAP,), 2 * LONG, jnp.int32)
        .at[slot_index]
        .set(jnp.arange(2 * LONG, dtype=jnp.int32))
    )
    return (slot_index, slot_owner)


def grouped(values, groups):
    return values.reshape(groups, LONG // groups, HEADS, HEAD_DIM)


def attend(queries, key_rows, value_rows, groups):
    scores = jnp.einsum(
        "gqhd,gkhd->ghqk",
        grouped(queries, groups),
        grouped(key_rows, groups),
        preferred_element_type=jnp.float32,
    ) * HEAD_DIM ** (-0.5)
    row_peak = jnp.max(scores, axis=-1, keepdims=True)
    exp_scores = jnp.exp(scores - row_peak)
    row_total = jnp.sum(exp_scores, axis=-1, keepdims=True)
    softmax_rows = (exp_scores / row_total).astype(jnp.bfloat16)
    attended = jnp.einsum(
        "ghqk,gkhd->gqhd",
        softmax_rows,
        grouped(value_rows, groups),
        preferred_element_type=jnp.float32,
    ).reshape(LONG, D)
    log_total = (row_peak + jnp.log(row_total))[..., 0]
    return (attended, jnp.transpose(log_total, (0, 2, 1)).reshape(LONG, HEADS))


def attend_back(queries, key_rows, value_rows, grad_attended, log_total, groups):
    query_set = grouped(queries, groups)
    key_set = grouped(key_rows, groups)
    value_set = grouped(value_rows, groups)
    grad_set = grouped(grad_attended, groups)
    scores = jnp.einsum(
        "gqhd,gkhd->ghqk", query_set, key_set, preferred_element_type=jnp.float32
    ) * HEAD_DIM ** (-0.5)
    totals = jnp.transpose(log_total.reshape(groups, LONG // groups, HEADS), (0, 2, 1))[..., None]
    soft_exact = jnp.exp(scores - totals)
    grad_values = jnp.einsum(
        "ghqk,gqhd->gkhd",
        soft_exact.astype(jnp.bfloat16),
        grad_set,
        preferred_element_type=jnp.float32,
    )
    grad_soft = jnp.einsum(
        "gqhd,gkhd->ghqk", grad_set, value_set, preferred_element_type=jnp.float32
    )
    delta = jnp.sum(soft_exact * grad_soft, axis=-1, keepdims=True)
    grad_scores = (soft_exact * (grad_soft - delta)).astype(jnp.bfloat16)
    grad_queries = jnp.einsum(
        "ghqk,gkhd->gqhd", grad_scores, key_set, preferred_element_type=jnp.float32
    ) * HEAD_DIM ** (-0.5)
    grad_keys = jnp.einsum(
        "ghqk,gqhd->gkhd", grad_scores, query_set, preferred_element_type=jnp.float32
    ) * HEAD_DIM ** (-0.5)
    return jnp.concatenate(
        [grad_queries.reshape(LONG, D), grad_keys.reshape(LONG, D), grad_values.reshape(LONG, D)],
        axis=1,
    )


def bias_order(grad_bias):
    lane_count = lax.axis_size("expert")
    group_count = lax.axis_size("dp")
    share = grad_bias.shape[0] // (lane_count * group_count)
    arranged = grad_bias.reshape(group_count, lane_count, share)
    return jnp.transpose(arranged, (1, 0, 2)).reshape(lane_count, group_count * share)


def body(
    tokens,
    bucket,
    image_length,
    routes,
    cotangent,
    w_qkv,
    w_out,
    w_ada,
    b_ada,
    w_router,
    w_shared_in,
    w_shared_out,
    w_expert_in,
    w_expert_out,
):
    w_qkv, w_out, w_ada, b_ada, w_router, w_shared_in, w_shared_out = (
        lax.all_gather(w_qkv, ("dp", "expert"), axis=0, tiled=True),
        lax.all_gather(w_out, ("dp", "expert"), axis=0, tiled=True),
        lax.all_gather(w_ada, ("dp", "expert"), axis=0, tiled=True),
        lax.all_gather(b_ada, ("dp", "expert"), axis=0, tiled=True),
        lax.all_gather(w_router, ("dp", "expert"), axis=0, tiled=True),
        lax.all_gather(w_shared_in, ("dp", "expert"), axis=0, tiled=True),
        lax.all_gather(w_shared_out, ("dp", "expert"), axis=0, tiled=True),
    )
    condition = jax.nn.silu(embed(bucket)).astype(jnp.bfloat16)
    modulation = product(condition, w_ada) + b_ada.astype(jnp.float32)
    shift_one, scale_one, gate_one, shift_two, scale_two, gate_two = [
        expand(modulation[:, span_index * D : (span_index + 1) * D]) for span_index in range(6)
    ]
    inputs_full = tokens.astype(jnp.float32)
    hat_one, inverse_one = normalize(inputs_full)
    normed_one = (hat_one * (1.0 + scale_one) + shift_one).astype(jnp.bfloat16)
    projected = product(normed_one, w_qkv).astype(jnp.bfloat16)
    queries = projected[:, :D].reshape(LONG, HEADS, HEAD_DIM)
    key_rows = projected[:, D : 2 * D].reshape(LONG, HEADS, HEAD_DIM)
    value_rows = projected[:, 2 * D :].reshape(LONG, HEADS, HEAD_DIM)
    is_long = image_length[0] == LONG
    attended, log_total = lax.cond(
        is_long,
        lambda: attend(queries, key_rows, value_rows, 1),
        lambda: attend(queries, key_rows, value_rows, LONG // SHORT),
    )
    attended_low = attended.astype(jnp.bfloat16)
    branch_att = product(attended_low, w_out)
    hidden_one = inputs_full + gate_one * branch_att
    hat_two, inverse_two = normalize(hidden_one)
    normed_two = (hat_two * (1.0 + scale_two) + shift_two).astype(jnp.bfloat16)
    pre_shared = product(normed_two, w_shared_in)
    gelu_shared = jax.nn.gelu(pre_shared).astype(jnp.bfloat16)
    shared = product(gelu_shared, w_shared_out)
    logits = product(normed_two, w_router)
    choose = (routes[:, :, None] == jnp.arange(EXPERTS, dtype=jnp.int32)[None, None, :]).astype(
        jnp.float32
    )
    picked_logits = jnp.sum(logits[:, None, :] * choose, axis=-1)
    gate_weights = jax.nn.softmax(picked_logits, axis=-1)
    slot_index, slot_owner = dispatch_slots(routes)
    padded = jnp.concatenate([normed_two, jnp.zeros((1, D), jnp.bfloat16)], axis=0)
    dispatched = padded[slot_owner // 2].reshape(EXPERTS, 1, CAP, D)
    arrived = lax.all_to_all(dispatched, "expert", split_axis=0, concat_axis=1, tiled=True)
    pre_rows = jnp.einsum(
        "encd,edf->encf", arrived, w_expert_in, preferred_element_type=jnp.float32
    )
    out_rows = jnp.einsum(
        "encf,efd->encd",
        jax.nn.gelu(pre_rows).astype(jnp.bfloat16),
        w_expert_out,
        preferred_element_type=jnp.float32,
    ).astype(jnp.bfloat16)
    back_rows = lax.all_to_all(out_rows, "expert", split_axis=1, concat_axis=0, tiled=True)
    back_rows, pre_expert, arrived = (back_rows, pre_rows, arrived)
    returned = back_rows.reshape(EXPERTS * CAP, D)
    pair_slots = slot_index.reshape(LONG, 2)
    picked = returned[pair_slots].astype(jnp.float32)
    mixture = jnp.sum(gate_weights[:, :, None] * picked, axis=1)
    branch_mlp = shared + mixture
    result = hidden_one + gate_two * branch_mlp
    grad_out = cotangent.astype(jnp.float32)
    grad_mlp = (gate_two * grad_out).astype(jnp.bfloat16)
    grad_mlp_full = grad_mlp.astype(jnp.float32)
    grad_shared_out = jnp.einsum(
        "lf,ld->fd", gelu_shared, grad_mlp, preferred_element_type=jnp.float32
    )
    grad_gelu = product(grad_mlp, w_shared_out.T)
    unused_shared, gelu_back = jax.vjp(jax.nn.gelu, pre_shared)
    grad_pre_shared = gelu_back(grad_gelu)[0].astype(jnp.bfloat16)
    grad_shared_in = jnp.einsum(
        "ld,lf->df", normed_two, grad_pre_shared, preferred_element_type=jnp.float32
    )
    grad_normed_two = product(grad_pre_shared, w_shared_in.T)
    grad_gates = jnp.sum(grad_mlp_full[:, None, :] * picked, axis=-1)
    grad_picked = gate_weights * (
        grad_gates - jnp.sum(gate_weights * grad_gates, axis=1, keepdims=True)
    )
    grad_logits = jnp.sum(grad_picked[:, :, None] * choose, axis=1)
    grad_router = jnp.einsum(
        "ld,le->de", normed_two.astype(jnp.float32), grad_logits, precision=HIGHEST
    )
    grad_normed_two = grad_normed_two + jnp.dot(
        grad_logits, w_router.astype(jnp.float32).T, precision=HIGHEST
    )
    gate_flat = jnp.concatenate([gate_weights.reshape(-1), jnp.zeros((1,), jnp.float32)])
    grad_padded = jnp.concatenate([grad_mlp_full, jnp.zeros((1, D), jnp.float32)], axis=0)
    grad_sent = (
        (gate_flat[slot_owner][:, None] * grad_padded[slot_owner // 2])
        .astype(jnp.bfloat16)
        .reshape(EXPERTS, 1, CAP, D)
    )
    grad_arrived = lax.all_to_all(grad_sent, "expert", split_axis=0, concat_axis=1, tiled=True)
    unused_expert, expert_back = jax.vjp(jax.nn.gelu, pre_expert)
    grad_expert_out = jnp.einsum(
        "encf,encd->efd",
        unused_expert.astype(jnp.bfloat16),
        grad_arrived,
        preferred_element_type=jnp.float32,
    )
    grad_gelu_expert = jnp.einsum(
        "encd,efd->encf", grad_arrived, w_expert_out, preferred_element_type=jnp.float32
    )
    grad_pre_expert = expert_back(grad_gelu_expert)[0].astype(jnp.bfloat16)
    grad_expert_in = jnp.einsum(
        "encd,encf->edf", arrived, grad_pre_expert, preferred_element_type=jnp.float32
    )
    grad_back = jnp.einsum(
        "encf,edf->encd", grad_pre_expert, w_expert_in, preferred_element_type=jnp.float32
    ).astype(jnp.bfloat16)
    grad_home = lax.all_to_all(
        grad_back, "expert", split_axis=1, concat_axis=0, tiled=True
    ).reshape(EXPERTS * CAP, D)
    grad_normed_two = grad_normed_two + jnp.sum(grad_home[pair_slots].astype(jnp.float32), axis=1)
    grad_expert_in, grad_expert_out = (
        lax.psum_scatter(
            grad_expert_in.astype(jnp.bfloat16), "dp", scatter_dimension=1, tiled=True
        ).astype(jnp.float32),
        lax.psum_scatter(
            grad_expert_out.astype(jnp.bfloat16), "dp", scatter_dimension=1, tiled=True
        ).astype(jnp.float32),
    )
    grad_hidden_one = grad_out + norm_back(
        grad_normed_two * (1.0 + scale_two), hat_two, inverse_two
    )
    grad_att = (gate_one * grad_hidden_one).astype(jnp.bfloat16)
    grad_w_out = jnp.einsum("ld,le->de", attended_low, grad_att, preferred_element_type=jnp.float32)
    grad_attended = product(grad_att, w_out.T).astype(jnp.bfloat16).reshape(LONG, HEADS, HEAD_DIM)
    grad_projected = lax.cond(
        is_long,
        lambda: attend_back(queries, key_rows, value_rows, grad_attended, log_total, 1),
        lambda: attend_back(queries, key_rows, value_rows, grad_attended, log_total, LONG // SHORT),
    ).astype(jnp.bfloat16)
    grad_w_qkv = jnp.einsum(
        "ld,le->de", normed_one, grad_projected, preferred_element_type=jnp.float32
    )
    grad_normed_one = product(grad_projected, w_qkv.T)
    grad_input = grad_hidden_one + norm_back(
        grad_normed_one * (1.0 + scale_one), hat_one, inverse_one
    )
    grad_modulation = jnp.concatenate(
        [
            block_sums(grad_normed_one),
            block_sums(grad_normed_one * hat_one),
            block_sums(grad_hidden_one * branch_att),
            block_sums(grad_normed_two),
            block_sums(grad_normed_two * hat_two),
            block_sums(grad_out * branch_mlp),
        ],
        axis=1,
    )
    grad_w_ada = jnp.einsum(
        "bd,be->de", condition.astype(jnp.float32), grad_modulation, precision=HIGHEST
    )
    grad_b_lanes = bias_order(jnp.sum(grad_modulation, axis=0))
    (
        grad_w_qkv,
        grad_w_out,
        grad_w_ada,
        grad_b_lanes,
        grad_router,
        grad_shared_in,
        grad_shared_out,
    ) = (
        lax.psum_scatter(
            grad_w_qkv.astype(jnp.bfloat16), "expert", scatter_dimension=1, tiled=True
        ).astype(jnp.float32),
        lax.psum_scatter(
            grad_w_out.astype(jnp.bfloat16), "expert", scatter_dimension=1, tiled=True
        ).astype(jnp.float32),
        lax.psum_scatter(
            grad_w_ada.astype(jnp.bfloat16), "expert", scatter_dimension=1, tiled=True
        ).astype(jnp.float32),
        lax.psum_scatter(
            grad_b_lanes.astype(jnp.bfloat16), "expert", scatter_dimension=0, tiled=True
        ).astype(jnp.float32),
        lax.psum_scatter(
            grad_router.astype(jnp.bfloat16), "expert", scatter_dimension=1, tiled=True
        ).astype(jnp.float32),
        lax.psum_scatter(
            grad_shared_in.astype(jnp.bfloat16), "expert", scatter_dimension=1, tiled=True
        ).astype(jnp.float32),
        lax.psum_scatter(
            grad_shared_out.astype(jnp.bfloat16), "expert", scatter_dimension=1, tiled=True
        ).astype(jnp.float32),
    )
    (
        grad_w_qkv,
        grad_w_out,
        grad_w_ada,
        grad_b_lanes,
        grad_router,
        grad_shared_in,
        grad_shared_out,
    ) = (
        lax.psum_scatter(
            grad_w_qkv.astype(jnp.bfloat16), "dp", scatter_dimension=0, tiled=True
        ).astype(jnp.float32),
        lax.psum_scatter(
            grad_w_out.astype(jnp.bfloat16), "dp", scatter_dimension=0, tiled=True
        ).astype(jnp.float32),
        lax.psum_scatter(
            grad_w_ada.astype(jnp.bfloat16), "dp", scatter_dimension=0, tiled=True
        ).astype(jnp.float32),
        lax.psum_scatter(
            grad_b_lanes.astype(jnp.bfloat16), "dp", scatter_dimension=1, tiled=True
        ).astype(jnp.float32),
        lax.psum_scatter(
            grad_router.astype(jnp.bfloat16), "dp", scatter_dimension=0, tiled=True
        ).astype(jnp.float32),
        lax.psum_scatter(
            grad_shared_in.astype(jnp.bfloat16), "dp", scatter_dimension=0, tiled=True
        ).astype(jnp.float32),
        lax.psum_scatter(
            grad_shared_out.astype(jnp.bfloat16), "dp", scatter_dimension=0, tiled=True
        ).astype(jnp.float32),
    )
    grad_b_ada = grad_b_lanes.reshape(-1)
    return (
        result.astype(jnp.bfloat16),
        grad_input.astype(jnp.bfloat16),
        grad_w_qkv,
        grad_w_out,
        grad_w_ada,
        grad_b_ada,
        grad_router,
        grad_shared_in,
        grad_shared_out,
        grad_expert_in,
        grad_expert_out,
    )


def solution(mesh):
    placed = (
        P(("dp", "expert"), None),
        P(("dp", "expert")),
        P(("dp", "expert")),
        P(("dp", "expert"), None),
        P(("dp", "expert"), None),
        P(("dp", "expert"), None),
        P(("dp", "expert"), None),
        P(("dp", "expert"), None),
        P(("dp", "expert")),
        P(("dp", "expert"), None),
        P(("dp", "expert"), None),
        P(("dp", "expert"), None),
        P("expert", None, None),
        P("expert", None, None),
    )
    return jax.shard_map(
        body,
        mesh=mesh,
        in_specs=placed,
        out_specs=(
            P(("dp", "expert"), None),
            P(("dp", "expert"), None),
            P("dp", "expert"),
            P("dp", "expert"),
            P("dp", "expert"),
            P(("dp", "expert")),
            P("dp", "expert"),
            P("dp", "expert"),
            P("dp", "expert"),
            P("expert", "dp", None),
            P("expert", "dp", None),
        ),
        check_vma=False,
    )
```

profile of v0, /device:TPU:8, one launch (start us, length us, event | category | flops | bytes accessed | tf_op | source)
XLA Modules:
  0.0 1686.3 jit_solution(3949807764921091048)
XLA Ops:
  12.1 40.9 %all-reduce.2 = bf16[4608]{0:T(1024)(128)(2,1)S(1)} all-reduce(bf16[4608]{0:T(1024)(128)(2,1)S(1)} %dynamic-update-slice), channel_id=1, replica_groups=mesh['dp'=8,'expert'=4] {'dp','expert'}, use_global_device_ids=true, to_apply=%add.2 | all-reduce | flops 4608 | bytes 18432
  57.6 27.2 %all-gather.7.cloned.1.call-done = bf16[768,4608]{1,0:T(8,128)(2,1)} async-done(((bf16[24,4608]{1,0:T(8,128)(2,1)}), bf16[768,4608]{1,0:T(8,128)(2,1)}) %all-gather.7.cloned.1.call-update) | async-done | bytes 7077904 | tf_op jit(solution)/shard_map/all_gather | solution.py:156
  91.3 54.4 %all-gather.9.cloned.1.call-done = bf16[768,2304]{1,0:T(8,128)(2,1)} async-done(((bf16[24,2304]{1,0:T(8,128)(2,1)}), bf16[768,2304]{1,0:T(8,128)(2,1)}) %all-gather.9.cloned.1.call-update) | async-done | bytes 3538960 | tf_op jit(solution)/shard_map/all_gather | solution.py:154
  154.1 74.3 %conditional.6 = (f32[1024,12]{0,1:T(8,128)S(1)}, bf16[1024,768]{0,1:T(8,128)(2,1)}) conditional(s32[]{:T(128)} %bitcast.36, (bf16[1024,768]{1,0:T(8,128)(2,1)}, bf16[1024,768]{1,0:T(8,128)(2,1)}, bf16[1024,768]{1,0:T(8,128)(2,1)}) %tuple.42, (bf16[1024,768]{1,0:T(8,128)(2,1)}, bf16[1024,768]{1,0:T(8,128)(2,1)}, bf16[1024,768]{1,0:T(8,128)(2,1)}) %tuple.42), branch_computations={%region_2.5_spmd, %region_5.8_spmd} | conditional | flops 3335245824 | bytes 173408304
  167.1 20.8 %multiply_reduce_fusion.1 = (f32[12,1024]{1,0:T(8,128)S(1)}, f32[12,1024,1024]{1,2,0:T(8,128)}) fusion(bf16[1024,12,64]{0,2,1:T(8,128)(2,1)} %bitcast.318, bf16[1024,12,64]{0,2,1:T(8,128)(2,1)S(1)} %bitcast.317), kind=kOutput, calls=%fused_computation.22 | convolution fusion | flops 1635766272 | bytes 53526528 | tf_op jit(solution)/shard_map/cond/branch_1_fun/gqhd,gkhd->ghqk/dot_general | solution.py:76
  188.0 20.1 %fusion.11 = f32[12,1024]{1,0:T(8,128)S(1)} fusion(f32[12,1024,1024]{1,2,0:T(8,128)} %get-tuple-element.254, f32[12,1024]{1,0:T(8,128)S(1)} %get-tuple-element.253), kind=kLoop, calls=%fused_computation.23 | loop fusion | flops 37736448 | bytes 50429952 | tf_op jit(solution)/shard_map/cond/branch_1_fun/reduce_sum | solution.py:84
  208.1 19.9 %fusion.13 = bf16[12,1024,64]{1,2,0:T(8,128)(2,1)} fusion(bf16[1024,12,64]{0,2,1:T(8,128)(2,1)S(1)} %bitcast.335, f32[12,1024,1024]{1,2,0:T(8,128)} %get-tuple-element.254, f32[12,1024]{1,0:T(8,128)S(1)} %fusion.11, f32[12,1024]{1,0:T(8,128)S(1)} %get-tuple-element.253), kind=kOutput, calls=%fused_computation.25 | convolution fusion | flops 1661730816 | bytes 53575680 | tf_op jit(solution)/shard_map/cond/branch_1_fun/ghqk,gkhd->gqhd/dot_general | solution.py:86
  235.9 31.6 %all-gather.13.cloned.1.call-done = bf16[768,3072]{1,0:T(8,128)(2,1)} async-done(((bf16[24,3072]{1,0:T(8,128)(2,1)}), bf16[768,3072]{1,0:T(8,128)(2,1)}) %all-gather.13.cloned.1.call-update) | async-done | bytes 4718608 | tf_op jit(solution)/shard_map/all_gather | solution.py:159
  287.8 65.3 %all-gather = bf16[32,24,8]{1,2,0:T(8,128)(2,1)S(1)} all-gather(bf16[1,24,8]{1,2,0:T(8,128)(2,1)S(1)} %bitcast.344), channel_id=1, replica_groups=mesh['dp'=8,'expert'=4] {'dp','expert'}, dimensions={0}, use_global_device_ids=true | all-gather | bytes 12672 | tf_op jit(solution)/shard_map/all_gather | solution.py:158
  394.0 12.3 gather_fusion.2
  411.8 15.1 fusion.50
  427.0 64.4 %all-to-all-done = bf16[8,1,288,768]{3,2,1,0:T(8,128)(2,1)} async-done(((bf16[8,1,288,768]{3,2,1,0:T(8,128)(2,1)}), bf16[8,1,288,768]{3,2,1,0:T(8,128)(2,1)}, u32[]{:S(2)}, u32[]{:S(2)}) %all-to-all-start) | async-done | bytes 3538976 | tf_op jit(solution)/shard_map/all_to_all | solution.py:197
  499.4 9.6 convolution_convert_fusion.3
  509.1 20.7 %fusion.53 = f32[2,4,288,3072]{3,2,1,0:T(8,128)} fusion(bf16[2,768,3072]{2,1,0:T(8,128)(2,1)} %param.30, bf16[4,2,1,288,768]{4,3,1,0,2:T(8,128)(2,1)} %bitcast.48), kind=kOutput, calls=%fused_computation.82 | convolution fusion | flops 10871635968 | bytes 41287680 | tf_op jit(solution)/shard_map/encd,edf->encf/dot_general | solution.py:198
  529.8 22.1 %fusion.89 = bf16[2,4,288,768]{3,2,1,0:T(8,128)(2,1)S(1)} fusion(bf16[2,3072,768]{2,1,0:T(8,128)(2,1)S(1)} %bitcast.347, f32[2,4,288,3072]{3,2,1,0:T(8,128)} %fusion.53), kind=kOutput, calls=%fused_computation.148 | convolution fusion | flops 10937106432 | bytes 41287680 | tf_op jit(solution)/shard_map/encf,efd->encd/dot_general | solution.py:201
  553.8 82.3 %all-to-all-done.2 = bf16[8,1,288,768]{3,2,1,0:T(8,128)(2,1)} async-done(((bf16[8,1,288,768]{3,2,1,0:T(8,128)(2,1)}), bf16[8,1,288,768]{3,2,1,0:T(8,128)(2,1)}, u32[]{:S(2)}, u32[]{:S(2)}) %all-to-all-start.2) | async-done | bytes 3538976 | tf_op jit(solution)/shard_map/all_to_all | solution.py:246
  636.1 22.7 %all-to-all-start.1 = ((bf16[2,4,288,768]{3,2,0,1:T(8,128)(2,1)}), bf16[2,4,288,768]{3,2,0,1:T(8,128)(2,1)S(1)}, u32[]{:S(2)}, u32[]{:S(2)}) async-start(bf16[2,4,288,768]{3,2,0,1:T(8,128)(2,1)} %copy.295), calls=%async_computation.1 | async-start | bytes 7077888 | tf_op jit(solution)/shard_map/all_to_all | solution.py:207
  658.8 33.6 %fusion.43 = bf16[2,4,288,3072]{3,2,1,0:T(8,128)(2,1)} fusion(f32[2,4,288,3072]{3,2,1,0:T(8,128)} %fusion.53, bf16[2,3072,768]{2,1,0:T(8,128)(2,1)} %param.31, bf16[4,2,1,288,768]{4,3,1,0,2:T(8,128)(2,1)} %bitcast.60), kind=kOutput, calls=%fused_computation.66 | convolution fusion | flops 11013193728 | bytes 55443456 | tf_op jit(solution)/shard_map/encd,efd->encf/dot_general | solution.py:254
  692.5 18.8 %fusion.92 = bf16[2,4,288,768]{3,2,1,0:T(8,128)(2,1)} fusion(bf16[2,4,288,3072]{3,2,1,0:T(8,128)(2,1)} %fusion.43, bf16[2,768,3072]{2,1,0:T(8,128)(2,1)} %param.30), kind=kOutput, calls=%fused_computation.149 | convolution fusion | flops 10873405440 | bytes 27131904 | tf_op jit(solution)/shard_map/encf,edf->encd/dot_general | solution.py:261
  715.2 17.3 %all-to-all-done.1 = bf16[2,4,288,768]{3,2,0,1:T(8,128)(2,1)S(1)} async-done(((bf16[2,4,288,768]{3,2,0,1:T(8,128)(2,1)}), bf16[2,4,288,768]{3,2,0,1:T(8,128)(2,1)S(1)}, u32[]{:S(2)}, u32[]{:S(2)}) %all-to-all-start.1) | async-done | bytes 3538976 | tf_op jit(solution)/shard_map/all_to_all | solution.py:207
  745.9 9.9 fusion.119
  755.8 12.5 gather_fusion.1
  776.2 17.3 %multiply_reduce_fusion.4 = (f32[1024,2]{1,0:T(8,128)}, f32[1024,768]{1,0:T(8,128)}) fusion(f32[1024,2,768]{2,1,0:T(2,128)} %reshape.517, f32[1024,768]{1,0:T(8,128)} %convert_element_type.229, f32[1024,2]{1,0:T(8,128)} %copy-done.28), kind=kLoop, calls=%fused_computation.90 | loop fusion | flops 5502976 | bytes 12599296 | tf_op jit(solution)/shard_map/reduce_sum | solution.py:228
  794.7 21.9 %all-to-all-done.3 = bf16[2,4,288,768]{3,2,0,1:T(8,128)(2,1)S(1)} async-done(((bf16[2,4,288,768]{3,2,0,1:T(8,128)(2,1)}), bf16[2,4,288,768]{3,2,0,1:T(8,128)(2,1)S(1)}, u32[]{:S(2)}, u32[]{:S(2)}) %all-to-all-start.3) | async-done | bytes 3538976 | tf_op jit(solution)/shard_map/all_to_all | solution.py:264
  816.6 9.5 gather_fusion.4
  834.2 12.1 reduce_sum.260
  852.2 16.8 fusion.112
  877.7 158.8 %conditional.7 = (bf16[1024,2304]{0,1:T(8,128)(2,1)}) conditional(s32[]{:T(128)} %bitcast.36, (bf16[1024,768]{1,0:T(8,128)(2,1)}, bf16[1024,768]{1,0:T(8,128)(2,1)}, f32[1024,12]{0,1:T(8,128)S(1)}, bf16[1024,768]{1,0:T(8,128)(2,1)S(1)}, bf16[1024,768]{1,0:T(8,128)(2,1)}) %tuple.144, (bf16[1024,768]{1,0:T(8,128)(2,1)}, ...), branch_computations={%region_24.26_spmd, %region_26.28_spmd} | conditional | flops 8221347840 | bytes 434356320
  893.2 20.9 %fusion.116 = f32[12,1024,1024]{1,2,0:T(8,128)} fusion(bf16[1024,12,64]{0,2,1:T(8,128)(2,1)} %bitcast.315, bf16[1024,12,64]{0,2,1:T(8,128)(2,1)S(1)} %bitcast.310), kind=kOutput, calls=%fused_computation.223 | convolution fusion | flops 1610612736 | bytes 53477376 | tf_op jit(solution)/shard_map/cond/branch_1_fun/gqhd,gkhd->ghqk/dot_general | solution.py:101
  914.0 19.3 %fusion.34 = bf16[12,1024,64]{1,2,0:T(8,128)(2,1)} fusion(bf16[1024,12,64]{0,2,1:T(8,128)(2,1)S(1)} %bitcast.313, f32[12,1024,1024]{1,2,0:T(8,128)} %fusion.116, f32[12,1024]{1,0:T(8,128)S(1)} %bitcast.330), kind=kOutput, calls=%fused_computation.53 | convolution fusion | flops 1648361472 | bytes 53526528 | tf_op jit(solution)/shard_map/cond/branch_1_fun/ghqk,gqhd->gkhd/dot_general | solution.py:106
  933.3 32.6 %multiply_reduce_fusion.3 = (f32[12,1024]{1,0:T(8,128)S(1)}, f32[12,1024,1024]{1,2,0:T(8,128)}) fusion(f32[12,1024,1024]{1,2,0:T(8,128)} %fusion.116, f32[12,1024]{1,0:T(8,128)S(1)} %bitcast.331, bf16[1024,12,64]{0,2,1:T(8,128)(2,1)S(1)} %bitcast.314, bf16[1024,12,64]{0,2,1:T(8,128)(2,1)} %bitcast.328), kind=kOutput, calls=%fused_computation.50 | convolution fusion | flops 1660932096 | bytes 103907328 | tf_op jit(solution)/shard_map/cond/branch_1_fun/gqhd,gkhd->ghqk/dot_general | solution.py:112
  965.9 40.9 %multiply_convert_fusion.1 = bf16[12,1024,1024]{1,2,0:T(8,128)(2,1)} fusion(f32[12,1024,1024]{1,2,0:T(8,128)} %get-tuple-element.258, f32[12,1024,1024]{1,2,0:T(8,128)} %fusion.116, f32[12,1024]{1,0:T(8,128)S(1)} %get-tuple-element.257, f32[12,1024]{1,0:T(8,128)S(1)} %bitcast.332), kind=kLoop, calls=%fused_computation.49 | loop fusion | flops 62914560 | bytes 125927424 | tf_op jit(solution)/shard_map/cond/branch_1_fun/convert_element_type | solution.py:116
  1006.8 13.9 convolution_multiply_fusion.1
  1020.8 12.8 convolution_multiply_fusion
  1070.1 10.3 copy.335
  1083.2 20.9 %all-reduce.5 = (bf16[4,1152]{1,0:T(4,128)(2,1)S(1)}, bf16[768,8]{0,1:T(8,128)(2,1)S(1)}) all-reduce(bf16[4,1152]{1,0:T(4,128)(2,1)S(1)} %convert_element_type.247, bf16[768,8]{0,1:T(8,128)(2,1)S(1)} %convolution_convert_fusion.7), channel_id=8, replica_groups=mesh['dp'=8,'expert'=4] {'expert'}, use_global_device_ids=true, to_apply=%region_43.44.clone | all-reduce | flops 10752 | bytes 43008
  1116.7 22.7 %bitcast_convert_fusion = bf16[2,3072,768]{2,1,0:T(8,128)(2,1)} fusion(bf16[4,2,1,288,768]{4,3,1,0,2:T(8,128)(2,1)} %bitcast.60, f32[2,4,288,3072]{3,2,1,0:T(8,128)} %fusion.53), kind=kOutput, calls=%fused_computation.68 | convolution fusion | flops 10940055552 | bytes 41287680 | tf_op jit(solution)/shard_map/encf,encd->efd/dot_general | solution.py:248
  1139.5 20.6 %bitcast_convert_fusion.1 = bf16[2,768,3072]{2,1,0:T(8,128)(2,1)} fusion(bf16[2,4,288,3072]{3,2,1,0:T(8,128)(2,1)} %fusion.43, bf16[2,4,288,768]{3,2,0,1:T(8,128)(2,1)} %bitcast.77), kind=kOutput, calls=%fused_computation.69 | convolution fusion | flops 10876354560 | bytes 27131904 | tf_op jit(solution)/shard_map/encd,encf->edf/dot_general | solution.py:258
  1160.2 80.2 %reduce-scatter.47.cloned.1.call-done = bf16[1152,768]{1,0:T(8,128)(2,1)} async-done(((bf16[4608,768]{1,0:T(8,128)(2,1)}), bf16[1152,768]{1,0:T(8,128)(2,1)}) %reduce-scatter.47.cloned.1.call-update) | async-done | bytes 1769488
  1248.6 28.8 %reduce-scatter.49.cloned.1.call-done = bf16[144,1]{1,0:T(8,128)(2,1)} async-done(((bf16[1152,1]{1,0:T(8,128)(2,1)}), bf16[144,1]{1,0:T(8,128)(2,1)}) %reduce-scatter.49.cloned.1.call-update) | async-done | bytes 304
  1278.8 35.6 %reduce-scatter.51.cloned.1.call-done = bf16[96,2]{1,0:T(8,128)(2,1)} async-done(((bf16[768,2]{1,0:T(8,128)(2,1)}), bf16[96,2]{1,0:T(8,128)(2,1)}) %reduce-scatter.51.cloned.1.call-update) | async-done | bytes 400
  1315.8 41.3 %reduce-scatter.53.cloned.1.call-done = bf16[384,192]{1,0:T(8,128)(2,1)} async-done(((bf16[3072,192]{1,0:T(8,128)(2,1)}), bf16[384,192]{1,0:T(8,128)(2,1)}) %reduce-scatter.53.cloned.1.call-update) | async-done | bytes 147472
  1358.9 38.4 %reduce-scatter.35.cloned.1.call-done = bf16[96,768]{1,0:T(8,128)(2,1)} async-done(((bf16[768,768]{1,0:T(8,128)(2,1)}), bf16[96,768]{1,0:T(8,128)(2,1)}) %reduce-scatter.35.cloned.1.call-update) | async-done | bytes 147472 | tf_op jit(solution)/shard_map/reduce_scatter | solution.py:364
  1399.0 35.7 %reduce-scatter.45.cloned.1.call-done = bf16[96,192]{1,0:T(8,128)(2,1)} async-done(((bf16[768,192]{1,0:T(8,128)(2,1)}), bf16[96,192]{1,0:T(8,128)(2,1)}) %reduce-scatter.45.cloned.1.call-update) | async-done | bytes 36880
  1436.3 37.7 %reduce-scatter.43.cloned.1.call-done = bf16[96,576]{1,0:T(8,128)(2,1)} async-done(((bf16[768,576]{1,0:T(8,128)(2,1)}), bf16[96,576]{1,0:T(8,128)(2,1)}) %reduce-scatter.43.cloned.1.call-update) | async-done | bytes 110608
  1476.0 78.4 %reduce-scatter.41.cloned.1.call-done = bf16[2,384,768]{2,1,0:T(8,128)(2,1)} async-done(((bf16[2,3072,768]{2,1,0:T(8,128)(2,1)}), bf16[2,384,768]{2,1,0:T(8,128)(2,1)}) %reduce-scatter.41.cloned.1.call-update) | async-done | bytes 1179664 | tf_op jit(solution)/shard_map/reduce_scatter | solution.py:272
  1557.2 77.4 %reduce-scatter.39.cloned.1.call-done = bf16[2,96,3072]{2,1,0:T(8,128)(2,1)} async-done(((bf16[2,768,3072]{2,1,0:T(8,128)(2,1)}), bf16[2,96,3072]{2,1,0:T(8,128)(2,1)}) %reduce-scatter.39.cloned.1.call-update) | async-done | bytes 1179664 | tf_op jit(solution)/shard_map/reduce_scatter | solution.py:269
  1637.6 40.2 %reduce-scatter.31.cloned.1.call-done = bf16[96,1152]{1,0:T(8,128)(2,1)} async-done(((bf16[768,1152]{1,0:T(8,128)(2,1)}), bf16[96,1152]{1,0:T(8,128)(2,1)}) %reduce-scatter.31.cloned.1.call-update) | async-done | bytes 221200 | tf_op jit(solution)/shard_map/reduce_scatter | solution.py:355
  (310 shorter events, 246.9 us)
Async XLA Ops:
  7.2 77.6 %all-gather.7.cloned.1.call-start = ((), (), s32[]{:S(2)}) async-start(), calls=%async_computation.18 | async-start | bytes 7299072 | tf_op jit(solution)/shard_map/all_gather | solution.py:156
  7.9 137.8 %all-gather.9.cloned.1.call-start = ((), (), s32[]{:S(2)}) async-start(), calls=%async_computation.19 | async-start | bytes 3649536 | tf_op jit(solution)/shard_map/all_gather | solution.py:154
  8.7 219.8 %all-gather.11.cloned.1.call-start = ((), (), s32[]{:S(2)}) async-start(), calls=%async_computation.20 | async-start | bytes 1216512 | tf_op jit(solution)/shard_map/all_gather | solution.py:155
  9.4 258.2 %all-gather.13.cloned.1.call-start = ((), (), s32[]{:S(2)}) async-start(), calls=%async_computation.21 | async-start | bytes 4866048 | tf_op jit(solution)/shard_map/all_gather | solution.py:159
  10.0 401.9 %all-gather.15.cloned.1.call-start = ((), (), s32[]{:S(2)}) async-start(), calls=%async_computation.22 | async-start | bytes 4866048 | tf_op jit(solution)/shard_map/all_gather | solution.py:160
  10.6 1096.2 %reduce-scatter.37.cloned.1.call-start = ((), (), s32[]{:S(2)}) async-start(), calls=%async_computation.28 | async-start | bytes 5898240 | tf_op jit(solution)/shard_map/reduce_scatter | solution.py:336
  55.4 35.2 %copy-start.52 = (f32[1024]{0:T(1024)}, f32[1024]{0:T(1024)S(1)}, u32[]{:S(2)}) copy-start(f32[1024]{0:T(1024)S(1)} %broadcast_multiply_fusion.6) | copy-start | bytes 12292
  57.4 33.1 %copy-start.61 = (f32[1024]{0:T(1024)}, f32[1024]{0:T(1024)S(1)}, u32[]{:S(2)}) copy-start(f32[1024]{0:T(1024)S(1)} %add_rsqrt_fusion.1) | copy-start | bytes 12292
  57.5 31.4 %copy-start.65 = (f32[4,384]{1,0:T(4,128)}, f32[4,384]{1,0:T(4,128)S(1)}, u32[]{:S(2)}) copy-start(f32[4,384]{1,0:T(4,128)S(1)} %get-tuple-element.273) | copy-start | bytes 18436
  57.5 31.4 %copy-start.67 = (f32[4,384]{1,0:T(4,128)}, f32[4,384]{1,0:T(4,128)S(1)}, u32[]{:S(2)}) copy-start(f32[4,384]{1,0:T(4,128)S(1)} %get-tuple-element.274) | copy-start | bytes 18436
  89.0 62.8 %copy-start.46 = (f32[4,768]{1,0:T(4,128)}, f32[4,768]{1,0:T(4,128)S(1)}, u32[]{:S(2)}) copy-start(f32[4,768]{1,0:T(4,128)S(1)} %get-tuple-element.269) | copy-start | bytes 36868
  89.0 139.4 %copy-start.50 = (f32[4,768]{1,0:T(4,128)}, f32[4,768]{1,0:T(4,128)S(1)}, u32[]{:S(2)}) copy-start(f32[4,768]{1,0:T(4,128)S(1)} %get-tuple-element.270) | copy-start | bytes 36868
  89.0 145.1 %copy-start.39 = (f32[4,768]{1,0:T(4,128)}, f32[4,768]{1,0:T(4,128)S(1)}, u32[]{:S(2)}) copy-start(f32[4,768]{1,0:T(4,128)S(1)} %get-tuple-element.267) | copy-start | bytes 36868
  91.3 60.5 %copy-start.32 = (bf16[1024,768]{1,0:T(8,128)(2,1)}, bf16[1024,768]{1,0:T(8,128)(2,1)S(1)}, u32[]{:S(2)}) copy-start(bf16[1024,768]{1,0:T(8,128)(2,1)S(1)} %fusion.79) | copy-start | bytes 4718596
  188.0 20.1 %copy-start.34 = (bf16[1024,768]{0,1:T(8,128)(2,1)S(1)}, bf16[1024,768]{0,1:T(8,128)(2,1)}, u32[]{:S(2)}) copy-start(bf16[1024,768]{0,1:T(8,128)(2,1)} %copy.287) | copy-start | bytes 4718596 | tf_op jit(solution)/shard_map/conditional.2
  234.2 40.3 %copy-start.54 = (f32[1024]{0:T(1024)}, f32[1024]{0:T(1024)S(1)}, u32[]{:S(2)}) copy-start(f32[1024]{0:T(1024)S(1)} %add_rsqrt_fusion) | copy-start | bytes 12292
  235.9 145.5 %copy-start.8 = (bf16[1024,768]{1,0:T(8,128)(2,1)}, bf16[1024,768]{1,0:T(8,128)(2,1)S(1)}, u32[]{:S(2)}) copy-start(bf16[1024,768]{1,0:T(8,128)(2,1)S(1)} %fusion.84) | copy-start | bytes 4718596
  235.9 43.1 %copy-start.14 = (bf16[1024,768]{1,0:T(8,128)(2,1)S(1)}, bf16[1024,768]{1,0:T(8,128)(2,1)}, u32[]{:S(2)}) copy-start(bf16[1024,768]{1,0:T(8,128)(2,1)} %fusion.82) | copy-start | bytes 4718596
  353.3 28.1 %copy-start.48 = (bf16[768,8]{0,1:T(8,128)(2,1)}, bf16[768,8]{0,1:T(8,128)(2,1)S(1)}, u32[]{:S(2)}) copy-start(bf16[768,8]{0,1:T(8,128)(2,1)S(1)} %reshape.522) | copy-start | bytes 36868
  374.0 117.4 %all-to-all-start = ((bf16[8,1,288,768]{3,2,1,0:T(8,128)(2,1)}), bf16[8,1,288,768]{3,2,1,0:T(8,128)(2,1)}, u32[]{:S(2)}, u32[]{:S(2)}) async-start(bf16[8,1,288,768]{3,2,1,0:T(8,128)(2,1)} %bitcast.312), calls=%async_computation | async-start | bytes 7077888 | tf_op jit(solution)/shard_map/all_to_all | solution.py:197
  427.0 72.5 %copy-start.9 = (bf16[1024,768]{1,0:T(8,128)(2,1)S(1)}, bf16[1024,768]{1,0:T(8,128)(2,1)}, u32[]{:S(2)}) copy-start(bf16[1024,768]{1,0:T(8,128)(2,1)} %copy-done.8) | copy-start | bytes 4718596
  491.4 144.7 %all-to-all-start.2 = ((bf16[8,1,288,768]{3,2,1,0:T(8,128)(2,1)}), bf16[8,1,288,768]{3,2,1,0:T(8,128)(2,1)}, u32[]{:S(2)}, u32[]{:S(2)}) async-start(bf16[8,1,288,768]{3,2,1,0:T(8,128)(2,1)} %multiply_convert_fusion.4), calls=%async_computation.2 | async-start | bytes 7077888 | tf_op jit(solution)/shard_map/all_to_all | solution.py:246
  499.4 610.0 %reduce-scatter.33.cloned.1.call-start = ((), (), s32[]{:S(2)}) async-start(), calls=%async_computation.26 | async-start | bytes 5898240 | tf_op jit(solution)/shard_map/reduce_scatter | solution.py:333
  509.0 20.7 %slice-start.3 = ((s8[9437184]{0:T(1024)(128)(4,1)}), s8[1048576]{0:T(1024)(128)(4,1)S(1)}, s32[]{:S(2)}) async-start(s8[9437184]{0:T(1024)(128)(4,1)} %bitcast.346), calls=%async_computation.40 | async-start | bytes 2097152
  509.0 20.7 %slice-start.4 = ((s8[9437184]{0:T(1024)(128)(4,1)}), s8[4194304]{0:T(1024)(128)(4,1)S(1)}, s32[]{:S(2)}) async-start(s8[9437184]{0:T(1024)(128)(4,1)} %bitcast.346), calls=%async_computation.41 | async-start | bytes 8388608
  509.1 20.7 %slice-start.5 = ((s8[9437184]{0:T(1024)(128)(4,1)}), s8[4194304]{0:T(1024)(128)(4,1)S(1)}, s32[]{:S(2)}) async-start(s8[9437184]{0:T(1024)(128)(4,1)} %bitcast.346), calls=%async_computation.42 | async-start | bytes 8388608
  636.1 96.4 %all-to-all-start.1 = ((bf16[2,4,288,768]{3,2,0,1:T(8,128)(2,1)}), bf16[2,4,288,768]{3,2,0,1:T(8,128)(2,1)S(1)}, u32[]{:S(2)}, u32[]{:S(2)}) async-start(bf16[2,4,288,768]{3,2,0,1:T(8,128)(2,1)} %copy.295), calls=%async_computation.1 | async-start | bytes 7077888 | tf_op jit(solution)/shard_map/all_to_all | solution.py:207
  734.3 82.3 %all-to-all-start.3 = ((bf16[2,4,288,768]{3,2,0,1:T(8,128)(2,1)}), bf16[2,4,288,768]{3,2,0,1:T(8,128)(2,1)S(1)}, u32[]{:S(2)}, u32[]{:S(2)}) async-start(bf16[2,4,288,768]{3,2,0,1:T(8,128)(2,1)} %copy.301), calls=%async_computation.3 | async-start | bytes 7077888 | tf_op jit(solution)/shard_map/all_to_all | solution.py:264
  741.3 368.7 %reduce-scatter.29.cloned.1.call-start = ((), (), s32[]{:S(2)}) async-start(), calls=%async_computation.24 | async-start | bytes 1474560 | tf_op jit(solution)/shard_map/reduce_scatter | solution.py:321
  834.1 12.2 copy-start.2
  834.1 12.2 copy-start.40
  834.1 12.2 copy-start.42
  852.2 18.5 %copy-start.51 = (f32[4,768]{1,0:T(4,128)S(1)}, f32[4,768]{1,0:T(4,128)}, u32[]{:S(2)}) copy-start(f32[4,768]{1,0:T(4,128)} %copy-done.50) | copy-start | bytes 36868
  874.9 239.3 %reduce-scatter.27.cloned.1.call-start = ((), (), s32[]{:S(2)}) async-start(), calls=%async_computation.23 | async-start | bytes 4423680 | tf_op jit(solution)/shard_map/reduce_scatter | solution.py:318
  965.9 40.9 %copy-start.23 = (bf16[1024,768]{0,1:T(8,128)(2,1)S(1)}, bf16[1024,768]{0,1:T(8,128)(2,1)}, u32[]{:S(2)}) copy-start(bf16[1024,768]{0,1:T(8,128)(2,1)} %copy.306) | copy-start | bytes 4718596 | tf_op jit(solution)/shard_map/conditional.3
  1020.8 12.8 copy-start.24
  1020.8 12.8 copy-start.31
  1045.0 195.3 %reduce-scatter.47.cloned.1.call-start = ((), (), s32[]{:S(2)}) async-start(), calls=%async_computation.33 | async-start | bytes 8847360
  1080.4 197.0 %reduce-scatter.49.cloned.1.call-start = ((), (), s32[]{:S(2)}) async-start(), calls=%async_computation.34 | async-start | bytes 331776
  1105.8 208.6 %reduce-scatter.51.cloned.1.call-start = ((), (), s32[]{:S(2)}) async-start(), calls=%async_computation.35 | async-start | bytes 221184
  1106.7 250.4 %reduce-scatter.53.cloned.1.call-start = ((), (), s32[]{:S(2)}) async-start(), calls=%async_computation.36 | async-start | bytes 1769472
  1109.3 288.0 %reduce-scatter.35.cloned.1.call-start = ((), (), s32[]{:S(2)}) async-start(), calls=%async_computation.27 | async-start | bytes 1327104 | tf_op jit(solution)/shard_map/reduce_scatter | solution.py:364
  1109.9 324.8 %reduce-scatter.45.cloned.1.call-start = ((), (), s32[]{:S(2)}) async-start(), calls=%async_computation.32 | async-start | bytes 442368
  1111.9 362.2 %reduce-scatter.43.cloned.1.call-start = ((), (), s32[]{:S(2)}) async-start(), calls=%async_computation.31 | async-start | bytes 1105920
  1116.5 437.9 %reduce-scatter.41.cloned.1.call-start = ((), (), s32[]{:S(2)}) async-start(), calls=%async_computation.30 | async-start | bytes 10616832 | tf_op jit(solution)/shard_map/reduce_scatter | solution.py:272
  1139.5 495.2 %reduce-scatter.39.cloned.1.call-start = ((), (), s32[]{:S(2)}) async-start(), calls=%async_computation.29 | async-start | bytes 10616832 | tf_op jit(solution)/shard_map/reduce_scatter | solution.py:269
  1160.1 84.2 %copy-start.6 = (bf16[1024,768]{1,0:T(8,128)(2,1)S(1)}, bf16[1024,768]{1,0:T(8,128)(2,1)}, u32[]{:S(2)}) copy-start(bf16[1024,768]{1,0:T(8,128)(2,1)} %param.18) | copy-start | bytes 4718596
  1160.1 517.7 %reduce-scatter.31.cloned.1.call-start = ((), (), s32[]{:S(2)}) async-start(), calls=%async_computation.25 | async-start | bytes 1990656 | tf_op jit(solution)/shard_map/reduce_scatter | solution.py:355
  (43 other events, 180.9 us)
Sparse Core Ops, SparseCore 0:
  10.8 73.9 all-gather.6
  87.6 58.1 all-gather.8
  148.5 52.4 all-gather.10
  203.7 63.8 all-gather.12
  270.2 62.5 all-gather.14
  334.9 120.7 reduce-scatter.36
  509.2 145.6 reduce-scatter.32
  875.0 29.0 reduce-scatter.28
  1045.1 69.0 reduce-scatter.26
  1116.4 123.9 reduce-scatter.46
  1244.0 33.3 reduce-scatter.48
  1280.8 33.5 reduce-scatter.50
  1318.6 38.4 reduce-scatter.52
  1360.6 36.7 reduce-scatter.34
  1400.8 33.8 reduce-scatter.44
  1438.3 35.7 reduce-scatter.42
  1477.8 76.4 reduce-scatter.40
  1558.1 76.4 reduce-scatter.38
  1638.4 39.3 reduce-scatter.30
where the time goes:
time: 1690 us
  waiting for transfers between devices  799 us (47%)
  matrix products  396 us (23%)
  local copies, waits for them, and re-layouts  153 us (9%)
  other arithmetic  133 us (8%)
  blocking collectives  127 us (8%)
  starting transfers between devices  46.2 us (3%)
    unnamed x25, waiting for transfers between devices  263 us
    all_to_all x1, waiting for transfers between devices, body(): lax.all_to_all(grad_sent, 'expert', split_axis=0, concat_axis=1, tiled=True)  82.3 us
    reduce_scatter x1, waiting for transfers between devices, body(): lax.psum_scatter(grad_expert_out.astype(jnp.bfloat16), 'dp', scatter_dime...  78.4 us
    reduce_scatter x1, waiting for transfers between devices, body(): lax.psum_scatter(grad_expert_in.astype(jnp.bfloat16), 'dp', scatter_dimen...  77.4 us
    dot_general x10, matrix products, product(): return jnp.dot(left_side, right_side, preferred_element_type=jnp.float32)  74 us
    all_gather x1, blocking collectives, body(): lax.all_gather(w_router, ('dp', 'expert'), axis=0, tiled=True)  65.3 us
    all_to_all x1, waiting for transfers between devices, body(): lax.all_to_all(dispatched, 'expert', split_axis=0, concat_axis=1, tiled=T...  64.4 us
    unnamed x2, blocking collectives  61.8 us
  transfers between devices with their start and end apart: 23, of which 18 were waited for; matrix products, arithmetic and copies ran while one was open for 39% of the time, Pallas kernels for 0%

commit v1 on v0

v1 whole, which is shorter than its diff:
```python
import math

import jax
import jax.numpy as jnp
from jax import lax
from jax.experimental import pallas as pl
from jax.experimental.pallas import tpu as pltpu
from jax.sharding import PartitionSpec as P

D = 768
HEADS = 12
HEAD_DIM = 64
EXPERTS = 8
LONG = 1024
SHORT = 256
BLOCKS = LONG // SHORT
CAP = 288
EXTRA = 16
BUCKETS = 50
PAIRS = HEADS // 2
FAR = 1e30
VMEM = 60 * 2**20

HIGHEST = lax.Precision.HIGHEST
BOTH = ("dp", "expert")
HBM = pl.BlockSpec(memory_space=pl.ANY)


def product(left_side, right_side):
    return jnp.dot(left_side, right_side, preferred_element_type=jnp.float32)


def product_nt(left_side, right_side):
    return lax.dot_general(
        left_side, right_side, (((1,), (1,)), ((), ())), preferred_element_type=jnp.float32
    )


def product_tn(left_side, right_side):
    return lax.dot_general(
        left_side, right_side, (((0,), (0,)), ((), ())), preferred_element_type=jnp.float32
    )


def embed(bucket):
    time_values = bucket.astype(jnp.float32) * (1000.0 / BUCKETS)
    half_width = D // 2
    frequency = jnp.exp(-math.log(10000.0) * jnp.arange(half_width, dtype=jnp.float32) / half_width)
    angles = time_values[:, None] * frequency[None, :]
    return jnp.concatenate([jnp.cos(angles), jnp.sin(angles)], axis=1)


def normalize(values):
    center = values - jnp.mean(values, axis=-1, keepdims=True)
    variance = jnp.mean(center * center, axis=-1, keepdims=True)
    inverse = lax.rsqrt(variance + 1e-06)
    return (center * inverse, inverse)


def norm_back(grad_hat, hat_values, inverse):
    return inverse * (
        grad_hat
        - jnp.mean(grad_hat, axis=-1, keepdims=True)
        - hat_values * jnp.mean(grad_hat * hat_values, axis=-1, keepdims=True)
    )


def expand(block_rows):
    return jnp.repeat(block_rows, SHORT, axis=0)


def block_sums(values):
    return jnp.sum(values.reshape(BLOCKS, SHORT, D), axis=1)


def split_three(values):
    first = lax.reduce_precision(values, 8, 7)
    second = lax.reduce_precision(values - first, 8, 7)
    return first, second, values - first - second


def attend_kernel(length_ref, q_ref, k_ref, v_ref, out_ref, total_ref):
    far = jnp.where(length_ref[0] == LONG, 0.0, FAR)
    lane = lax.broadcasted_iota(jnp.int32, (1, 2 * HEAD_DIM), 1)
    first = lane < HEAD_DIM
    keys, vals = k_ref[...], v_ref[...]
    zero, one = jnp.zeros_like(keys), jnp.ones_like(vals)
    key_set = (jnp.where(first, keys, zero), jnp.where(first, zero, keys))
    value_set = (jnp.where(first, vals, one), jnp.where(first, one, vals))
    for i in range(BLOCKS):
        rows = slice(i * SHORT, (i + 1) * SHORT)
        q = q_ref[rows, :] * jnp.asarray(HEAD_DIM**-0.5, jnp.bfloat16)
        outs, totals = [], []
        for h in range(2):
            scores = product_nt(q, key_set[h])
            parts = [scores[:, j * SHORT : (j + 1) * SHORT] for j in range(BLOCKS)]
            away = [0.0 if i == j else far for j in range(BLOCKS)]
            peak = None
            for part, distance in zip(parts, away):
                here = jnp.max(part, axis=1, keepdims=True) - distance
                peak = here if peak is None else jnp.maximum(peak, here)
            soft = jnp.concatenate(
                [
                    jnp.exp(part - (peak + distance)).astype(jnp.bfloat16)
                    for part, distance in zip(parts, away)
                ],
                axis=1,
            )
            mixed = product(soft, value_set[h])
            total = mixed[:, HEAD_DIM : HEAD_DIM + 1] if h == 0 else mixed[:, 0:1]
            outs.append(mixed / total)
            totals.append(peak + jnp.log(total))
        out_ref[rows, :] = jnp.where(first, outs[0], outs[1]).astype(jnp.bfloat16)
        flipped = jnp.transpose(jnp.where(first, totals[0], totals[1]))
        total_ref[0, 0:1, rows] = flipped[0:1, :]
        total_ref[0, 1:2, rows] = flipped[HEAD_DIM : HEAD_DIM + 1, :]


def attend_back_kernel(
    length_ref, q_ref, k_ref, v_ref, grad_ref, out_ref, total_ref, result_ref, sum_ref
):
    pair = pl.program_id(0)
    far = jnp.where(length_ref[0] == LONG, 0.0, FAR)
    lane = lax.broadcasted_iota(jnp.int32, (1, 2 * HEAD_DIM), 1)
    first = lane < HEAD_DIM
    place = lax.broadcasted_iota(jnp.int32, (1, LONG), 1) // SHORT
    q = q_ref[...] * jnp.asarray(HEAD_DIM**-0.5, jnp.bfloat16)
    grad, keys = grad_ref[...], k_ref[...]
    zero = jnp.zeros_like(keys)
    query_set = (jnp.where(first, q, zero), jnp.where(first, zero, q))
    grad_set = (jnp.where(first, grad, zero), jnp.where(first, zero, grad))
    key_set = (jnp.where(first, keys, zero), jnp.where(first, zero, keys))
    flipped = jnp.transpose(grad.astype(jnp.float32) * out_ref[...].astype(jnp.float32))
    deltas = (
        jnp.sum(flipped[:HEAD_DIM], axis=0, keepdims=True),
        jnp.sum(flipped[HEAD_DIM:], axis=0, keepdims=True),
    )
    lanes = pl.ds(pl.multiple_of(pair * 2 * HEAD_DIM, 2 * HEAD_DIM), 2 * HEAD_DIM)
    lanes_k = pl.ds(pl.multiple_of(D + pair * 2 * HEAD_DIM, 2 * HEAD_DIM), 2 * HEAD_DIM)
    lanes_v = pl.ds(pl.multiple_of(2 * D + pair * 2 * HEAD_DIM, 2 * HEAD_DIM), 2 * HEAD_DIM)
    for j in range(BLOCKS):
        rows = slice(j * SHORT, (j + 1) * SHORT)
        key_rows, value_rows = k_ref[rows, :], v_ref[rows, :]
        grad_keys = grad_values = 0.0
        for h in range(2):
            total = total_ref[0, h : h + 1, :] + jnp.where(place == j, 0.0, far)
            soft = jnp.exp(product_nt(key_rows, query_set[h]) - total)
            grad_soft = product_nt(value_rows, grad_set[h])
            grad_scores = (soft * (grad_soft - deltas[h])).astype(jnp.bfloat16)
            grad_values += product(soft.astype(jnp.bfloat16), grad_set[h])
            grad_keys += product(grad_scores, query_set[h])
            update = product_tn(grad_scores, key_set[h][rows, :])
            if j == 0 and h == 0:
                sum_ref[...] = update
            else:
                sum_ref[...] += update
        result_ref[rows, lanes_k] = grad_keys.astype(jnp.bfloat16)
        result_ref[rows, lanes_v] = grad_values.astype(jnp.bfloat16)
    result_ref[:, lanes] = (sum_ref[...] * HEAD_DIM**-0.5).astype(jnp.bfloat16)


def column_spec(start):
    return pl.BlockSpec((LONG, 2 * HEAD_DIM), lambda pair: (0, start + pair))


def attend(image_length, projected):
    return pl.pallas_call(
        attend_kernel,
        grid=(PAIRS,),
        in_specs=[
            pl.BlockSpec(memory_space=pltpu.SMEM),
            column_spec(0),
            column_spec(PAIRS),
            column_spec(2 * PAIRS),
        ],
        out_specs=[
            column_spec(0),
            pl.BlockSpec((1, 2, LONG), lambda pair: (pair, 0, 0)),
        ],
        out_shape=[
            jax.ShapeDtypeStruct((LONG, D), jnp.bfloat16),
            jax.ShapeDtypeStruct((PAIRS, 2, LONG), jnp.float32),
        ],
        compiler_params=pltpu.CompilerParams(vmem_limit_bytes=VMEM),
        cost_estimate=pl.CostEstimate(
            flops=16 * LONG * LONG * D, bytes_accessed=8 * LONG * D, transcendentals=HEADS * LONG * LONG
        ),
        name="attend",
    )(image_length, projected, projected, projected)


def attend_back(image_length, projected, grad_attended, attended, log_total):
    return pl.pallas_call(
        attend_back_kernel,
        grid=(PAIRS,),
        in_specs=[
            pl.BlockSpec(memory_space=pltpu.SMEM),
            column_spec(0),
            column_spec(PAIRS),
            column_spec(2 * PAIRS),
            column_spec(0),
            column_spec(0),
            pl.BlockSpec((1, 2, LONG), lambda pair: (pair, 0, 0)),
        ],
        out_specs=pl.BlockSpec((LONG, 3 * D), lambda pair: (0, 0)),
        out_shape=jax.ShapeDtypeStruct((LONG, 3 * D), jnp.bfloat16),
        scratch_shapes=[pltpu.VMEM((LONG, 2 * HEAD_DIM), jnp.float32)],
        compiler_params=pltpu.CompilerParams(vmem_limit_bytes=VMEM),
        cost_estimate=pl.CostEstimate(
            flops=40 * LONG * LONG * D, bytes_accessed=16 * LONG * D, transcendentals=HEADS * LONG * LONG
        ),
        name="attend_back",
    )(image_length, projected, projected, projected, grad_attended, attended, log_total)


def turn_kernel(rows_ref, turned_ref):
    turned_ref[...] = jnp.transpose(rows_ref[...])


def turn(rows):
    count, wide = rows.shape
    return pl.pallas_call(
        turn_kernel,
        grid=(count // SHORT,),
        in_specs=[pl.BlockSpec((SHORT, wide), lambda i: (i, 0))],
        out_specs=pl.BlockSpec((wide, SHORT), lambda i: (0, i)),
        out_shape=jax.ShapeDtypeStruct((wide, count), rows.dtype),
        cost_estimate=pl.CostEstimate(flops=0, bytes_accessed=4 * count * wide, transcendentals=0),
        name="turn",
    )(rows)


def whole(shape):
    return pl.BlockSpec(shape, lambda *_: (0,) * len(shape), pipeline_mode=pl.Buffered(1))


def gelu_pair(values):
    slope, cubic = math.sqrt(2.0 / math.pi), 0.044715
    square = values * values
    gate = 0.5 + 0.5 * jnp.tanh(values * (slope + slope * cubic * square))
    result = values * gate
    return result, gate + result * (1.0 - gate) * (2.0 * slope + 6.0 * slope * cubic * square)


def ffn_step(rows_ref, grad_ref, w_in_ref, w_out_ref, gelu_ref, pre_ref, out_sum, back_sum, turned_ref, size, turn):
    step = pl.program_id(0)
    count = rows_ref.shape[0]
    w_in = w_in_ref[0]
    w_out = w_out_ref[...].reshape(w_in.shape[1], D)
    for start in range(0, count, size):
        rows = slice(start, start + size)
        pre = product(rows_ref[rows, :], w_in)
        grad_gelu = product_nt(grad_ref[rows, :], w_out)
        value, slope = gelu_pair(pre)
        value = value.astype(jnp.bfloat16)
        grad_pre = (grad_gelu * slope).astype(jnp.bfloat16)
        gelu_ref[rows, :] = value
        pre_ref[rows, :] = grad_pre
        out_sum[rows, :] += product(value, w_out)
        back_sum[rows, :] += product_nt(grad_pre, w_in)
    place = pl.ds(pl.multiple_of(jnp.minimum(step, count // turn - 1) * turn, turn), turn)
    turned_ref[:, place] = jnp.transpose(rows_ref[place, :])


def shared_kernel(rows_ref, grad_ref, w_in_ref, w_out_ref, *refs):
    out_ref, back_ref, gelu_ref, pre_ref, turned_ref = refs[-5:]

    @pl.when(pl.program_id(0) == 0)
    def _():
        out_ref[...] = jnp.zeros_like(out_ref)
        back_ref[...] = jnp.zeros_like(back_ref)

    ffn_step(
        rows_ref, grad_ref, w_in_ref, w_out_ref, gelu_ref, pre_ref, out_ref, back_ref, turned_ref, 256, 256
    )


def below(values):
    values = jnp.concatenate(
        [jnp.broadcast_to(values, (CAP, 128)), jnp.zeros((384 - CAP, 128), jnp.float32)], axis=0
    )
    values = jnp.transpose(values)[:EXTRA]
    first = values.astype(jnp.bfloat16).astype(jnp.float32)
    second = (values - first).astype(jnp.bfloat16).astype(jnp.float32)
    row = lax.broadcasted_iota(jnp.int32, values.shape, 0)
    values = jnp.where(row == 0, first, jnp.where(row == 1, second, values - first - second))
    return jnp.concatenate([values, jnp.zeros((EXTRA, D - 384), jnp.float32)], axis=1).astype(jnp.bfloat16)


def routed_kernel(senders, *refs):
    row_refs, grad_refs, refs = refs[:senders], refs[senders : 2 * senders], refs[2 * senders :]
    w_in_ref, w_out_ref = refs[:2]
    refs = refs[-2 * senders - 8 :]
    out_refs, back_refs = refs[:senders], refs[senders : 2 * senders]
    gelu_ref, pre_ref, weighted_ref, turned_ref, rows_ref, gate_ref, out_sum, back_sum = refs[2 * senders :]
    step, last = pl.program_id(0), pl.num_programs(0) - 1

    @pl.when(step == 0)
    def _():
        out_sum[...] = jnp.zeros_like(out_sum)
        back_sum[...] = jnp.zeros_like(back_sum)
        for k in range(senders):
            rows = slice(k * CAP, (k + 1) * CAP)
            rows_ref[rows, :] = row_refs[k][:CAP, :]
            pieces = row_refs[k][CAP : CAP + EXTRA, :384].astype(jnp.float32)
            gates = pieces[0:1] + pieces[1:2] + pieces[2:3]
            gate_ref[rows, :] = jnp.transpose(jnp.broadcast_to(gates, (128, 384)))[:CAP]
            weighted = gate_ref[rows, 0:1] * grad_refs[k][...].astype(jnp.float32)
            weighted_ref[rows, :] = weighted.astype(jnp.bfloat16)

    ffn_step(
        rows_ref,
        weighted_ref,
        w_in_ref,
        w_out_ref,
        gelu_ref,
        pre_ref,
        out_sum,
        back_sum,
        turned_ref,
        CAP,
        384,
    )

    @pl.when(step == last)
    def _():
        for k in range(senders):
            rows = slice(k * CAP, (k + 1) * CAP)
            result = out_sum[rows, :]
            out_refs[k][...] = (gate_ref[rows, 0:1] * result).astype(jnp.bfloat16)
            back_refs[k][:CAP, :] = back_sum[rows, :].astype(jnp.bfloat16)
            dots = jnp.sum(
                grad_refs[k][...].astype(jnp.float32) * result.astype(jnp.bfloat16).astype(jnp.float32),
                axis=1,
                keepdims=True,
            )
            back_refs[k][CAP:, :] = below(dots)


def ffn_call(kernel, name, operands, specs, w_in, w_out, place, outs, hidden, scratch, width=512, w_out_spec=None):
    ff, count = w_in.shape[2], outs[hidden].shape[0]
    column = pl.BlockSpec((count, width), lambda step: (0, step))
    out_specs = [column if at in (hidden, hidden + 1) else whole(out.shape) for at, out in enumerate(outs)]
    return pl.pallas_call(
        kernel,
        grid=(ff // width,),
        in_specs=specs
        + [
            pl.BlockSpec((1, D, width), lambda step: (place, 0, step)),
            w_out_spec or pl.BlockSpec((1, width, D), lambda step: (place, step, 0)),
        ],
        out_specs=out_specs,
        out_shape=outs,
        scratch_shapes=scratch,
        compiler_params=pltpu.CompilerParams(vmem_limit_bytes=VMEM),
        cost_estimate=pl.CostEstimate(
            flops=8 * count * D * ff, bytes_accessed=4 * count * ff + 4 * D * ff, transcendentals=count * ff
        ),
        name=name,
    )(*operands, w_in, w_out)


def shared_expert(rows, grad, w_in, w_out):
    kept = jax.ShapeDtypeStruct((LONG, D), jnp.float32)
    hidden = jax.ShapeDtypeStruct((LONG, w_in.shape[1]), jnp.bfloat16)
    turned = jax.ShapeDtypeStruct((D, LONG), jnp.bfloat16)
    full = whole((LONG, D))
    return ffn_call(
        shared_kernel,
        "shared_expert",
        [rows, grad],
        [full, full],
        w_in[None],
        w_out[0],
        0,
        [kept, kept, hidden, hidden, turned],
        2,
        [],
        D,
        w_out[1],
    )


def routed_expert(rows, grads, w_in, w_out, place):
    senders = len(rows)
    count, operands = senders * CAP, list(rows) + list(grads)
    hidden = jax.ShapeDtypeStruct((count, w_in.shape[2]), jnp.bfloat16)
    result = ffn_call(
        lambda *refs: routed_kernel(senders, *refs),
        "routed_expert",
        operands,
        [whole(operand.shape) for operand in operands],
        w_in,
        w_out,
        place,
        [jax.ShapeDtypeStruct((CAP, D), jnp.bfloat16)] * senders
        + [jax.ShapeDtypeStruct((CAP + EXTRA, D), jnp.bfloat16)] * senders
        + [
            hidden,
            hidden,
            jax.ShapeDtypeStruct((count, D), jnp.bfloat16),
            jax.ShapeDtypeStruct((D, count), jnp.bfloat16),
        ],
        2 * senders,
        [
            pltpu.VMEM((count, D), jnp.bfloat16),
            pltpu.VMEM((count, 128), jnp.float32),
            pltpu.VMEM((count, D), jnp.float32),
            pltpu.VMEM((count, D), jnp.float32),
        ],
    )
    return (result[:senders], result[senders : 2 * senders]) + tuple(result[2 * senders :])


def expert_outer_kernel(added, which_ref, gelu_ref, grad_ref, rows_ref, pre_ref, *refs):
    out_ref, step = refs[-1], pl.program_id(0)
    chips, tall = out_ref.shape[0], gelu_ref.shape[1]
    depth, count = rows_ref.shape[2:]

    @pl.when(step < chips)
    def _():
        result = product_tn(gelu_ref[...], grad_ref[...])
        if added:
            result = result + refs[0][step, :tall, :].astype(jnp.float32)
        out_ref[step, :tall, :] = result.astype(jnp.bfloat16)

    @pl.when(step >= chips)
    def _():
        result = product(rows_ref[...].reshape(chips * depth, count), pre_ref[...])
        result = result.reshape(chips, depth, D)
        place = pl.ds(pl.multiple_of(tall + (step - chips) * depth, 32), depth)
        if added:
            result = result + refs[0][:, place, :].astype(jnp.float32)
        out_ref[:, place, :] = result.astype(jnp.bfloat16)


def attention_outer_kernel(added, which_ref, normed_ref, mixed_ref, projected_ref, grad_ref, *refs):
    out_ref, step = refs[-1], pl.program_id(0)
    chips = out_ref.shape[0]
    depth, count = normed_ref.shape[2:]
    place = pl.ds(pl.multiple_of(step * depth, 32), depth)

    def put(left_ref, right_ref):
        result = product(left_ref[...].reshape(chips * depth, count), right_ref[...])
        result = result.reshape(chips, depth, D)
        if added:
            result = result + refs[0][:, place, :].astype(jnp.float32)
        out_ref[:, place, :] = result.astype(jnp.bfloat16)

    @pl.when(step < 3)
    def _():
        put(normed_ref, projected_ref)

    @pl.when(step == 3)
    def _():
        put(mixed_ref, grad_ref)


def outer_call(kernel, name, steps, which, operands, specs, rows, came, tokens, flops):
    chips = lax.axis_size("dp") // 2
    full = whole((chips, rows, D))
    extra = [] if came is None else [came]
    return pl.pallas_call(
        lambda *refs: kernel(came is not None, *refs),
        grid_spec=pltpu.PrefetchScalarGridSpec(
            num_scalar_prefetch=1,
            grid=(steps,),
            in_specs=specs + [full] * len(extra) + [HBM] * len(tokens),
            out_specs=full,
        ),
        out_shape=jax.ShapeDtypeStruct((chips, rows, D), jnp.bfloat16),
        compiler_params=pltpu.CompilerParams(vmem_limit_bytes=VMEM),
        cost_estimate=pl.CostEstimate(
            flops=flops,
            bytes_accessed=sum(2 * operand.size for operand in operands) + 4 * chips * rows * D,
            transcendentals=0,
        ),
        name=name,
    )(jnp.reshape(which, (1,)).astype(jnp.int32), *operands, *extra, *tokens)


def by_device(turned):
    n_dp = lax.axis_size("dp")
    return turned.reshape(n_dp // 2, 2, turned.shape[0] // n_dp, turned.shape[1])


def plain_outer(pairs):
    n_dp = lax.axis_size("dp")

    def make(which, came, tokens):
        parts = []
        for turned, right in pairs:
            result = product(turned, right).reshape(n_dp // 2, 2, turned.shape[0] // n_dp, right.shape[1])
            result = at_place(result, which, 1).reshape(n_dp // 2, -1, right.shape[1] // D, D)
            parts.append(jnp.swapaxes(result, 1, 2).reshape(n_dp // 2, -1, D))
        parts = jnp.concatenate(parts, axis=1)
        parts = parts if came is None else parts + came.astype(jnp.float32)
        return parts.astype(jnp.bfloat16)

    return make


def expert_outer(gelu, grad, turned, grad_pre):
    n_dp, (count, ff) = lax.axis_size("dp"), gelu.shape
    chips, tall, depth = n_dp // 2, ff // n_dp, D // n_dp
    if tall % 128 or depth % 32:
        return plain_outer([(jnp.swapaxes(gelu, 0, 1), grad), (turned, grad_pre)])
    turned = by_device(turned)
    specs = [
        pl.BlockSpec((count, tall), lambda i, which: (0, 2 * jnp.minimum(i, chips - 1) + which[0])),
        whole((count, D)),
        pl.BlockSpec((chips, 1, depth, count), lambda i, which: (0, which[0], 0, 0)),
        pl.BlockSpec((count, D), lambda i, which: (0, jnp.maximum(i - chips, 0))),
    ]
    return lambda which, came, tokens: outer_call(
        expert_outer_kernel,
        "expert_outer",
        chips + ff // D,
        which,
        [gelu, grad, turned, grad_pre],
        specs,
        tall + ff // D * depth,
        came,
        tokens,
        2 * count * D * ff,
    )


def attention_outer(left, grad_projected, grad_att):
    n_dp = lax.axis_size("dp")
    chips, depth = n_dp // 2, D // n_dp
    if depth % 32:
        return plain_outer([(left[0], grad_projected), (left[1], grad_att)])
    own = pl.BlockSpec((chips, 1, depth, LONG), lambda i, which: (0, which[0], 0, 0))
    specs = [
        own,
        own,
        pl.BlockSpec((LONG, D), lambda i, which: (0, jnp.minimum(i, 2))),
        whole((LONG, D)),
    ]
    operands = [by_device(left[0]), by_device(left[1]), grad_projected, grad_att]
    return lambda which, came, tokens: outer_call(
        attention_outer_kernel,
        "attention_outer",
        4,
        which,
        operands,
        specs,
        4 * depth,
        came,
        tokens,
        4 * LONG * D * D,
    )


def to_core(make, tokens=()):
    return make(1 - lax.axis_index("dp") % 2, None, list(tokens))


def from_core(sent):
    return lax.ppermute(sent, "dp", [(i, i ^ 1) for i in range(lax.axis_size("dp"))])


def with_core(make, came, tokens=()):
    return make(lax.axis_index("dp") % 2, came, list(tokens))


def combine_kernel(count, dotted, ids_ref, slots_ref, base_ref, *refs):
    block_refs, refs = refs[:count], refs[count:]
    out_ref, dots_out_ref, rows_ref, dots_ref = refs
    size = block_refs[0].shape[0]

    @pl.when(pl.program_id(0) == 0)
    def _():
        for at, block_ref in enumerate(block_refs):
            rows_ref[at * size : (at + 1) * size, :] = block_ref[...]
            if dotted:
                pieces = block_ref[CAP:, :size].astype(jnp.float32)
                dots_ref[:, at * size : (at + 1) * size] = pieces[0:1] + pieces[1:2] + pieces[2:3]

    ids = ids_ref[...]
    first, second = slots_ref[:, 0:1] == ids, slots_ref[:, 1:2] == ids
    hold = jnp.where(first | second, 1.0, 0.0).astype(jnp.bfloat16)
    out_ref[...] = base_ref[...] + product(hold, rows_ref[...])
    if dotted:
        dots = dots_ref[...]
        dots_out_ref[:, 0:1] = jnp.sum(jnp.where(first, dots, 0.0), axis=1, keepdims=True)
        dots_out_ref[:, 1:2] = jnp.sum(jnp.where(second, dots, 0.0), axis=1, keepdims=True)


def combine(ids, slots, base, blocks, dotted):
    total = ids.shape[1]
    patch = pl.BlockSpec((SHORT, D), lambda i: (i, 0))
    pair = pl.BlockSpec((SHORT, 2), lambda i: (i, 0))
    return pl.pallas_call(
        lambda *refs: combine_kernel(len(blocks), dotted, *refs),
        grid=(BLOCKS,),
        in_specs=[whole(ids.shape), pair, patch] + [whole(block.shape) for block in blocks],
        out_specs=[patch, pair],
        out_shape=[
            jax.ShapeDtypeStruct((LONG, D), jnp.float32),
            jax.ShapeDtypeStruct((LONG, 2), jnp.float32),
        ],
        scratch_shapes=[pltpu.VMEM((total, D), jnp.bfloat16), pltpu.VMEM((1, total), jnp.float32)],
        compiler_params=pltpu.CompilerParams(vmem_limit_bytes=VMEM),
        cost_estimate=pl.CostEstimate(
            flops=2 * LONG * total * D, bytes_accessed=2 * total * D + 8 * LONG * D, transcendentals=0
        ),
        name="combine",
    )(ids, slots, base, *blocks)


def sums_kernel(groups, *refs):
    out_ref, in_ref = refs[-2:]
    depth, wide = in_ref.shape[1:]
    expert, step = pl.program_id(0), pl.program_id(1)
    start = 0
    for at, count in enumerate(groups):
        parts = refs[start : start + count]
        start += count

        @pl.when(expert == at)
        def _(parts=parts):
            total = parts[0][...].astype(jnp.float32)
            for part in parts[1:]:
                total = total + part[...].astype(jnp.float32)

            @pl.when(step == 0)
            def _():
                out_ref[0] = total

            @pl.when(step == 1)
            def _():
                for j in range(wide // D):
                    in_ref[0, :, j * D : (j + 1) * D] = total[j * depth : (j + 1) * depth, :]


def expert_sums(pieces, tall, depth, wide):
    count = len(pieces)

    def spec(at, row):
        def index(expert, step):
            return row // tall + jnp.where(expert == at, step, 0 if at else 1), 0

        return pl.BlockSpec((tall, D), index)

    return pl.pallas_call(
        lambda *refs: sums_kernel([len(group) for group in pieces], *refs),
        grid=(count, 2),
        in_specs=[spec(at, row) for at, group in enumerate(pieces) for _, row in group],
        out_specs=[
            pl.BlockSpec((1, tall, D), lambda expert, step: (expert, 0, 0)),
            pl.BlockSpec((1, depth, wide), lambda expert, step: (expert, 0, 0)),
        ],
        out_shape=[
            jax.ShapeDtypeStruct((count, tall, D), jnp.float32),
            jax.ShapeDtypeStruct((count, depth, wide), jnp.float32),
        ],
        compiler_params=pltpu.CompilerParams(vmem_limit_bytes=VMEM),
        cost_estimate=pl.CostEstimate(
            flops=0, bytes_accessed=32 * count * tall * D, transcendentals=0
        ),
        name="expert_sums",
    )(*[array for group in pieces for array, _ in group])


def dispatch_kernel(count, ids_ref, slots_ref, gates_ref, rows_ref, *out_refs):
    size = ids_ref.shape[0] // count
    for at, out_ref in enumerate(out_refs):
        ids = ids_ref[at * size : (at + 1) * size, :]
        first, second = slots_ref[0:1, :] == ids, slots_ref[1:2, :] == ids
        hold = jnp.where(first | second, 1.0, 0.0).astype(jnp.bfloat16)
        out_ref[:CAP, :] = product(hold, rows_ref[...])[:CAP].astype(jnp.bfloat16)
        gates = jnp.where(first, gates_ref[0:1, :], 0.0) + jnp.where(second, gates_ref[1:2, :], 0.0)
        out_ref[CAP:, :] = below(jnp.sum(gates, axis=1, keepdims=True)[:CAP])


def dispatch(ids, slots, gates, rows, count):
    size = ids.shape[0] // count
    return pl.pallas_call(
        lambda *refs: dispatch_kernel(count, *refs),
        out_shape=[jax.ShapeDtypeStruct((size, D), jnp.bfloat16)] * count,
        compiler_params=pltpu.CompilerParams(vmem_limit_bytes=VMEM),
        cost_estimate=pl.CostEstimate(
            flops=2 * LONG * ids.shape[0] * D, bytes_accessed=2 * (LONG + ids.shape[0]) * D, transcendentals=0
        ),
        name="dispatch",
    )(ids, slots, gates, rows)


def gather_kernel(n_dp, n_ex, own_ref, all_ref, here_sem, z_out, z_in, chip_out, chip_in, core_out, core_in):
    dp, ex = lax.axis_index("dp"), lax.axis_index("expert")
    chips = n_dp // 2

    def along(axis, distance):
        if axis == "expert":
            return (dp, ex ^ distance)
        return (dp ^ distance, ex)

    routes = (
        [("expert", k) for k in range(1, n_ex)] + [("dp", 2 * k) for k in range(1, chips)] + [("dp", 1)]
    )
    barrier = pltpu.get_barrier_semaphore()
    for route in routes:
        pl.semaphore_signal(barrier, inc=1, device_id=along(*route), device_id_type=pl.DeviceIdType.MESH)
    pl.semaphore_wait(barrier, len(routes))

    def send(source, target, sent, came, device):
        copy = pltpu.make_async_remote_copy(
            src_ref=source,
            dst_ref=target,
            send_sem=sent,
            recv_sem=came,
            device_id=device,
            device_id_type=pl.DeviceIdType.MESH,
        )
        copy.start()
        return copy

    def wait_for(target, came):
        pltpu.make_async_remote_copy(
            src_ref=target,
            dst_ref=target,
            send_sem=came,
            recv_sem=came,
            device_id=(dp, ex),
            device_id_type=pl.DeviceIdType.MESH,
        ).wait_recv()

    def group(device, first=0, count=n_ex):
        return all_ref.at[pl.ds(device * n_ex + first, count)]

    mine = all_ref.at[dp * n_ex + ex]
    here = pltpu.make_async_copy(own_ref, mine, here_sem)
    here.start()
    sends = [
        send(own_ref, mine, z_out.at[k], z_in.at[k], along("expert", k)) for k in range(1, n_ex)
    ]
    for k in range(1, n_ex):
        wait_for(all_ref.at[dp * n_ex + (ex ^ k)], z_in.at[k])
    here.wait()
    direct = [1, 2] if chips == 4 else list(range(1, chips))
    for k in direct:
        sends.append(send(group(dp), group(dp), chip_out.at[k], chip_in.at[k], along("dp", 2 * k)))
    sends.append(send(group(dp), group(dp), core_out.at[0], core_in.at[0], along("dp", 1)))
    for k in direct:
        other = dp ^ (2 * k)
        wait_for(group(other), chip_in.at[k])
        if chips == 4:
            part = group(other, (k - 1) * (n_ex // 2), n_ex // 2)
            sends.append(send(part, part, chip_out.at[2 + k], chip_in.at[2 + k], along("dp", 2 * (3 - k))))
        sends.append(send(group(other), group(other), core_out.at[k], core_in.at[k], along("dp", 1)))
    if chips == 4:
        other = dp ^ 6
        for k in direct:
            wait_for(group(other, (k - 1) * (n_ex // 2), n_ex // 2), chip_in.at[2 + k])
        sends.append(send(group(other), group(other), core_out.at[3], core_in.at[3], along("dp", 1)))
    for k in range(chips):
        wait_for(group(dp ^ (2 * k) ^ 1), core_in.at[k])
    for copy in sends:
        copy.wait_send()


def gather(own):
    n_dp, n_ex = lax.axis_size("dp"), lax.axis_size("expert")
    chips = n_dp // 2
    counts = (n_ex, n_ex, max(chips, 5), max(chips, 5), chips, chips)
    return pl.pallas_call(
        lambda *refs: gather_kernel(n_dp, n_ex, *refs),
        in_specs=[HBM],
        out_specs=HBM,
        out_shape=jax.ShapeDtypeStruct((n_dp * n_ex,) + own.shape, own.dtype),
        scratch_shapes=[pltpu.SemaphoreType.DMA] + [pltpu.SemaphoreType.DMA((count,)) for count in counts],
        compiler_params=pltpu.CompilerParams(collective_id=0, has_side_effects=True),
        cost_estimate=pl.CostEstimate(flops=0, bytes_accessed=64 * own.size, transcendentals=0),
        name="gather",
    )(own)


def swap(parts, axis):
    return lax.all_to_all(parts, axis, 0, 0, tiled=True)


def at_place(parts, place, axis=0):
    return lax.dynamic_index_in_dim(parts, place, axis, keepdims=False)


def from_expert(parts):
    size, me = parts.shape[0], lax.axis_index("expert")
    arrived = [at_place(parts, me)]
    for distance in range(1, size):
        route = [(i, i ^ distance) for i in range(size)]
        arrived.append(lax.ppermute(at_place(parts, me ^ distance), "expert", route))
    return arrived


def together(live, work, *operands):
    def never(*operands):
        return jax.tree.map(lambda out: jnp.zeros(out.shape, out.dtype), jax.eval_shape(work, *operands))

    return lax.cond(live, work, never, *operands)


def to_expert(blocks, distances=None):
    size = len(blocks)
    return [
        lax.ppermute(blocks[distance], "expert", [(i, i ^ distance) for i in range(size)])
        if distance
        else blocks[0]
        for distance in (range(size) if distances is None else distances)
    ]


def from_chips(parts, distances):
    chips, me = lax.axis_size("dp") // 2, lax.axis_index("dp") // 2
    arrived = []
    for distance in distances if parts else []:
        route = [(i, i ^ (2 * distance)) for i in range(2 * chips)]
        part = jnp.concatenate([at_place(array, me ^ distance) for array in parts], axis=0)
        arrived.append(lax.ppermute(part, "dp", route) if distance else part)
    return arrived


def total_of(arrived):
    total = arrived[0].astype(jnp.float32)
    for part in arrived[1:]:
        total = total + part.astype(jnp.float32)
    return total


def body(
    tokens,
    bucket,
    image_length,
    routes,
    cotangent,
    w_qkv,
    w_out,
    w_ada,
    b_ada,
    w_router,
    w_shared_in,
    w_shared_out,
    w_expert_in,
    w_expert_out,
):
    n_dp, n_ex = lax.axis_size("dp"), lax.axis_size("expert")
    n, chips = n_dp * n_ex, n_dp // 2
    dp = lax.axis_index("dp")
    share = D // n
    ff = w_shared_in.shape[1]
    wide = w_ada.shape[1]
    column = wide // n

    ada_parts = jnp.swapaxes(w_ada.reshape(share, n, column), 0, 1)
    bucket_row = jnp.zeros((1, 1, column), jnp.bfloat16).at[0, 0, :BLOCKS].set(bucket.astype(jnp.bfloat16))
    ada_parts = jnp.concatenate([ada_parts, jnp.broadcast_to(bucket_row, (n, 1, column))], axis=1)
    ada_parts = swap(ada_parts, BOTH)
    ada_columns = ada_parts[:, :share].reshape(D, column)
    buckets = ada_parts[:, share, :BLOCKS].astype(jnp.int32).reshape(n * BLOCKS)
    condition = jax.nn.silu(embed(buckets)).astype(jnp.bfloat16)
    modulation = product(condition, ada_columns) + b_ada.astype(jnp.float32)
    w_qkv = w_qkv + (0.0 * modulation[0, 0]).astype(jnp.bfloat16)
    modulation = swap(modulation.reshape(n, BLOCKS, column), BOTH)
    modulation = jnp.swapaxes(modulation, 0, 1).reshape(BLOCKS, wide)

    def span(index):
        return expand(modulation[:, index * D : (index + 1) * D])

    shift_one, scale_one, gate_one, shift_two, scale_two, gate_two = [span(index) for index in range(6)]

    w_qkv = gather(w_qkv).reshape(D, 3 * D)
    router_rows = jnp.zeros((8, D), jnp.bfloat16).at[0, : share * EXPERTS].set(w_router.reshape(-1))
    packed = jnp.concatenate(
        [w_shared_out, w_out]
        + [w_shared_in[:, at * D : (at + 1) * D] for at in range(ff // D)]
        + [router_rows],
        axis=0,
    )
    packed = lax.all_gather(packed, BOTH, axis=0, tiled=False)
    start = ff // n
    w_out = packed[:, start : start + share].reshape(D, D)
    w_shared_in = jnp.concatenate(
        [
            packed[:, start + (1 + at) * share : start + (2 + at) * share].reshape(D, D)
            for at in range(ff // D)
        ],
        axis=1,
    )
    w_router = packed[:, start + (1 + ff // D) * share, : share * EXPERTS].reshape(D, EXPERTS)
    if start % 16 == 0:
        w_shared_out = packed, pl.BlockSpec((D // start, start, D), lambda step: (step, 0, 0))
    else:
        w_shared_out = packed[:, :start].reshape(1, ff, D), None

    choose = [routes[:, k : k + 1] == jnp.arange(EXPERTS, dtype=jnp.int32)[None, :] for k in range(2)]
    named = (choose[0] | choose[1]).astype(jnp.bfloat16)
    position = jnp.arange(LONG, dtype=jnp.int32)
    earlier = (position[:, None] > position[None, :]).astype(jnp.bfloat16)
    before = product(earlier, named)
    slots = [
        routes[:, k] * CAP + jnp.sum(jnp.where(choose[k], before, 0.0), axis=1).astype(jnp.int32)
        for k in range(2)
    ]
    local = EXPERTS // n_ex
    ex = lax.axis_index("expert")
    near = jnp.stack([ex ^ k for k in range(n_ex)]).astype(jnp.int32)

    def slot_ids(which, size):
        place = jnp.arange(size, dtype=jnp.int32)
        experts = jnp.asarray(which, jnp.int32)[:, None] + near[None, :] * local
        return jnp.where(place < CAP, (experts * CAP)[:, :, None] + place, -1).reshape(-1)

    def hold(at, size):
        ids = slot_ids([at], size)[:, None]
        return ((ids == slots[0][None, :]) | (ids == slots[1][None, :])).astype(jnp.bfloat16)

    slot_pairs = jnp.stack(slots, axis=1)

    grad_out = cotangent.astype(jnp.float32)
    grad_mlp = (gate_two * grad_out).astype(jnp.bfloat16)

    def grad_blocks(at, grad_mlp):
        blocks = product(hold(at, CAP), grad_mlp).astype(jnp.bfloat16).reshape(n_ex, CAP, D)
        return [blocks[k] for k in range(n_ex)]

    grad_sent = grad_blocks(0, grad_mlp)
    live = image_length[0] > 0

    inputs_full = tokens.astype(jnp.float32)
    hat_one, inverse_one = normalize(inputs_full)
    normed_one = (hat_one * (1.0 + scale_one) + shift_one).astype(jnp.bfloat16)
    projected = product(normed_one, w_qkv).astype(jnp.bfloat16)
    def attention_part(projected, blocks, grad_mlp):
        others = [grad_blocks(at, grad_mlp) for at in range(1, local)]
        return *attend(image_length, projected), to_expert(blocks), others

    attended, log_total, grad_rows, grad_sent = together(
        live, attention_part, projected, grad_sent, grad_mlp
    )
    grad_rows = [grad_rows]
    branch_att = product(attended, w_out)
    hidden_one = inputs_full + gate_one * branch_att
    hat_two, inverse_two = normalize(hidden_one)
    normed_two = (hat_two * (1.0 + scale_two) + shift_two).astype(jnp.bfloat16)

    logits = product(normed_two, w_router)
    picked_logits = jnp.stack([jnp.sum(jnp.where(pick, logits, 0.0), axis=-1) for pick in choose], axis=-1)
    gate_weights = jax.nn.softmax(picked_logits, axis=-1)
    full = CAP + EXTRA

    blocks = dispatch(
        slot_ids(range(local), full)[:, None],
        jnp.stack(slots),
        jnp.swapaxes(gate_weights, 0, 1),
        normed_two,
        local * n_ex,
    )
    sent = [blocks[at * n_ex : (at + 1) * n_ex] for at in range(local)]

    tall = ff // n_dp
    size = tall + ff // D * (D // n_dp)
    near_chips, far_chips = list(range(min(3, chips))), list(range(3, chips))

    def split_expert(part):
        blocks = jnp.swapaxes(part[tall:].reshape(ff // D, D // n_dp, D), 0, 1)
        return part[:tall], blocks.reshape(D // n_dp, ff)

    pieces = [[] for _ in range(1 + local)]

    def note(arrays, *which):
        for row, at in enumerate(which):
            pieces[at] += [(array, row * size) for array in arrays]

    def sum_of(at):
        return total_of([array[row : row + size] for array, row in pieces[at]])

    def first_part(normed_two, grad_mlp, blocks):
        results = shared_expert(normed_two, grad_mlp, w_shared_in, w_shared_out)
        half = to_core(expert_outer(results[2], grad_mlp, results[4], results[3]))
        return results, half, to_expert(blocks)

    results, shared_half, arrived = together(live, first_part, normed_two, grad_mlp, sent[0])
    shared, grad_normed_two, gelu_shared, grad_pre_shared, turned_shared = results

    def second_part(rows, grads, others):
        results = routed_expert(rows, grads, w_expert_in, w_expert_out, 0)
        half = to_core(expert_outer(results[2], results[4], results[5], results[3]))
        return results, half, [to_expert(blocks) for blocks in others]

    def weights_part(gelu, weighted, turned, grad_pre, half, shared_half, grads):
        came = [from_core(half), from_core(shared_half)]
        kept = [with_core(expert_outer(gelu, weighted, turned, grad_pre), came[0])]
        make = expert_outer(gelu_shared, grad_mlp, turned_shared, grad_pre_shared)
        kept.append(with_core(make, came[1], kept))
        return kept, [to_expert(blocks) for blocks in grads]

    results, half, others = together(live, second_part, arrived, grad_rows[0], sent[1:])
    outs, backs, gelu, grad_pre, weighted, turned_rows = results
    arrived = [arrived] + others
    (kept_first, kept_shared), others = together(
        live, weights_part, gelu, weighted, turned_rows, grad_pre, half, shared_half, grad_sent
    )
    grad_rows += others
    out_rows, grad_home, kept_last = [outs], [], []

    def third_part(rows, grads, at, backs, kept):
        results = routed_expert(rows, grads, w_expert_in, w_expert_out, at)
        half = to_core(expert_outer(results[2], results[4], results[5], results[3]))
        return results, half, to_expert(backs), from_chips(kept, near_chips)

    def fourth_part(gelu, weighted, turned, grad_pre, half, backs, kept):
        kept_now = with_core(expert_outer(gelu, weighted, turned, grad_pre), from_core(half))
        return kept_now, to_expert(backs), from_chips(kept, far_chips), [turn(normed_one), turn(attended)]

    if local == 1:
        turned = [turn(normed_one), turn(attended)]
        backs = to_expert(backs)
        note(from_chips([kept_first], near_chips), 0)
        note(from_chips([kept_shared], near_chips + far_chips), 1)
    for at in range(1, local):
        results, half, home, part = together(
            live,
            lambda rows, grads, backs, kept, at=at: third_part(rows, grads, at, backs, kept),
            arrived[at],
            grad_rows[at],
            backs,
            [kept_first, kept_shared] if at == 1 else kept_last[-1:],
        )
        note(part, *((0, 1) if at == 1 else (at,)))
        outs, backs, gelu, grad_pre, weighted, turned_rows = results
        out_rows.append(outs)
        grad_home.append(home)
        kept_now, backs, part, turned = together(
            live,
            fourth_part,
            gelu,
            weighted,
            turned_rows,
            grad_pre,
            half,
            backs,
            [kept_shared] if at == 1 else kept_last[-1:],
        )
        note(part, 1 if at == 1 else at)
        kept_last.append(kept_now)
    grad_home.append(backs)

    def fifth_part(grad_normed_two, grad_home, others, kept):
        ids = slot_ids(range(local), full)[None, :]
        grad_normed_two, grad_gates = combine(ids, slot_pairs, grad_normed_two, sum(grad_home, []), True)
        grad_picked = gate_weights * (
            grad_gates - jnp.sum(gate_weights * grad_gates, axis=1, keepdims=True)
        )
        grad_logits = jnp.where(choose[0], grad_picked[:, 0:1], 0.0) + jnp.where(
            choose[1], grad_picked[:, 1:2], 0.0
        )
        logit_parts = jnp.concatenate(split_three(grad_logits), axis=1).astype(jnp.bfloat16)
        grad_router = product_tn(normed_two, logit_parts).reshape(D, 3, EXPERTS).sum(axis=1)
        grad_normed_two = grad_normed_two + product_nt(
            logit_parts, jnp.concatenate([w_router, w_router, w_router], axis=1)
        )

        grad_hidden_one = cotangent.astype(jnp.float32) + norm_back(
            grad_normed_two * (1.0 + span(4)), hat_two, inverse_two
        )
        grad_att = (span(2) * grad_hidden_one).astype(jnp.bfloat16)
        grad_attended = product_nt(grad_att, w_out).astype(jnp.bfloat16)
        grad_spans = [
            block_sums(grad_hidden_one * product(attended, w_out)),
            block_sums(grad_normed_two),
            block_sums(grad_normed_two * hat_two),
        ]
        results = (grad_router, grad_spans, grad_hidden_one, grad_att, grad_attended)
        return results, [to_expert(blocks) for blocks in others], from_chips(kept, near_chips)

    results, returned, part = together(
        live, fifth_part, grad_normed_two, grad_home, out_rows[:-1], kept_last[-1:]
    )
    grad_router, grad_spans, grad_hidden_one, grad_att, grad_attended = results
    note(part, local)

    def sixth_part(projected, grad_attended, attended, log_total, blocks, kept):
        result = attend_back(image_length, projected, grad_attended, attended, log_total)
        half = to_core(attention_outer(turned, result, grad_att))
        grad_shared_out, grad_shared_in = split_expert(sum_of(1).astype(jnp.bfloat16))
        rows = (D // n_dp) * (ff // n_ex) // D
        shared_parts = jnp.concatenate(
            [
                jnp.swapaxes(grad_shared_in.reshape(D // n_dp, n_ex, ff // n_ex), 0, 1).reshape(
                    n_ex, rows, D
                ),
                jnp.swapaxes(grad_shared_out.reshape(ff // n_dp, n_ex, D // n_ex), 0, 1).reshape(
                    n_ex, rows, D
                ),
            ],
            axis=1,
        )
        return result, half, to_expert(blocks), from_chips(kept, far_chips), shared_parts

    grad_projected, half, rows, part, shared_parts = together(
        live,
        sixth_part,
        projected,
        grad_attended,
        attended,
        log_total,
        out_rows[-1],
        [kept_first] + kept_last[-1:],
    )
    note(part, *([0, local] if local > 1 else [0]))
    returned.append(rows)

    def seventh_part(grad_projected, half, shared_parts):
        came = from_core(half)
        grad_normed_one = product_nt(grad_projected, w_qkv)
        hat_one, inverse_one = normalize(tokens.astype(jnp.float32))
        grad_input = grad_hidden_one + norm_back(
            grad_normed_one * (1.0 + span(1)), hat_one, inverse_one
        )
        spans = [block_sums(grad_normed_one), block_sums(grad_normed_one * hat_one)]
        kept = with_core(attention_outer(turned, grad_projected, grad_att), came)
        return grad_input.astype(jnp.bfloat16), spans, kept, from_expert(shared_parts)

    grad_input, spans, kept, shared_parts = together(
        live, seventh_part, grad_projected, half, shared_parts
    )

    def eighth_part(kept, returned):
        arrived = from_chips([kept], list(range(chips)))
        routed = [group for at, group in enumerate(pieces) if at != 1]
        grad_expert_out, grad_expert_in = expert_sums(routed, tall, D // n_dp, ff)
        ids = slot_ids(range(local), CAP)[None, :]
        branch_mlp = combine(ids, slot_pairs, shared, sum(returned, []), False)[0]
        result = hidden_one + span(5) * branch_mlp
        last_span = block_sums(cotangent.astype(jnp.float32) * branch_mlp)
        return arrived, grad_expert_out, grad_expert_in, result.astype(jnp.bfloat16), last_span

    attention_parts, grad_expert_out, grad_expert_in, result, last_span = together(
        live, eighth_part, kept, returned
    )
    grad_modulation = jnp.concatenate(spans + grad_spans + [last_span], axis=1)

    own_wide, router_rows, router_columns = wide // n_ex, D // n_dp, EXPERTS // n_ex
    by_expert = jnp.swapaxes(grad_modulation.reshape(BLOCKS, n_ex, own_wide), 0, 1)
    message = jnp.concatenate(
        [
            jnp.broadcast_to(
                by_expert.reshape(1, n_ex, BLOCKS * own_wide), (n_dp, n_ex, BLOCKS * own_wide)
            ),
            jnp.sum(grad_modulation, axis=0).reshape(n_dp, n_ex, column),
            jnp.swapaxes(grad_router.reshape(n_dp, router_rows, n_ex, router_columns), 1, 2).reshape(
                n_dp, n_ex, router_rows * router_columns
            ),
        ],
        axis=2,
    )
    length = message.shape[2]
    message = jnp.pad(message, ((0, 0), (0, 0), (0, -length % 128))).reshape(n, -1, 128)
    message = swap(message, BOTH).reshape(n, -1)
    at = BLOCKS * own_wide
    every_modulation = message[:, :at].reshape(n * BLOCKS, own_wide)
    grad_b_ada = jnp.sum(message[:, at : at + column], axis=0)
    grad_router = jnp.sum(message[:, at + column : length], axis=0).reshape(router_rows, router_columns)
    own_condition = lax.dynamic_slice_in_dim(condition, dp * (D // n_dp), D // n_dp, axis=1)

    attention_parts = total_of(attention_parts).astype(jnp.bfloat16).reshape(4, D // n_dp, D)
    attention_parts = jnp.concatenate(
        [
            jnp.swapaxes(attention_parts[:3], 0, 1).reshape(D // n_dp, n_ex, 3 * D // n_ex),
            attention_parts[3].reshape(D // n_dp, n_ex, D // n_ex),
        ],
        axis=2,
    )
    rest = (D // n_dp) * 4 // n_ex
    attention_parts = jnp.swapaxes(attention_parts, 0, 1).reshape(n_ex, rest, D)

    parts = together(live, from_expert, attention_parts)
    grad_w_ada = lax.dot_general(
        own_condition.astype(jnp.float32),
        every_modulation,
        (((0,), (0,)), ((), ())),
        precision=HIGHEST,
        preferred_element_type=jnp.float32,
    )
    attention_parts = total_of(parts).reshape(D // n_dp, 4 * D // n_ex)
    shared_parts = total_of(shared_parts)
    half = shared_parts.shape[0] // 2
    return (
        result,
        grad_input,
        attention_parts[:, : 3 * D // n_ex],
        attention_parts[:, 3 * D // n_ex :],
        grad_w_ada,
        grad_b_ada,
        grad_router,
        shared_parts[:half].reshape(D // n_dp, ff // n_ex),
        shared_parts[half:].reshape(ff // n_dp, D // n_ex),
        grad_expert_in,
        grad_expert_out,
    )


def solution(mesh):
    rows, flat = P(BOTH, None), P(BOTH)
    spread = P("dp", "expert")
    return jax.shard_map(
        body,
        mesh=mesh,
        in_specs=(
            rows,
            flat,
            flat,
            rows,
            rows,
            rows,
            rows,
            rows,
            flat,
            rows,
            rows,
            rows,
            P("expert", None, None),
            P("expert", None, None),
        ),
        out_specs=(
            rows,
            rows,
            spread,
            spread,
            spread,
            flat,
            spread,
            spread,
            spread,
            P("expert", "dp", None),
            P("expert", "dp", None),
        ),
        check_vma=False,
    )
```

time: 1690 us -> 693 us (0.41)
  waiting for transfers between devices: 799 us -> 74 us
  Pallas kernels: 0 us -> 364 us
  matrix products: 396 us -> 34.3 us
  blocking collectives: 127 us -> 0 us
  local copies, waits for them, and re-layouts: 153 us -> 69.7 us
  other arithmetic: 133 us -> 56.8 us
  starting transfers between devices: 46.2 us -> 64 us
    pallas_call x0 -> x20, Pallas kernels: none -> 364 us  [the longest x8 101 us: outer_call(): pl.pallas_call(lambda *refs: kernel(came is not None, *refs), grid_spec=p...]
    dot_general x20 -> x5, matrix products: 322 us -> 16.4 us  [the longest x3 14.1 us: product_nt(): lax.dot_general(left_side, right_side, (((1,), (1,)), ((), ())), preferre...]
    unnamed x25 -> x1, waiting for transfers between devices: 263 us -> 0.02 us
    reduce_scatter x8 -> x0, waiting for transfers between devices: 237 us -> none  [the longest x1 78.4 us: body(): lax.psum_scatter(grad_expert_out.astype(jnp.bfloat16), 'dp', scatter_dime...]
    all_to_all x4 -> x3, waiting for transfers between devices: 186 us -> 6.27 us  [swap(): return lax.all_to_all(parts, axis, 0, 0, tiled=True)]
    all_gather x5 -> x1, waiting for transfers between devices: 113 us -> 0.02 us  [body(): packed = lax.all_gather(packed, BOTH, axis=0, tiled=False)]
    ppermute x0 -> x43, waiting for transfers between devices: none -> 67.7 us  [the longest x6 33.6 us: from_expert(): lax.ppermute(at_place(parts, me ^ distance), 'expert', route)]
    all_gather x1 -> x0, blocking collectives: 65.3 us -> none  [body(): lax.all_gather(w_router, ('dp', 'expert'), axis=0, tiled=True)]
  transfers between devices with their start and end apart: 23 -> 47, of which waited for: 18 -> 12; matrix products, arithmetic and copies ran while one was open for 39% -> 15% of each run, Pallas kernels for 0% -> 51%
where the time goes in v1:
time: 693 us; the launch traced here: 682 us
  Pallas kernels  364 us (53%)
  waiting for transfers between devices  74 us (11%)
  local copies, waits for them, and re-layouts  69.7 us (10%)
  starting transfers between devices  64 us (9%)
  other arithmetic  56.8 us (8%)
  matrix products  34.3 us (5%)
  between operations  15.8 us (2%)
    pallas_call x8, Pallas kernels, outer_call(): pl.pallas_call(lambda *refs: kernel(came is not None, *refs), grid_spec=p...  101 us
    pallas_call x3, Pallas kernels, ffn_call(): pl.pallas_call(kernel, grid=(ff // width,), in_specs=specs + [pl.BlockSpe...  96.3 us
    pallas_call x1, Pallas kernels, gather(): pl.pallas_call(lambda *refs: gather_kernel(n_dp, n_ex, *refs), in_specs=[...  53.2 us
    pallas_call x1, Pallas kernels, attend_back(): pl.pallas_call(attend_back_kernel, grid=(PAIRS,), in_specs=[pl.BlockSpec(...  42.4 us
    ppermute x6, waiting for transfers between devices, from_expert(): lax.ppermute(at_place(parts, me ^ distance), 'expert', route)  33.6 us
    ppermute x24, starting transfers between devices, to_expert(): lax.ppermute(blocks[distance], 'expert', [(i, i ^ distance) for i in rang...  31 us
    ppermute x24, waiting for transfers between devices, to_expert(): lax.ppermute(blocks[distance], 'expert', [(i, i ^ distance) for i in rang...  30.6 us
    pallas_call x1, Pallas kernels, attend(): pl.pallas_call(attend_kernel, grid=(PAIRS,), in_specs=[pl.BlockSpec(memor...  27 us
  transfers between devices with their start and end apart: 47, of which 12 were waited for; matrix products, arithmetic and copies ran while one was open for 15% of the time, Pallas kernels for 51%

profile of v1, /device:TPU:8, one launch (start us, length us, event | category | flops | bytes accessed | tf_op | source)
XLA Modules:
  0.0 682.1 jit_solution(7013412932636125287)
XLA Ops:
  17.1 6.0 all-to-all-start
  28.7 6.3 all-to-all-done
  38.6 5.5 all-to-all-start.1
  45.4 53.2 %gather.1 = bf16[32,24,2304]{2,1,0:T(8,128)(2,1)} custom-call(bf16[24,2304]{1,0:T(8,128)(2,1)} %broadcast_add_fusion.refs_0_), custom_call_target="tpu_custom_call" | custom-call | bytes 3538944 | tf_op jit(solution)/shard_map/gather/pallas_call | solution.py:768
  104.5 5.4 convolution_convert_fusion.1
  109.9 45.9 %conditional.11 = (bf16[1024,768]{1,0:T(8,128)(2,1)}, f32[6,2,1024]{2,1,0:T(2,128)S(1)}, bf16[288,768]{1,0:T(8,128)(2,1)}, bf16[288,768]{1,0:T(8,128)(2,1)}, bf1...) conditional(s32[]{:T(128)} %bitcast.60, () %tuple.132, ...), branch_computations={%region_4.5_spmd, %region_5.6_spmd} | conditional | flops 14701266944 | bytes 29157716 | solution.py:801
  116.5 27.0 %attend.1 = (bf16[1024,768]{1,0:T(8,128)(2,1)}, f32[6,2,1024]{2,1,0:T(2,128)S(1)}) custom-call(s32[4]{0:T(128)S(1)} %get-tuple-element.349.length_ref, bf16[1024,2304]{1,0:T(8,128)(2,1)} %get-tuple-element.350.q_ref.k_ref.v_ref, bf16[1024,2304]{1,0:T(8,128)(2,1)} %get-tuple-element.350.q_ref.k_ref.v_ref, bf16[1024,2304]{1,0:T(8,128)(2,1)} %get-tuple-element.350.q_ref.k_ref.v_ref), custom_call_target="tpu_custom_call" | custom-call | flops 12884901888 | bytes 6291456 | tf_op jit(solution)/shard_map/cond/branch_1_fun/attend/pallas_call | solution.py:167
  148.8 6.4 collective-permute-done.33
  155.8 5.0 fusion.69
  167.3 4.2 fusion.49
  173.3 9.0 %dispatch.1 = (bf16[304,768]{1,0:T(8,128)(2,1)}, bf16[304,768]{1,0:T(8,128)(2,1)}, bf16[304,768]{1,0:T(8,128)(2,1)}, bf16[304,768]{1,0:T(8,128)(2,1)}, bf16[304,...) custom-call(s32[2432,1]{1,0:T(8,128)} %select_n.208.refs_0_, ...), custom_call_target="tpu_custom_call" | custom-call | flops 3825205248 | bytes 5308416 | tf_op jit(solution)/shard_map/dispatch/pallas_call | solution.py:680
  182.3 5.4 pad_maximum_fusion.8
  187.7 44.4 %conditional.12 = (f32[1024,768]{1,0:T(8,128)}, f32[1024,768]{1,0:T(8,128)}, bf16[1024,3072]{1,0:T(8,128)(2,1)}, bf16[1024,3072]{1,0:T(8,128)(2,1)}, bf16[768,10...) conditional(s32[]{:T(128)} %bitcast.60, () %tuple.131, ...), branch_computations={%region_11.12_spmd, %region_12.13_spmd} | conditional | flops 24159191040 | bytes 52789596 | solution.py:801
  191.4 28.1 %shared_expert.1 = (f32[1024,768]{1,0:T(8,128)}, f32[1024,768]{1,0:T(8,128)}, bf16[1024,3072]{1,0:T(8,128)(2,1)}, bf16[1024,3072]{1,0:T(8,128)(2,1)}, bf16[768,1024]{1,0:T(8,128)(2,1)}) custom-call(bf16[1024,768]{1,0:T(8,128)(2,1)S(1)} %get-tuple-element.362.rows_ref, bf16[1024,768]{1,0:T(8,128)(2,1)S(1)} %get-tuple-element.363.grad_ref.refs_2_, ...), custom_call_target="tpu_custom_call" | custom-call | flops 19327352832 | bytes 22020096 | tf_op jit(solution)/shard_map/cond/branch_1_fun/shared_expert/pallas_call | solution.py:344
  219.6 12.5 %expert_outer.6 = bf16[4,768,768]{2,1,0:T(8,128)(2,1)} custom-call(s32[1]{0:T(128)} %bitcast.1.refs_0_, bf16[1024,3072]{1,0:T(8,128)(2,1)} %get-tuple-element.1161.refs_1_, bf16[1024,768]{1,0:T(8,128)(2,1)S(1)} %get-tuple-element.363.grad_ref.refs_2_, bf16[4,2,96,1024]{3,2,1,0:T(8,128)(2,1)} %bitcast.2.refs_3_, bf16[1024,3072]{1,0:T(8,128)(2,1)} %get-tuple-element.1162.refs_4_), custom_call_target="tpu_custom_call" | custom-call | flops 4831838208 | bytes 25165824 | tf_op jit(solution)/shard_map/cond/branch_1_fun/expert_outer/pallas_call | solution.py:463
  232.1 51.7 %conditional.13 = (bf16[288,768]{1,0:T(8,128)(2,1)}, bf16[288,768]{1,0:T(8,128)(2,1)}, bf16[288,768]{1,0:T(8,128)(2,1)}, bf16[288,768]{1,0:T(8,128)(2,1)}, bf16[...) conditional(s32[]{:T(128)} %bitcast.60, () %tuple.130, ...), branch_computations={%region_13.14_spmd, %region_14.15_spmd} | conditional | flops 27179089920 | bytes 56328596 | solution.py:801
  235.9 34.1 %routed_expert.2 = (bf16[288,768]{1,0:T(8,128)(2,1)}, bf16[288,768]{1,0:T(8,128)(2,1)}, bf16[288,768]{1,0:T(8,128)(2,1)}, bf16[288,768]{1,0:T(8,128)(2,1)}, bf16...) custom-call(bf16[304,768]{1,0:T(8,128)(2,1)} %get-tuple-element.375., ...), custom_call_target="tpu_custom_call" | custom-call | flops 21743271936 | bytes 23592960 | tf_op jit(solution)/shard_map/cond/branch_1_fun/routed_expert/pallas_call | solution.py:344
  270.0 13.9 %expert_outer.7 = bf16[4,768,768]{2,1,0:T(8,128)(2,1)} custom-call(s32[1]{0:T(128)} %bitcast.3.refs_0_, bf16[1152,3072]{1,0:T(8,128)(2,1)} %get-tuple-element.1194.refs_1_, bf16[1152,768]{1,0:T(8,128)(2,1)} %get-tuple-element.1196.refs_2_, bf16[4,2,96,1152]{3,2,1,0:T(8,128)(2,1)} %bitcast.4.refs_3_, bf16[1152,3072]{1,0:T(8,128)(2,1)} %get-tuple-element.1195.refs_4_), custom_call_target="tpu_custom_call" | custom-call | flops 5435817984 | bytes 27131904 | tf_op jit(solution)/shard_map/cond/branch_1_fun/expert_outer/pallas_call | solution.py:463
  283.9 39.6 %conditional.14 = (bf16[4,768,768]{2,1,0:T(8,128)(2,1)}, bf16[4,768,768]{2,1,0:T(8,128)(2,1)}, bf16[288,768]{1,0:T(8,128)(2,1)}, bf16[288,768]{1,0:T(8,128)(2,1)...) conditional(s32[]{:T(128)} %bitcast.60, () %tuple.136, (bf16[768,1152]{1,0:T(8,128)(2,1)}, ...), branch_computations={%region_15.16_spmd, %region_16.17_spmd} | conditional | flops 10267656192 | bytes 95355272 | solution.py:801
  292.2 15.3 %expert_outer.8.refs_6_ = bf16[4,768,768]{2,1,0:T(8,128)(2,1)} custom-call(s32[1]{0:T(128)} %bitcast.5.refs_0_, bf16[1152,3072]{1,0:T(8,128)(2,1)} %get-tuple-element.401.refs_1_, bf16[1152,768]{1,0:T(8,128)(2,1)} %get-tuple-element.402.refs_2_, bf16[4,2,96,1152]{3,2,1,0:T(8,128)(2,1)} %bitcast.6.refs_3_, bf16[1152,3072]{1,0:T(8,128)(2,1)} %get-tuple-element.404.refs_4_, ...), custom_call_target="tpu_custom_call" | custom-call | flops 5435817984 | bytes 27131904 | tf_op jit(solution)/shard_map/cond/branch_1_fun/expert_outer/pallas_call | solution.py:463
  307.5 13.9 %expert_outer.9 = bf16[4,768,768]{2,1,0:T(8,128)(2,1)} custom-call(s32[1]{0:T(128)} %bitcast.5.refs_0_, bf16[1024,3072]{1,0:T(8,128)(2,1)} %get-tuple-element.406.refs_1_, bf16[1024,768]{1,0:T(8,128)(2,1)S(1)} %get-tuple-element.407.refs_2_, bf16[4,2,96,1024]{3,2,1,0:T(8,128)(2,1)} %bitcast.7.refs_3_, bf16[1024,3072]{1,0:T(8,128)(2,1)} %get-tuple-element.409.refs_4_, ...), custom_call_target="tpu_custom_call" | custom-call | flops 4831838208 | bytes 25165824 | tf_op jit(solution)/shard_map/cond/branch_1_fun/expert_outer/pallas_call | solution.py:463
  323.5 64.3 %conditional.15 = (bf16[288,768]{1,0:T(8,128)(2,1)}, bf16[288,768]{1,0:T(8,128)(2,1)}, bf16[288,768]{1,0:T(8,128)(2,1)}, bf16[288,768]{1,0:T(8,128)(2,1)}, bf16[...) conditional(s32[]{:T(128)} %bitcast.60, () %tuple.129, ...), branch_computations={%region_17.18_spmd, %region_18.19_spmd} | conditional | flops 27193245696 | bytes 105382632 | solution.py:801
  323.9 4.5 dynamic-slice_bitcast_fusion
  339.9 34.1 %routed_expert.3 = (bf16[288,768]{1,0:T(8,128)(2,1)}, bf16[288,768]{1,0:T(8,128)(2,1)}, bf16[288,768]{1,0:T(8,128)(2,1)}, bf16[288,768]{1,0:T(8,128)(2,1)}, bf16...) custom-call(bf16[304,768]{1,0:T(8,128)(2,1)S(1)} %copy-done.44, ...), custom_call_target="tpu_custom_call" | custom-call | flops 21743271936 | bytes 23592960 | tf_op jit(solution)/shard_map/cond/branch_1_fun/routed_expert/pallas_call | solution.py:344
  373.9 13.9 %expert_outer.10 = bf16[4,768,768]{2,1,0:T(8,128)(2,1)} custom-call(s32[1]{0:T(128)} %bitcast.8.refs_0_, bf16[1152,3072]{1,0:T(8,128)(2,1)} %get-tuple-element.1243.refs_1_, bf16[1152,768]{1,0:T(8,128)(2,1)} %get-tuple-element.1245.refs_2_, bf16[4,2,96,1152]{3,2,1,0:T(8,128)(2,1)} %bitcast.9.refs_3_, bf16[1152,3072]{1,0:T(8,128)(2,1)} %get-tuple-element.1244.refs_4_), custom_call_target="tpu_custom_call" | custom-call | flops 5435817984 | bytes 27131904 | tf_op jit(solution)/shard_map/cond/branch_1_fun/expert_outer/pallas_call | solution.py:463
  389.2 49.7 %conditional.16 = (bf16[4,768,768]{2,1,0:T(8,128)(2,1)}, bf16[304,768]{1,0:T(8,128)(2,1)}, bf16[304,768]{1,0:T(8,128)(2,1)}, bf16[304,768]{1,0:T(8,128)(2,1)}, b...) conditional(s32[]{:T(128)} %bitcast.60, () %tuple.141, ...), branch_computations={%region_19.20_spmd, %region_20.21_spmd} | conditional | flops 5435817984 | bytes 64979472 | solution.py:801
  405.7 15.3 %expert_outer.11 = bf16[4,768,768]{2,1,0:T(8,128)(2,1)} custom-call(s32[1]{0:T(128)} %bitcast.16.refs_0_, bf16[1152,3072]{1,0:T(8,128)(2,1)} %get-tuple-element.443.refs_1_, bf16[1152,768]{1,0:T(8,128)(2,1)} %get-tuple-element.444.refs_2_, bf16[4,2,96,1152]{3,2,1,0:T(8,128)(2,1)} %bitcast.17.refs_3_, bf16[1152,3072]{1,0:T(8,128)(2,1)} %get-tuple-element.446.refs_4_, ...), custom_call_target="tpu_custom_call" | custom-call | flops 5435817984 | bytes 27131904 | tf_op jit(solution)/shard_map/cond/branch_1_fun/expert_outer/pallas_call | solution.py:463
  421.0 6.9 %collective-permute-done.18 = bf16[304,768]{1,0:T(8,128)(2,1)} collective-permute-done((bf16[304,768]{1,0:T(8,128)(2,1)}, bf16[304,768]{1,0:T(8,128)(2,1)}, u32[]{:S(2)}, u32[]{:S(2)}) %collective-permute-start.18) | collective-permute-done | bytes 466976 | tf_op jit(solution)/shard_map/cond/branch_1_fun/ppermute | solution.py:807
  427.9 11.0 %collective-permute-done.19 = bf16[304,768]{1,0:T(8,128)(2,1)} collective-permute-done((bf16[304,768]{1,0:T(8,128)(2,1)}, bf16[304,768]{1,0:T(8,128)(2,1)}, u32[]{:S(2)}, u32[]{:S(2)}) %collective-permute-start.19) | collective-permute-done | bytes 466976 | tf_op jit(solution)/shard_map/cond/branch_1_fun/ppermute | solution.py:807
  439.0 46.6 %conditional.17 = (f32[768,8]{0,1:T(8,128)S(1)}, f32[4,768]{1,0:T(4,128)S(1)}, f32[4,768]{1,0:T(4,128)S(1)}, f32[4,768]{1,0:T(4,128)S(1)}, f32[1024,768]{1,0:T(8...) conditional(s32[]{:T(128)} %bitcast.60, () %tuple.140, ...), branch_computations={%region_21.22_spmd, %region_22.30_spmd} | conditional | flops 6332856320 | bytes 93059104 | solution.py:801
  451.3 10.7 %combine.2 = (f32[1024,768]{1,0:T(8,128)}, f32[1024,2]{1,0:T(8,128)}) custom-call(s32[1,2432]{1,0:T(1,128)} %select_n.166.refs_0_, s32[1024,2]{1,0:T(8,128)} %copy.90.refs_1_, f32[1024,768]{1,0:T(8,128)} %get-tuple-element.460.refs_2_, bf16[304,768]{1,0:T(8,128)(2,1)} %get-tuple-element.461.refs_3_, bf16[304,768]{1,0:T(8,128)(2,1)} %get-tuple-element.462.refs_4_, ...), custom_call_target="tpu_custom_call" | custom-call | flops 3825205248 | bytes 10027008 | tf_op jit(solution)/shard_map/cond/branch_1_fun/combine/pallas_call | solution.py:595
  473.7 4.0 convolution_convert_fusion
  481.5 4.1 collective-permute-done.36
  485.6 67.5 %conditional.18 = (bf16[1024,2304]{1,0:T(8,128)(2,1)}, bf16[4,384,768]{2,1,0:T(8,128)(2,1)}, bf16[288,768]{1,0:T(8,128)(2,1)}, bf16[288,768]{1,0:T(8,128)(2,1)},...) conditional(s32[]{:T(128)} %bitcast.60, () %tuple.139, ...), branch_computations={%region_30.31_spmd, %region_31.32_spmd} | conditional | flops 34639970304 | bytes 76874376 | solution.py:801
  496.9 42.4 %attend_back.1.refs_3_ = bf16[1024,2304]{1,0:T(8,128)(2,1)} custom-call(s32[4]{0:T(128)S(1)} %copy-done.43, bf16[1024,2304]{1,0:T(8,128)(2,1)} %get-tuple-element.486.q_ref.k_ref.v_ref, bf16[1024,2304]{1,0:T(8,128)(2,1)} %get-tuple-element.486.q_ref.k_ref.v_ref, bf16[1024,2304]{1,0:T(8,128)(2,1)} %get-tuple-element.486.q_ref.k_ref.v_ref, ...), custom_call_target="tpu_custom_call" | custom-call | flops 32212254720 | bytes 12582912 | tf_op jit(solution)/shard_map/cond/branch_1_fun/attend_back/pallas_call | solution.py:193
  545.4 7.6 %attention_outer.2 = bf16[4,384,768]{2,1,0:T(8,128)(2,1)} custom-call(s32[1]{0:T(128)} %bitcast.29.refs_0_, bf16[4,2,96,1024]{3,2,1,0:T(8,128)(2,1)} %bitcast.30.refs_1_, bf16[4,2,96,1024]{3,2,1,0:T(8,128)(2,1)} %bitcast.31.refs_2_, bf16[1024,2304]{1,0:T(8,128)(2,1)} %attend_back.1.refs_3_, bf16[1024,768]{1,0:T(8,128)(2,1)} %get-tuple-element.492.refs_4_), custom_call_target="tpu_custom_call" | custom-call | flops 2415919104 | bytes 14155776 | tf_op jit(solution)/shard_map/cond/branch_1_fun/attention_outer/pallas_call | solution.py:463
  553.1 44.7 %conditional.19 = (bf16[1024,768]{1,0:T(8,128)(2,1)}, f32[4,768]{1,0:T(4,128)S(1)}, f32[4,768]{1,0:T(4,128)S(1)}, bf16[4,384,768]{2,1,0:T(8,128)(2,1)}, f32[192,...) conditional(s32[]{:T(128)} %bitcast.60, () %tuple.145, ...), branch_computations={%region_32.33_spmd, %region_33.40_spmd} | conditional | flops 6063634432 | bytes 77820512 | solution.py:801
  558.8 7.2 %fusion.11 = (f32[1024]{0:T(1024)S(1)}, f32[1024]{0:T(1024)S(1)}, f32[1024,768]{1,0:T(8,128)S(1)}) fusion(f32[4,768]{1,0:T(4,128)S(1)} %slice_add_fusion, f32[1024]{0:T(1024)S(1)} %add_rsqrt_fusion, f32[1024]{0:T(1024)S(1)} %broadcast_multiply_fusion.2, bf16[1024,768]{1,0:T(8,128)(2,1)S(1)} %get-tuple-element.504, ...), kind=kOutput, calls=%fused_computation.31 | convolution fusion | flops 3629381632 | bytes 13004800 | tf_op jit(solution)/shard_map/cond/branch_1_fun/dot_general | solution.py:34
  568.6 4.3 fusion.9
  576.4 7.7 %collective-permute-done.42 = bf16[192,768]{1,0:T(8,128)(2,1)} collective-permute-done((bf16[192,768]{1,0:T(8,128)(2,1)S(1)}, bf16[192,768]{1,0:T(8,128)(2,1)}, u32[]{:S(2)}, u32[]{:S(2)}) %collective-permute-start.42) | collective-permute-done | bytes 294944 | tf_op jit(solution)/shard_map/cond/branch_1_fun/ppermute | solution.py:793
  589.5 8.3 %attention_outer.3 = bf16[4,384,768]{2,1,0:T(8,128)(2,1)} custom-call(s32[1]{0:T(128)} %bitcast.40.refs_0_, bf16[4,2,96,1024]{3,2,1,0:T(8,128)(2,1)} %bitcast.41.refs_1_, bf16[4,2,96,1024]{3,2,1,0:T(8,128)(2,1)} %bitcast.42.refs_2_, bf16[1024,2304]{1,0:T(8,128)(2,1)} %get-tuple-element.505.refs_3_, bf16[1024,768]{1,0:T(8,128)(2,1)} %get-tuple-element.510.refs_4_, ...), custom_call_target="tpu_custom_call" | custom-call | flops 2415919104 | bytes 14155776 | tf_op jit(solution)/shard_map/cond/branch_1_fun/attention_outer/pallas_call | solution.py:463
  597.9 35.7 %conditional.20 = (f32[2,384,768]{2,1,0:T(8,128)}, f32[2,96,3072]{2,1,0:T(8,128)}, bf16[1024,768]{1,0:T(8,128)(2,1)}, f32[4,768]{1,0:T(4,128)S(1)}, f32[384,768]...) conditional(s32[]{:T(128)} %bitcast.60, () %tuple.128, ...), branch_computations={%region_40.41_spmd, %region_41.43_spmd} | conditional | flops 3630368512 | bytes 77951240 | solution.py:801
  606.0 9.0 %combine.3 = (f32[1024,768]{1,0:T(8,128)}, f32[1024,2]{1,0:T(8,128)}) custom-call(s32[1,2304]{1,0:T(1,128)} %select_n.182.refs_0_, s32[1024,2]{1,0:T(8,128)} %copy.93.refs_1_, f32[1024,768]{1,0:T(8,128)} %get-tuple-element.527.refs_2_, bf16[288,768]{1,0:T(8,128)(2,1)} %get-tuple-element.528.refs_3_, bf16[288,768]{1,0:T(8,128)(2,1)} %get-tuple-element.529.refs_4_, ...), custom_call_target="tpu_custom_call" | custom-call | flops 3623878656 | bytes 9830400 | tf_op jit(solution)/shard_map/cond/branch_1_fun/combine/pallas_call | solution.py:595
  618.5 8.2 %expert_sums.1 = (f32[2,384,768]{2,1,0:T(8,128)}, f32[2,96,3072]{2,1,0:T(8,128)}) custom-call(bf16[1536,768]{1,0:T(8,128)(2,1)} %get-tuple-element.513.refs_0_, bf16[1536,768]{1,0:T(8,128)(2,1)} %get-tuple-element.514.refs_1_, bf16[1536,768]{1,0:T(8,128)(2,1)} %get-tuple-element.515.refs_2_, bf16[1536,768]{1,0:T(8,128)(2,1)} %get-tuple-element.516.refs_3_.refs_7_, ...), custom_call_target="tpu_custom_call" | custom-call | bytes 18874368 | tf_op jit(solution)/shard_map/cond/branch_1_fun/expert_sums/pallas_call | solution.py:647
  641.6 29.5 %conditional.21 = (f32[96,768]{1,0:T(8,128)S(1)}, f32[96,768]{1,0:T(8,128)S(1)}, f32[96,768]{1,0:T(8,128)S(1)}, f32[96,768]{1,0:T(8,128)}, f32[96,576]{1,0:T(8,128)S(1)}, /*index=5*/f32[96,192]{1,0:T(8,128)S(1)}) conditional(s32[]{:T(128)} %bitcast.60, () %tuple.148, bf16[4,96,768]{1,2,0:T(8,128)(2,1)S(1)} %maximum_bitcast_fusion), branch_computations={%region_43.44_spmd, %region_44.45_spmd} | conditional | flops 516113 | bytes 6488440 | solution.py:801
  646.0 8.6 %collective-permute-done.24 = bf16[96,768]{1,0:T(8,128)(2,1)S(1)} collective-permute-done((bf16[96,768]{1,0:T(8,128)(2,1)S(1)}, bf16[96,768]{1,0:T(8,128)(2,1)S(1)}, u32[]{:S(2)}, u32[]{:S(2)}) %collective-permute-start.24) | collective-permute-done | bytes 147488 | tf_op jit(solution)/shard_map/cond/branch_1_fun/ppermute | solution.py:793
  654.6 8.9 %collective-permute-done.25 = bf16[96,768]{1,0:T(8,128)(2,1)S(1)} collective-permute-done((bf16[96,768]{1,0:T(8,128)(2,1)S(1)}, bf16[96,768]{1,0:T(8,128)(2,1)S(1)}, u32[]{:S(2)}, u32[]{:S(2)}) %collective-permute-start.25) | collective-permute-done | bytes 147488 | tf_op jit(solution)/shard_map/cond/branch_1_fun/ppermute | solution.py:793
  663.5 4.9 collective-permute-done.26
  (361 shorter events, 190.2 us)
Async XLA Ops:
  7.2 148.6 %all-gather.3.cloned.1.call-start = ((), (), s32[]{:S(2)}) async-start(), calls=%async_computation.3 | async-start | bytes 11354112 | tf_op jit(solution)/shard_map/all_gather | solution.py:880
  17.1 17.8 %all-to-all-start = ((bf16[32,2,1800]{2,1,0:T(2,128)(2,1)}), bf16[32,2,1800]{2,1,0:T(2,128)(2,1)S(1)}, u32[]{:S(2)}, u32[]{:S(2)}) async-start(bf16[32,2,1800]{2,1,0:T(2,128)(2,1)} %reshape.857), calls=%async_computation | async-start | bytes 491520 | tf_op jit(solution)/shard_map/all_to_all | solution.py:781
  23.3 86.6 %copy-start.37 = (s32[4]{0:T(128)}, s32[4]{0:T(128)S(1)}, u32[]{:S(2)}) copy-start(s32[4]{0:T(128)S(1)} %get-tuple-element.1057) | copy-start | bytes 52
  38.6 60.0 %all-to-all-start.1 = ((f32[32,4,144]{2,1,0:T(4,128)}), f32[32,4,144]{2,1,0:T(4,128)S(1)}, u32[]{:S(2)}, u32[]{:S(2)}) async-start(f32[32,4,144]{2,1,0:T(4,128)} %reshape.822), calls=%async_computation.1 | async-start | bytes 262144 | tf_op jit(solution)/shard_map/all_to_all | solution.py:781
  111.0 37.8 %collective-permute-start.31 = (bf16[288,768]{1,0:T(8,128)(2,1)}, bf16[288,768]{1,0:T(8,128)(2,1)}, u32[]{:S(2)}, u32[]{:S(2)}) collective-permute-start(bf16[288,768]{1,0:T(8,128)(2,1)} %slice.247), channel_id=1, source_target_pairs={{0,1},{1,0},{2,3},{3,2},{4,5},{5,4},{6,7},{7,6},{8,9},{9,8},{10,11... | collective-permute-start | bytes 1327112 | tf_op jit(solution)/shard_map/cond/branch_1_fun/ppermute | solution.py:807
  111.8 37.0 %collective-permute-start.32 = (bf16[288,768]{1,0:T(8,128)(2,1)}, bf16[288,768]{1,0:T(8,128)(2,1)}, u32[]{:S(2)}, u32[]{:S(2)}) collective-permute-start(bf16[288,768]{1,0:T(8,128)(2,1)} %slice.248), channel_id=1, source_target_pairs={{0,2},{1,3},{2,0},{3,1},{4,6},{5,7},{6,4},{7,5},{8,10},{9,11},{10,... | collective-permute-start | bytes 1327112 | tf_op jit(solution)/shard_map/cond/branch_1_fun/ppermute | solution.py:807
  114.7 40.6 %collective-permute-start.33 = (bf16[288,768]{1,0:T(8,128)(2,1)}, bf16[288,768]{1,0:T(8,128)(2,1)}, u32[]{:S(2)}, u32[]{:S(2)}) collective-permute-start(bf16[288,768]{1,0:T(8,128)(2,1)} %slice.249), channel_id=1, source_target_pairs={{0,3},{1,2},{2,1},{3,0},{4,7},{5,6},{6,5},{7,4},{8,11},{9,10},{10,... | collective-permute-start | bytes 1327112 | tf_op jit(solution)/shard_map/cond/branch_1_fun/ppermute | solution.py:807
  187.9 44.2 %collective-permute-start = (bf16[304,768]{1,0:T(8,128)(2,1)}, bf16[304,768]{1,0:T(8,128)(2,1)}, u32[]{:S(2)}, u32[]{:S(2)}) collective-permute-start(bf16[304,768]{1,0:T(8,128)(2,1)} %get-tuple-element.372), channel_id=1, source_target_pairs={{0,1},{1,0},{2,3},{3,2},{4,5},{5,4},{6,7},{7,6},{8,9},{9,8},{10,11... | collective-permute-start | bytes 1400840 | tf_op jit(solution)/shard_map/cond/branch_1_fun/ppermute | solution.py:807
  188.0 44.2 %collective-permute-start.1 = (bf16[304,768]{1,0:T(8,128)(2,1)}, bf16[304,768]{1,0:T(8,128)(2,1)}, u32[]{:S(2)}, u32[]{:S(2)}) collective-permute-start(bf16[304,768]{1,0:T(8,128)(2,1)} %get-tuple-element.373), channel_id=1, source_target_pairs={{0,2},{1,3},{2,0},{3,1},{4,6},{5,7},{6,4},{7,5},{8,10},{9,11},{10,... | collective-permute-start | bytes 1400840 | tf_op jit(solution)/shard_map/cond/branch_1_fun/ppermute | solution.py:807
  190.0 42.1 %collective-permute-start.2 = (bf16[304,768]{1,0:T(8,128)(2,1)}, bf16[304,768]{1,0:T(8,128)(2,1)}, u32[]{:S(2)}, u32[]{:S(2)}) collective-permute-start(bf16[304,768]{1,0:T(8,128)(2,1)} %get-tuple-element.374), channel_id=1, source_target_pairs={{0,3},{1,2},{2,1},{3,0},{4,7},{5,6},{6,5},{7,4},{8,11},{9,10},{10,... | collective-permute-start | bytes 1400840 | tf_op jit(solution)/shard_map/cond/branch_1_fun/ppermute | solution.py:807
  232.4 51.5 %collective-permute-start.3 = (bf16[304,768]{1,0:T(8,128)(2,1)}, bf16[304,768]{1,0:T(8,128)(2,1)}, u32[]{:S(2)}, u32[]{:S(2)}) collective-permute-start(bf16[304,768]{1,0:T(8,128)(2,1)} %get-tuple-element.398), channel_id=1, source_target_pairs={{0,1},{1,0},{2,3},{3,2},{4,5},{5,4},{6,7},{7,6},{8,9},{9,8},{10,11... | collective-permute-start | bytes 1400840 | tf_op jit(solution)/shard_map/cond/branch_1_fun/ppermute | solution.py:807
  233.4 50.5 %collective-permute-start.4 = (bf16[304,768]{1,0:T(8,128)(2,1)}, bf16[304,768]{1,0:T(8,128)(2,1)}, u32[]{:S(2)}, u32[]{:S(2)}) collective-permute-start(bf16[304,768]{1,0:T(8,128)(2,1)} %get-tuple-element.399), channel_id=1, source_target_pairs={{0,2},{1,3},{2,0},{3,1},{4,6},{5,7},{6,4},{7,5},{8,10},{9,11},{10,... | collective-permute-start | bytes 1400840 | tf_op jit(solution)/shard_map/cond/branch_1_fun/ppermute | solution.py:807
  234.5 49.4 %collective-permute-start.5 = (bf16[304,768]{1,0:T(8,128)(2,1)}, bf16[304,768]{1,0:T(8,128)(2,1)}, u32[]{:S(2)}, u32[]{:S(2)}) collective-permute-start(bf16[304,768]{1,0:T(8,128)(2,1)} %get-tuple-element.400), channel_id=1, source_target_pairs={{0,3},{1,2},{2,1},{3,0},{4,7},{5,6},{6,5},{7,4},{8,11},{9,10},{10,... | collective-permute-start | bytes 1400840 | tf_op jit(solution)/shard_map/cond/branch_1_fun/ppermute | solution.py:807
  283.9 8.3 %collective-permute-start.6 = (bf16[4,768,768]{2,1,0:T(8,128)(2,1)}, bf16[4,768,768]{2,1,0:T(8,128)(2,1)}, u32[]{:S(2)}, u32[]{:S(2)}) collective-permute-start(bf16[4,768,768]{2,1,0:T(8,128)(2,1)} %get-tuple-element.405), channel_id=1, source_target_pairs={{0,4},{4,0},{8,12},{12,8},{16,20},{20,16},{24,28},{28,24},{1,5},{5... | collective-permute-start | bytes 14155784 | tf_op jit(solution)/shard_map/cond/branch_1_fun/ppermute | solution.py:561
  284.0 23.5 %collective-permute-start.7 = (bf16[4,768,768]{2,1,0:T(8,128)(2,1)}, bf16[4,768,768]{2,1,0:T(8,128)(2,1)}, u32[]{:S(2)}, u32[]{:S(2)}) collective-permute-start(bf16[4,768,768]{2,1,0:T(8,128)(2,1)} %get-tuple-element.410), channel_id=1, source_target_pairs={{0,4},{4,0},{8,12},{12,8},{16,20},{20,16},{24,28},{28,24},{1,5},{5... | collective-permute-start | bytes 14155784 | tf_op jit(solution)/shard_map/cond/branch_1_fun/ppermute | solution.py:561
  284.5 36.9 %collective-permute-start.10 = (bf16[288,768]{1,0:T(8,128)(2,1)}, bf16[288,768]{1,0:T(8,128)(2,1)}, u32[]{:S(2)}, u32[]{:S(2)}) collective-permute-start(bf16[288,768]{1,0:T(8,128)(2,1)} %get-tuple-element.414), channel_id=1, source_target_pairs={{0,3},{1,2},{2,1},{3,0},{4,7},{5,6},{6,5},{7,4},{8,11},{9,10},{10,... | collective-permute-start | bytes 1327112 | tf_op jit(solution)/shard_map/cond/branch_1_fun/ppermute | solution.py:807
  285.0 36.3 %collective-permute-start.8 = (bf16[288,768]{1,0:T(8,128)(2,1)}, bf16[288,768]{1,0:T(8,128)(2,1)}, u32[]{:S(2)}, u32[]{:S(2)}) collective-permute-start(bf16[288,768]{1,0:T(8,128)(2,1)} %get-tuple-element.412), channel_id=1, source_target_pairs={{0,1},{1,0},{2,3},{3,2},{4,5},{5,4},{6,7},{7,6},{8,9},{9,8},{10,11... | collective-permute-start | bytes 1327112 | tf_op jit(solution)/shard_map/cond/branch_1_fun/ppermute | solution.py:807
  287.8 35.6 %collective-permute-start.9 = (bf16[288,768]{1,0:T(8,128)(2,1)}, bf16[288,768]{1,0:T(8,128)(2,1)}, u32[]{:S(2)}, u32[]{:S(2)}) collective-permute-start(bf16[288,768]{1,0:T(8,128)(2,1)} %get-tuple-element.413), channel_id=1, source_target_pairs={{0,2},{1,3},{2,0},{3,1},{4,6},{5,7},{6,4},{7,5},{8,10},{9,11},{10,... | collective-permute-start | bytes 1327112 | tf_op jit(solution)/shard_map/cond/branch_1_fun/ppermute | solution.py:807
  330.0 57.8 %collective-permute-start.14 = (bf16[1536,768]{1,0:T(8,128)(2,1)}, bf16[1536,768]{1,0:T(8,128)(2,1)}, u32[]{:S(2)}, u32[]{:S(2)}) collective-permute-start(bf16[1536,768]{1,0:T(8,128)(2,1)} %pad_maximum_fusion.1), channel_id=1, source_target_pairs={{0,8},{4,12},{8,0},{12,4},{16,24},{20,28},{24,16},{28,20},{1,9},{5... | collective-permute-start | bytes 7077896 | tf_op jit(solution)/shard_map/cond/branch_1_fun/ppermute | solution.py:820
  332.6 55.2 %collective-permute-start.15 = (bf16[1536,768]{1,0:T(8,128)(2,1)}, bf16[1536,768]{1,0:T(8,128)(2,1)}, u32[]{:S(2)}, u32[]{:S(2)}) collective-permute-start(bf16[1536,768]{1,0:T(8,128)(2,1)} %pad_maximum_fusion.2), channel_id=1, source_target_pairs={{0,16},{4,20},{8,24},{12,28},{16,0},{20,4},{24,8},{28,12},{1,17},{... | collective-permute-start | bytes 7077896 | tf_op jit(solution)/shard_map/cond/branch_1_fun/ppermute | solution.py:820
  333.6 54.2 %collective-permute-start.11 = (bf16[304,768]{1,0:T(8,128)(2,1)}, bf16[304,768]{1,0:T(8,128)(2,1)}, u32[]{:S(2)}, u32[]{:S(2)}) collective-permute-start(bf16[304,768]{1,0:T(8,128)(2,1)} %get-tuple-element.438), channel_id=1, source_target_pairs={{0,1},{1,0},{2,3},{3,2},{4,5},{5,4},{6,7},{7,6},{8,9},{9,8},{10,11... | collective-permute-start | bytes 1400840 | tf_op jit(solution)/shard_map/cond/branch_1_fun/ppermute | solution.py:807
  336.9 50.9 %collective-permute-start.12 = (bf16[304,768]{1,0:T(8,128)(2,1)}, bf16[304,768]{1,0:T(8,128)(2,1)}, u32[]{:S(2)}, u32[]{:S(2)}) collective-permute-start(bf16[304,768]{1,0:T(8,128)(2,1)} %get-tuple-element.439), channel_id=1, source_target_pairs={{0,2},{1,3},{2,0},{3,1},{4,6},{5,7},{6,4},{7,5},{8,10},{9,11},{10,... | collective-permute-start | bytes 1400840 | tf_op jit(solution)/shard_map/cond/branch_1_fun/ppermute | solution.py:807
  337.0 50.8 %collective-permute-start.13 = (bf16[304,768]{1,0:T(8,128)(2,1)}, bf16[304,768]{1,0:T(8,128)(2,1)}, u32[]{:S(2)}, u32[]{:S(2)}) collective-permute-start(bf16[304,768]{1,0:T(8,128)(2,1)} %get-tuple-element.440), channel_id=1, source_target_pairs={{0,3},{1,2},{2,1},{3,0},{4,7},{5,6},{6,5},{7,4},{8,11},{9,10},{10,... | collective-permute-start | bytes 1400840 | tf_op jit(solution)/shard_map/cond/branch_1_fun/ppermute | solution.py:807
  389.4 16.3 %collective-permute-start.16 = (bf16[4,768,768]{2,1,0:T(8,128)(2,1)}, bf16[4,768,768]{2,1,0:T(8,128)(2,1)}, u32[]{:S(2)}, u32[]{:S(2)}) collective-permute-start(bf16[4,768,768]{2,1,0:T(8,128)(2,1)} %get-tuple-element.447), channel_id=1, source_target_pairs={{0,4},{4,0},{8,12},{12,8},{16,20},{20,16},{24,28},{28,24},{1,5},{5... | collective-permute-start | bytes 14155784 | tf_op jit(solution)/shard_map/cond/branch_1_fun/ppermute | solution.py:561
  392.0 46.9 %collective-permute-start.20 = (bf16[768,768]{1,0:T(8,128)(2,1)}, bf16[768,768]{1,0:T(8,128)(2,1)}, u32[]{:S(2)}, u32[]{:S(2)}) collective-permute-start(bf16[768,768]{1,0:T(8,128)(2,1)} %dynamic-slice_bitcast_fusion.6), channel_id=1, source_target_pairs={{0,24},{4,28},{8,16},{12,20},{16,8},{20,12},{24,0},{28,4},{1,25},{... | collective-permute-start | bytes 3538952 | tf_op jit(solution)/shard_map/cond/branch_1_fun/ppermute | solution.py:820
  393.5 27.5 %collective-permute-start.17 = (bf16[304,768]{1,0:T(8,128)(2,1)}, bf16[304,768]{1,0:T(8,128)(2,1)}, u32[]{:S(2)}, u32[]{:S(2)}) collective-permute-start(bf16[304,768]{1,0:T(8,128)(2,1)} %get-tuple-element.449), channel_id=1, source_target_pairs={{0,1},{1,0},{2,3},{3,2},{4,5},{5,4},{6,7},{7,6},{8,9},{9,8},{10,11... | collective-permute-start | bytes 1400840 | tf_op jit(solution)/shard_map/cond/branch_1_fun/ppermute | solution.py:807
  396.4 31.5 %collective-permute-start.18 = (bf16[304,768]{1,0:T(8,128)(2,1)}, bf16[304,768]{1,0:T(8,128)(2,1)}, u32[]{:S(2)}, u32[]{:S(2)}) collective-permute-start(bf16[304,768]{1,0:T(8,128)(2,1)} %get-tuple-element.450), channel_id=1, source_target_pairs={{0,2},{1,3},{2,0},{3,1},{4,6},{5,7},{6,4},{7,5},{8,10},{9,11},{10,... | collective-permute-start | bytes 1400840 | tf_op jit(solution)/shard_map/cond/branch_1_fun/ppermute | solution.py:807
  396.4 42.4 %collective-permute-start.19 = (bf16[304,768]{1,0:T(8,128)(2,1)}, bf16[304,768]{1,0:T(8,128)(2,1)}, u32[]{:S(2)}, u32[]{:S(2)}) collective-permute-start(bf16[304,768]{1,0:T(8,128)(2,1)} %get-tuple-element.451), channel_id=1, source_target_pairs={{0,3},{1,2},{2,1},{3,0},{4,7},{5,6},{6,5},{7,4},{8,11},{9,10},{10,... | collective-permute-start | bytes 1400840 | tf_op jit(solution)/shard_map/cond/branch_1_fun/ppermute | solution.py:807
  442.9 42.7 %collective-permute-start.37 = (bf16[768,768]{1,0:T(8,128)(2,1)}, bf16[768,768]{1,0:T(8,128)(2,1)}, u32[]{:S(2)}, u32[]{:S(2)}) collective-permute-start(bf16[768,768]{1,0:T(8,128)(2,1)} %get-tuple-element.1094), channel_id=1, source_target_pairs={{0,8},{4,12},{8,0},{12,4},{16,24},{20,28},{24,16},{28,20},{1,9},{5... | collective-permute-start | bytes 3538952 | tf_op jit(solution)/shard_map/cond/branch_1_fun/ppermute | solution.py:820
  444.0 41.5 %collective-permute-start.38 = (bf16[768,768]{1,0:T(8,128)(2,1)}, bf16[768,768]{1,0:T(8,128)(2,1)}, u32[]{:S(2)}, u32[]{:S(2)}) collective-permute-start(bf16[768,768]{1,0:T(8,128)(2,1)} %get-tuple-element.1093), channel_id=1, source_target_pairs={{0,16},{4,20},{8,24},{12,28},{16,0},{20,4},{24,8},{28,12},{1,17},{... | collective-permute-start | bytes 3538952 | tf_op jit(solution)/shard_map/cond/branch_1_fun/ppermute | solution.py:820
  444.9 36.6 %collective-permute-start.34 = (bf16[288,768]{1,0:T(8,128)(2,1)}, bf16[288,768]{1,0:T(8,128)(2,1)}, u32[]{:S(2)}, u32[]{:S(2)}) collective-permute-start(bf16[288,768]{1,0:T(8,128)(2,1)} %get-tuple-element.481), channel_id=1, source_target_pairs={{0,1},{1,0},{2,3},{3,2},{4,5},{5,4},{6,7},{7,6},{8,9},{9,8},{10,11... | collective-permute-start | bytes 1327112 | tf_op jit(solution)/shard_map/cond/branch_1_fun/ppermute | solution.py:807
  444.9 36.6 %collective-permute-start.35 = (bf16[288,768]{1,0:T(8,128)(2,1)}, bf16[288,768]{1,0:T(8,128)(2,1)}, u32[]{:S(2)}, u32[]{:S(2)}) collective-permute-start(bf16[288,768]{1,0:T(8,128)(2,1)} %get-tuple-element.482), channel_id=1, source_target_pairs={{0,2},{1,3},{2,0},{3,1},{4,6},{5,7},{6,4},{7,5},{8,10},{9,11},{10,... | collective-permute-start | bytes 1327112 | tf_op jit(solution)/shard_map/cond/branch_1_fun/ppermute | solution.py:807
  447.0 38.6 %collective-permute-start.36 = (bf16[288,768]{1,0:T(8,128)(2,1)}, bf16[288,768]{1,0:T(8,128)(2,1)}, u32[]{:S(2)}, u32[]{:S(2)}) collective-permute-start(bf16[288,768]{1,0:T(8,128)(2,1)} %get-tuple-element.483), channel_id=1, source_target_pairs={{0,3},{1,2},{2,1},{3,0},{4,7},{5,6},{6,5},{7,4},{8,11},{9,10},{10,... | collective-permute-start | bytes 1327112 | tf_op jit(solution)/shard_map/cond/branch_1_fun/ppermute | solution.py:807
  489.3 63.8 %collective-permute-start.30 = (bf16[1536,768]{1,0:T(8,128)(2,1)}, bf16[1536,768]{1,0:T(8,128)(2,1)}, u32[]{:S(2)}, u32[]{:S(2)}) collective-permute-start(bf16[1536,768]{1,0:T(8,128)(2,1)} %pad_maximum_fusion.3), channel_id=1, source_target_pairs={{0,24},{4,28},{8,16},{12,20},{16,8},{20,12},{24,0},{28,4},{1,25},{... | collective-permute-start | bytes 7077896 | tf_op jit(solution)/shard_map/cond/branch_1_fun/ppermute | solution.py:820
  490.8 62.3 %collective-permute-start.27 = (bf16[288,768]{1,0:T(8,128)(2,1)}, bf16[288,768]{1,0:T(8,128)(2,1)}, u32[]{:S(2)}, u32[]{:S(2)}) collective-permute-start(bf16[288,768]{1,0:T(8,128)(2,1)} %get-tuple-element.494), channel_id=1, source_target_pairs={{0,1},{1,0},{2,3},{3,2},{4,5},{5,4},{6,7},{7,6},{8,9},{9,8},{10,11... | collective-permute-start | bytes 1327112 | tf_op jit(solution)/shard_map/cond/branch_1_fun/ppermute | solution.py:807
  490.8 62.3 %collective-permute-start.28 = (bf16[288,768]{1,0:T(8,128)(2,1)}, bf16[288,768]{1,0:T(8,128)(2,1)}, u32[]{:S(2)}, u32[]{:S(2)}) collective-permute-start(bf16[288,768]{1,0:T(8,128)(2,1)} %get-tuple-element.495), channel_id=1, source_target_pairs={{0,2},{1,3},{2,0},{3,1},{4,6},{5,7},{6,4},{7,5},{8,10},{9,11},{10,... | collective-permute-start | bytes 1327112 | tf_op jit(solution)/shard_map/cond/branch_1_fun/ppermute | solution.py:807
  492.9 60.2 %collective-permute-start.29 = (bf16[288,768]{1,0:T(8,128)(2,1)}, bf16[288,768]{1,0:T(8,128)(2,1)}, u32[]{:S(2)}, u32[]{:S(2)}) collective-permute-start(bf16[288,768]{1,0:T(8,128)(2,1)} %get-tuple-element.496), channel_id=1, source_target_pairs={{0,3},{1,2},{2,1},{3,0},{4,7},{5,6},{6,5},{7,4},{8,11},{9,10},{10,... | collective-permute-start | bytes 1327112 | tf_op jit(solution)/shard_map/cond/branch_1_fun/ppermute | solution.py:807
  553.5 35.9 %collective-permute-start.39 = (bf16[4,384,768]{2,1,0:T(8,128)(2,1)}, bf16[4,384,768]{2,1,0:T(8,128)(2,1)}, u32[]{:S(2)}, u32[]{:S(2)}) collective-permute-start(bf16[4,384,768]{2,1,0:T(8,128)(2,1)} %get-tuple-element.511), channel_id=1, source_target_pairs={{0,4},{4,0},{8,12},{12,8},{16,20},{20,16},{24,28},{28,24},{1,5},{5... | collective-permute-start | bytes 7077896 | tf_op jit(solution)/shard_map/cond/branch_1_fun/ppermute | solution.py:561
  554.4 18.5 %collective-permute-start.40 = (bf16[192,768]{1,0:T(8,128)(2,1)}, bf16[192,768]{1,0:T(8,128)(2,1)}, u32[]{:S(2)}, u32[]{:S(2)}) collective-permute-start(bf16[192,768]{1,0:T(8,128)(2,1)} %get-tuple-element.1077), channel_id=1, source_target_pairs={{0,1},{1,0},{2,3},{3,2},{4,5},{5,4},{6,7},{7,6},{8,9},{9,8},{10,11... | collective-permute-start | bytes 884744 | tf_op jit(solution)/shard_map/cond/branch_1_fun/ppermute | solution.py:793
  555.3 21.0 %collective-permute-start.41 = (bf16[192,768]{1,0:T(8,128)(2,1)S(1)}, bf16[192,768]{1,0:T(8,128)(2,1)}, u32[]{:S(2)}, u32[]{:S(2)}) collective-permute-start(bf16[192,768]{1,0:T(8,128)(2,1)S(1)} %get-tuple-element.1079), channel_id=1, source_target_pairs={{0,2},{1,3},{2,0},{3,1},{4,6},{5,7},{6,4},{7,5},{8,10},{9,11},{10,... | collective-permute-start | bytes 884744 | tf_op jit(solution)/shard_map/cond/branch_1_fun/ppermute | solution.py:793
  556.5 27.6 %collective-permute-start.42 = (bf16[192,768]{1,0:T(8,128)(2,1)S(1)}, bf16[192,768]{1,0:T(8,128)(2,1)}, u32[]{:S(2)}, u32[]{:S(2)}) collective-permute-start(bf16[192,768]{1,0:T(8,128)(2,1)S(1)} %get-tuple-element.1078), channel_id=1, source_target_pairs={{0,3},{1,2},{2,1},{3,0},{4,7},{5,6},{6,5},{7,4},{8,11},{9,10},{10,... | collective-permute-start | bytes 884744 | tf_op jit(solution)/shard_map/cond/branch_1_fun/ppermute | solution.py:793
  600.6 29.4 %collective-permute-start.21 = (bf16[384,768]{1,0:T(8,128)(2,1)}, bf16[384,768]{1,0:T(8,128)(2,1)}, u32[]{:S(2)}, u32[]{:S(2)}) collective-permute-start(bf16[384,768]{1,0:T(8,128)(2,1)} %get-tuple-element.1087), channel_id=1, source_target_pairs={{0,8},{4,12},{8,0},{12,4},{16,24},{20,28},{24,16},{28,20},{1,9},{5... | collective-permute-start | bytes 1769480 | tf_op jit(solution)/shard_map/cond/branch_1_fun/ppermute | solution.py:820
  601.8 28.2 %collective-permute-start.22 = (bf16[384,768]{1,0:T(8,128)(2,1)}, bf16[384,768]{1,0:T(8,128)(2,1)}, u32[]{:S(2)}, u32[]{:S(2)}) collective-permute-start(bf16[384,768]{1,0:T(8,128)(2,1)} %get-tuple-element.1086), channel_id=1, source_target_pairs={{0,16},{4,20},{8,24},{12,28},{16,0},{20,4},{24,8},{28,12},{1,17},{... | collective-permute-start | bytes 1769480 | tf_op jit(solution)/shard_map/cond/branch_1_fun/ppermute | solution.py:820
  602.6 26.3 %collective-permute-start.23 = (bf16[384,768]{1,0:T(8,128)(2,1)}, bf16[384,768]{1,0:T(8,128)(2,1)S(1)}, u32[]{:S(2)}, u32[]{:S(2)}) collective-permute-start(bf16[384,768]{1,0:T(8,128)(2,1)} %get-tuple-element.1085), channel_id=1, source_target_pairs={{0,24},{4,28},{8,16},{12,20},{16,8},{20,12},{24,0},{28,4},{1,25},{... | collective-permute-start | bytes 1769480 | tf_op jit(solution)/shard_map/cond/branch_1_fun/ppermute | solution.py:820
  636.1 35.1 %all-to-all-start.2 = ((f32[32,39,128]{2,1,0:T(8,128)}), f32[32,39,128]{2,1,0:T(8,128)S(1)}, u32[]{:S(2)}, u32[]{:S(2)}) async-start(f32[32,39,128]{2,1,0:T(8,128)} %reshape.835), calls=%async_computation.2 | async-start | bytes 1310720 | tf_op jit(solution)/shard_map/all_to_all | solution.py:781
  641.9 12.7 %collective-permute-start.24 = (bf16[96,768]{1,0:T(8,128)(2,1)S(1)}, bf16[96,768]{1,0:T(8,128)(2,1)S(1)}, u32[]{:S(2)}, u32[]{:S(2)}) collective-permute-start(bf16[96,768]{1,0:T(8,128)(2,1)S(1)} %bitcast.232), channel_id=1, source_target_pairs={{0,1},{1,0},{2,3},{3,2},{4,5},{5,4},{6,7},{7,6},{8,9},{9,8},{10,11... | collective-permute-start | bytes 442376 | tf_op jit(solution)/shard_map/cond/branch_1_fun/ppermute | solution.py:793
  642.3 21.2 %collective-permute-start.25 = (bf16[96,768]{1,0:T(8,128)(2,1)S(1)}, bf16[96,768]{1,0:T(8,128)(2,1)S(1)}, u32[]{:S(2)}, u32[]{:S(2)}) collective-permute-start(bf16[96,768]{1,0:T(8,128)(2,1)S(1)} %bitcast.233), channel_id=1, source_target_pairs={{0,2},{1,3},{2,0},{3,1},{4,6},{5,7},{6,4},{7,5},{8,10},{9,11},{10,... | collective-permute-start | bytes 442376 | tf_op jit(solution)/shard_map/cond/branch_1_fun/ppermute | solution.py:793
  645.2 23.2 %collective-permute-start.26 = (bf16[96,768]{1,0:T(8,128)(2,1)S(1)}, bf16[96,768]{1,0:T(8,128)(2,1)S(1)}, u32[]{:S(2)}, u32[]{:S(2)}) collective-permute-start(bf16[96,768]{1,0:T(8,128)(2,1)S(1)} %bitcast.234), channel_id=1, source_target_pairs={{0,3},{1,2},{2,1},{3,0},{4,7},{5,6},{6,5},{7,4},{8,11},{9,10},{10,... | collective-permute-start | bytes 442376 | tf_op jit(solution)/shard_map/cond/branch_1_fun/ppermute | solution.py:793
  (44 other events, 725.3 us)
Sparse Core Ops, SparseCore 0:
  13.8 115.0 all-gather.2

commit v2 on v1

--- a/solution.py
+++ b/solution.py
@@ -337,18 +337,21 @@
             back_refs[k][CAP:, :] = below(dots)
 
 
-def ffn_call(kernel, name, operands, specs, w_in, w_out, place, outs, hidden, scratch, width=512, w_out_spec=None):
-    ff, count = w_in.shape[2], outs[hidden].shape[0]
+def ffn_call(kernel, name, operands, specs, w_in, w_out, place, outs, hidden, scratch, width=512, w_specs=None):
+    count, ff = outs[hidden].shape
     column = pl.BlockSpec((count, width), lambda step: (0, step))
     out_specs = [column if at in (hidden, hidden + 1) else whole(out.shape) for at, out in enumerate(outs)]
     return pl.pallas_call(
         kernel,
         grid=(ff // width,),
         in_specs=specs
-        + [
-            pl.BlockSpec((1, D, width), lambda step: (place, 0, step)),
-            w_out_spec or pl.BlockSpec((1, width, D), lambda step: (place, step, 0)),
-        ],
+        + (
+            w_specs
+            or [
+                pl.BlockSpec((1, D, width), lambda step: (place, 0, step)),
+                pl.BlockSpec((1, width, D), lambda step: (place, step, 0)),
+            ]
+        ),
         out_specs=out_specs,
         out_shape=outs,
         scratch_shapes=scratch,
@@ -362,7 +365,7 @@
 
 def shared_expert(rows, grad, w_in, w_out):
     kept = jax.ShapeDtypeStruct((LONG, D), jnp.float32)
-    hidden = jax.ShapeDtypeStruct((LONG, w_in.shape[1]), jnp.bfloat16)
+    hidden = jax.ShapeDtypeStruct((LONG, w_in.shape[0] * D), jnp.bfloat16)
     turned = jax.ShapeDtypeStruct((D, LONG), jnp.bfloat16)
     full = whole((LONG, D))
     return ffn_call(
@@ -370,14 +373,17 @@
         "shared_expert",
         [rows, grad],
         [full, full],
-        w_in[None],
+        w_in,
         w_out[0],
         0,
         [kept, kept, hidden, hidden, turned],
         2,
         [],
         D,
-        w_out[1],
+        [
+            pl.BlockSpec((1, D, D), lambda step: (step, 0, 0)),
+            w_out[1] or pl.BlockSpec((1, D, D), lambda step: (0, step, 0)),
+        ],
     )
 
 
@@ -421,7 +427,7 @@
     def _():
         result = product_tn(gelu_ref[...], grad_ref[...])
         if added:
-            result = result + refs[0][step, :tall, :].astype(jnp.float32)
+            result = result + refs[0][0].astype(jnp.float32)
         out_ref[step, :tall, :] = result.astype(jnp.bfloat16)
 
     @pl.when(step >= chips)
@@ -430,7 +436,7 @@
         result = result.reshape(chips, depth, D)
         place = pl.ds(pl.multiple_of(tall + (step - chips) * depth, 32), depth)
         if added:
-            result = result + refs[0][:, place, :].astype(jnp.float32)
+            result = result + refs[1][...].astype(jnp.float32)
         out_ref[:, place, :] = result.astype(jnp.bfloat16)
 
 
@@ -456,16 +462,16 @@
         put(mixed_ref, grad_ref)
 
 
-def outer_call(kernel, name, steps, which, operands, specs, rows, came, tokens, flops):
+def outer_call(kernel, name, steps, which, operands, specs, rows, came, came_specs, tokens, flops):
     chips = lax.axis_size("dp") // 2
     full = whole((chips, rows, D))
-    extra = [] if came is None else [came]
+    extra = [] if came is None else [came] * len(came_specs or [full])
     return pl.pallas_call(
         lambda *refs: kernel(came is not None, *refs),
         grid_spec=pltpu.PrefetchScalarGridSpec(
             num_scalar_prefetch=1,
             grid=(steps,),
-            in_specs=specs + [full] * len(extra) + [HBM] * len(tokens),
+            in_specs=specs + (came_specs or [full])[: len(extra)] + [HBM] * len(tokens),
             out_specs=full,
         ),
         out_shape=jax.ShapeDtypeStruct((chips, rows, D), jnp.bfloat16),
@@ -521,6 +527,12 @@
         specs,
         tall + ff // D * depth,
         came,
+        [
+            pl.BlockSpec((1, tall, D), lambda i, which: (jnp.minimum(i, chips - 1), 0, 0)),
+            pl.BlockSpec(
+                (chips, depth, D), lambda i, which: (0, tall // depth + jnp.maximum(i - chips, 0), 0)
+            ),
+        ],
         tokens,
         2 * count * D * ff,
     )
@@ -548,6 +560,7 @@
         specs,
         4 * depth,
         came,
+        None,
         tokens,
         4 * LONG * D * D,
     )
@@ -880,13 +893,8 @@
     packed = lax.all_gather(packed, BOTH, axis=0, tiled=False)
     start = ff // n
     w_out = packed[:, start : start + share].reshape(D, D)
-    w_shared_in = jnp.concatenate(
-        [
-            packed[:, start + (1 + at) * share : start + (2 + at) * share].reshape(D, D)
-            for at in range(ff // D)
-        ],
-        axis=1,
-    )
+    w_shared_in = packed[:, start + share : start + (1 + ff // D) * share].reshape(n, ff // D, share, D)
+    w_shared_in = jnp.swapaxes(w_shared_in, 0, 1).reshape(ff // D, D, D)
     w_router = packed[:, start + (1 + ff // D) * share, : share * EXPERTS].reshape(D, EXPERTS)
     if start % 16 == 0:
         w_shared_out = packed, pl.BlockSpec((D // start, start, D), lambda step: (step, 0, 0))
@@ -1156,8 +1164,8 @@
         axis=2,
     )
     length = message.shape[2]
-    message = jnp.pad(message, ((0, 0), (0, 0), (0, -length % 128))).reshape(n, -1, 128)
-    message = swap(message, BOTH).reshape(n, -1)
+    message = jnp.pad(message.astype(jnp.bfloat16), ((0, 0), (0, 0), (0, -length % 128))).reshape(n, -1, 128)
+    message = swap(message, BOTH).reshape(n, -1).astype(jnp.float32)
     at = BLOCKS * own_wide
     every_modulation = message[:, :at].reshape(n * BLOCKS, own_wide)
     grad_b_ada = jnp.sum(message[:, at : at + column], axis=0)

time: 693 us -> 682 us (0.984)
    ppermute x6, waiting for transfers between devices: 33.6 us -> 26.6 us  [from_expert(): lax.ppermute(at_place(parts, me ^ distance), 'expert', route)]
    unnamed x76 -> x81, local copies, waits for them, and re-layouts: 13.4 us -> 13.9 us
where the time goes in v2:
time: 682 us; the launch traced here: 671 us
  Pallas kernels  362 us (53%)
  local copies, waits for them, and re-layouts  71 us (10%)
  waiting for transfers between devices  68.7 us (10%)
  starting transfers between devices  64 us (9%)
  other arithmetic  51.4 us (8%)
  matrix products  34.2 us (5%)
  between operations  15.9 us (2%)
    pallas_call x8, Pallas kernels, outer_call(): pl.pallas_call(lambda *refs: kernel(came is not None, *refs), grid_spec=p...  99 us
    pallas_call x3, Pallas kernels, ffn_call(): pl.pallas_call(kernel, grid=(ff // width,), in_specs=specs + (w_specs or...  96.3 us
    pallas_call x1, Pallas kernels, gather(): pl.pallas_call(lambda *refs: gather_kernel(n_dp, n_ex, *refs), in_specs=[...  53.2 us
    pallas_call x1, Pallas kernels, attend_back(): pl.pallas_call(attend_back_kernel, grid=(PAIRS,), in_specs=[pl.BlockSpec(...  42.5 us
    ppermute x24, waiting for transfers between devices, to_expert(): lax.ppermute(blocks[distance], 'expert', [(i, i ^ distance) for i in rang...  32.3 us
    ppermute x24, starting transfers between devices, to_expert(): lax.ppermute(blocks[distance], 'expert', [(i, i ^ distance) for i in rang...  31 us
    pallas_call x1, Pallas kernels, attend(): pl.pallas_call(attend_kernel, grid=(PAIRS,), in_specs=[pl.BlockSpec(memor...  27 us
    ppermute x6, waiting for transfers between devices, from_expert(): lax.ppermute(at_place(parts, me ^ distance), 'expert', route)  26.6 us
  transfers between devices with their start and end apart: 47, of which 12 were waited for; matrix products, arithmetic and copies ran while one was open for 15% of the time, Pallas kernels for 51%

profile of v2, /device:TPU:8, one launch (start us, length us, event | category | flops | bytes accessed | tf_op | source)
XLA Modules:
  0.0 671.0 jit_solution(12911572918155564490)
XLA Ops:
  17.1 6.0 all-to-all-start
  28.7 6.3 all-to-all-done
  38.6 5.5 all-to-all-start.1
  45.4 53.2 %gather.1 = bf16[32,24,2304]{2,1,0:T(8,128)(2,1)} custom-call(bf16[24,2304]{1,0:T(8,128)(2,1)} %broadcast_add_fusion.refs_0_), custom_call_target="tpu_custom_call" | custom-call | bytes 3538944 | tf_op jit(solution)/shard_map/gather/pallas_call | solution.py:781
  104.5 5.4 convolution_convert_fusion.1
  109.9 45.9 %conditional.11 = (bf16[1024,768]{1,0:T(8,128)(2,1)}, f32[6,2,1024]{2,1,0:T(2,128)S(1)}, bf16[288,768]{1,0:T(8,128)(2,1)}, bf16[288,768]{1,0:T(8,128)(2,1)}, bf1...) conditional(s32[]{:T(128)} %bitcast.60, () %tuple.132, ...), branch_computations={%region_4.5_spmd, %region_5.6_spmd} | conditional | flops 14701266944 | bytes 29157716 | solution.py:814
  116.5 27.0 %attend.1 = (bf16[1024,768]{1,0:T(8,128)(2,1)}, f32[6,2,1024]{2,1,0:T(2,128)S(1)}) custom-call(s32[4]{0:T(128)S(1)} %get-tuple-element.350.length_ref, bf16[1024,2304]{1,0:T(8,128)(2,1)} %get-tuple-element.351.q_ref.k_ref.v_ref, bf16[1024,2304]{1,0:T(8,128)(2,1)} %get-tuple-element.351.q_ref.k_ref.v_ref, bf16[1024,2304]{1,0:T(8,128)(2,1)} %get-tuple-element.351.q_ref.k_ref.v_ref), custom_call_target="tpu_custom_call" | custom-call | flops 12884901888 | bytes 6291456 | tf_op jit(solution)/shard_map/cond/branch_1_fun/attend/pallas_call | solution.py:167
  148.8 6.5 collective-permute-done.33
  163.7 4.2 fusion.49
  174.8 9.0 %dispatch.1 = (bf16[304,768]{1,0:T(8,128)(2,1)}, bf16[304,768]{1,0:T(8,128)(2,1)}, bf16[304,768]{1,0:T(8,128)(2,1)}, bf16[304,768]{1,0:T(8,128)(2,1)}, bf16[304,...) custom-call(s32[2432,1]{1,0:T(8,128)} %select_n.208.refs_0_, ...), custom_call_target="tpu_custom_call" | custom-call | flops 3825205248 | bytes 5308416 | tf_op jit(solution)/shard_map/dispatch/pallas_call | solution.py:693
  183.8 44.4 %conditional.12 = (f32[1024,768]{1,0:T(8,128)}, f32[1024,768]{1,0:T(8,128)}, bf16[1024,3072]{1,0:T(8,128)(2,1)}, bf16[1024,3072]{1,0:T(8,128)(2,1)}, bf16[768,10...) conditional(s32[]{:T(128)} %bitcast.60, () %tuple.131, ...), branch_computations={%region_11.12_spmd, %region_12.13_spmd} | conditional | flops 24159191040 | bytes 52789596 | solution.py:814
  187.5 28.1 %shared_expert.1 = (f32[1024,768]{1,0:T(8,128)}, f32[1024,768]{1,0:T(8,128)}, bf16[1024,3072]{1,0:T(8,128)(2,1)}, bf16[1024,3072]{1,0:T(8,128)(2,1)}, bf16[768,1024]{1,0:T(8,128)(2,1)}) custom-call(bf16[1024,768]{1,0:T(8,128)(2,1)S(1)} %get-tuple-element.363.rows_ref, bf16[1024,768]{1,0:T(8,128)(2,1)S(1)} %get-tuple-element.364.grad_ref.refs_2_, ...), custom_call_target="tpu_custom_call" | custom-call | flops 19327352832 | bytes 22020096 | tf_op jit(solution)/shard_map/cond/branch_1_fun/shared_expert/pallas_call | solution.py:344
  215.7 12.5 %expert_outer.6 = bf16[4,768,768]{2,1,0:T(8,128)(2,1)} custom-call(s32[1]{0:T(128)} %bitcast.1.refs_0_, bf16[1024,3072]{1,0:T(8,128)(2,1)} %get-tuple-element.1161.refs_1_, bf16[1024,768]{1,0:T(8,128)(2,1)S(1)} %get-tuple-element.364.grad_ref.refs_2_, bf16[4,2,96,1024]{3,2,1,0:T(8,128)(2,1)} %bitcast.2.refs_3_, bf16[1024,3072]{1,0:T(8,128)(2,1)} %get-tuple-element.1162.refs_4_), custom_call_target="tpu_custom_call" | custom-call | flops 4831838208 | bytes 25165824 | tf_op jit(solution)/shard_map/cond/branch_1_fun/expert_outer/pallas_call | solution.py:469
  228.2 51.7 %conditional.13 = (bf16[288,768]{1,0:T(8,128)(2,1)}, bf16[288,768]{1,0:T(8,128)(2,1)}, bf16[288,768]{1,0:T(8,128)(2,1)}, bf16[288,768]{1,0:T(8,128)(2,1)}, bf16[...) conditional(s32[]{:T(128)} %bitcast.60, () %tuple.130, ...), branch_computations={%region_13.14_spmd, %region_14.15_spmd} | conditional | flops 27179089920 | bytes 56328596 | solution.py:814
  232.0 34.1 %routed_expert.2 = (bf16[288,768]{1,0:T(8,128)(2,1)}, bf16[288,768]{1,0:T(8,128)(2,1)}, bf16[288,768]{1,0:T(8,128)(2,1)}, bf16[288,768]{1,0:T(8,128)(2,1)}, bf16...) custom-call(bf16[304,768]{1,0:T(8,128)(2,1)} %get-tuple-element.376., ...), custom_call_target="tpu_custom_call" | custom-call | flops 21743271936 | bytes 23592960 | tf_op jit(solution)/shard_map/cond/branch_1_fun/routed_expert/pallas_call | solution.py:344
  266.1 13.9 %expert_outer.7 = bf16[4,768,768]{2,1,0:T(8,128)(2,1)} custom-call(s32[1]{0:T(128)} %bitcast.3.refs_0_, bf16[1152,3072]{1,0:T(8,128)(2,1)} %get-tuple-element.1194.refs_1_, bf16[1152,768]{1,0:T(8,128)(2,1)} %get-tuple-element.1196.refs_2_, bf16[4,2,96,1152]{3,2,1,0:T(8,128)(2,1)} %bitcast.4.refs_3_, bf16[1152,3072]{1,0:T(8,128)(2,1)} %get-tuple-element.1195.refs_4_), custom_call_target="tpu_custom_call" | custom-call | flops 5435817984 | bytes 27131904 | tf_op jit(solution)/shard_map/cond/branch_1_fun/expert_outer/pallas_call | solution.py:469
  280.0 39.6 %conditional.14 = (bf16[4,768,768]{2,1,0:T(8,128)(2,1)}, bf16[4,768,768]{2,1,0:T(8,128)(2,1)}, bf16[288,768]{1,0:T(8,128)(2,1)}, bf16[288,768]{1,0:T(8,128)(2,1)...) conditional(s32[]{:T(128)} %bitcast.60, () %tuple.136, (bf16[768,1152]{1,0:T(8,128)(2,1)}, ...), branch_computations={%region_15.16_spmd, %region_16.17_spmd} | conditional | flops 10267656192 | bytes 95355272 | solution.py:814
  288.3 14.7 %expert_outer.8.refs_7_ = bf16[4,768,768]{2,1,0:T(8,128)(2,1)} custom-call(s32[1]{0:T(128)} %bitcast.5.refs_0_, bf16[1152,3072]{1,0:T(8,128)(2,1)} %get-tuple-element.402.refs_1_, bf16[1152,768]{1,0:T(8,128)(2,1)} %get-tuple-element.403.refs_2_, bf16[4,2,96,1152]{3,2,1,0:T(8,128)(2,1)} %bitcast.6.refs_3_, bf16[1152,3072]{1,0:T(8,128)(2,1)} %get-tuple-element.405.refs_4_, ...), custom_call_target="tpu_custom_call" | custom-call | flops 5435817984 | bytes 27131904 | tf_op jit(solution)/shard_map/cond/branch_1_fun/expert_outer/pallas_call | solution.py:469
  303.0 13.3 %expert_outer.9 = bf16[4,768,768]{2,1,0:T(8,128)(2,1)} custom-call(s32[1]{0:T(128)} %bitcast.5.refs_0_, bf16[1024,3072]{1,0:T(8,128)(2,1)} %get-tuple-element.407.refs_1_, bf16[1024,768]{1,0:T(8,128)(2,1)S(1)} %get-tuple-element.408.refs_2_, bf16[4,2,96,1024]{3,2,1,0:T(8,128)(2,1)} %bitcast.7.refs_3_, bf16[1024,3072]{1,0:T(8,128)(2,1)} %get-tuple-element.410.refs_4_, ...), custom_call_target="tpu_custom_call" | custom-call | flops 4831838208 | bytes 25165824 | tf_op jit(solution)/shard_map/cond/branch_1_fun/expert_outer/pallas_call | solution.py:469
  319.6 64.3 %conditional.15 = (bf16[288,768]{1,0:T(8,128)(2,1)}, bf16[288,768]{1,0:T(8,128)(2,1)}, bf16[288,768]{1,0:T(8,128)(2,1)}, bf16[288,768]{1,0:T(8,128)(2,1)}, bf16[...) conditional(s32[]{:T(128)} %bitcast.60, () %tuple.129, ...), branch_computations={%region_17.18_spmd, %region_18.19_spmd} | conditional | flops 27193245696 | bytes 105382632 | solution.py:814
  320.0 4.5 dynamic-slice_bitcast_fusion
  336.0 34.1 %routed_expert.3 = (bf16[288,768]{1,0:T(8,128)(2,1)}, bf16[288,768]{1,0:T(8,128)(2,1)}, bf16[288,768]{1,0:T(8,128)(2,1)}, bf16[288,768]{1,0:T(8,128)(2,1)}, bf16...) custom-call(bf16[304,768]{1,0:T(8,128)(2,1)S(1)} %copy-done.46, ...), custom_call_target="tpu_custom_call" | custom-call | flops 21743271936 | bytes 23592960 | tf_op jit(solution)/shard_map/cond/branch_1_fun/routed_expert/pallas_call | solution.py:344
  370.0 13.8 %expert_outer.10 = bf16[4,768,768]{2,1,0:T(8,128)(2,1)} custom-call(s32[1]{0:T(128)} %bitcast.8.refs_0_, bf16[1152,3072]{1,0:T(8,128)(2,1)} %get-tuple-element.1243.refs_1_, bf16[1152,768]{1,0:T(8,128)(2,1)} %get-tuple-element.1245.refs_2_, bf16[4,2,96,1152]{3,2,1,0:T(8,128)(2,1)} %bitcast.9.refs_3_, bf16[1152,3072]{1,0:T(8,128)(2,1)} %get-tuple-element.1244.refs_4_), custom_call_target="tpu_custom_call" | custom-call | flops 5435817984 | bytes 27131904 | tf_op jit(solution)/shard_map/cond/branch_1_fun/expert_outer/pallas_call | solution.py:469
  385.3 49.7 %conditional.16 = (bf16[4,768,768]{2,1,0:T(8,128)(2,1)}, bf16[304,768]{1,0:T(8,128)(2,1)}, bf16[304,768]{1,0:T(8,128)(2,1)}, bf16[304,768]{1,0:T(8,128)(2,1)}, b...) conditional(s32[]{:T(128)} %bitcast.60, () %tuple.141, ...), branch_computations={%region_19.20_spmd, %region_20.21_spmd} | conditional | flops 5435817984 | bytes 64979472 | solution.py:814
  394.0 3.9 turn.2
  397.9 3.9 turn.3
  401.8 14.8 %expert_outer.11 = bf16[4,768,768]{2,1,0:T(8,128)(2,1)} custom-call(s32[1]{0:T(128)} %bitcast.16.refs_0_, bf16[1152,3072]{1,0:T(8,128)(2,1)} %get-tuple-element.444.refs_1_, bf16[1152,768]{1,0:T(8,128)(2,1)} %get-tuple-element.445.refs_2_, bf16[4,2,96,1152]{3,2,1,0:T(8,128)(2,1)} %bitcast.17.refs_3_, bf16[1152,3072]{1,0:T(8,128)(2,1)} %get-tuple-element.447.refs_4_, ...), custom_call_target="tpu_custom_call" | custom-call | flops 5435817984 | bytes 27131904 | tf_op jit(solution)/shard_map/cond/branch_1_fun/expert_outer/pallas_call | solution.py:469
  416.6 7.5 %collective-permute-done.18 = bf16[304,768]{1,0:T(8,128)(2,1)} collective-permute-done((bf16[304,768]{1,0:T(8,128)(2,1)}, bf16[304,768]{1,0:T(8,128)(2,1)}, u32[]{:S(2)}, u32[]{:S(2)}) %collective-permute-start.18) | collective-permute-done | bytes 466976 | tf_op jit(solution)/shard_map/cond/branch_1_fun/ppermute | solution.py:820
  424.0 11.0 %collective-permute-done.19 = bf16[304,768]{1,0:T(8,128)(2,1)} collective-permute-done((bf16[304,768]{1,0:T(8,128)(2,1)}, bf16[304,768]{1,0:T(8,128)(2,1)}, u32[]{:S(2)}, u32[]{:S(2)}) %collective-permute-start.19) | collective-permute-done | bytes 466976 | tf_op jit(solution)/shard_map/cond/branch_1_fun/ppermute | solution.py:820
  435.1 46.6 %conditional.17 = (bf16[768,8]{0,1:T(8,128)(2,1)S(1)}, f32[4,768]{1,0:T(4,128)S(1)}, f32[4,768]{1,0:T(4,128)S(1)}, f32[4,768]{1,0:T(4,128)S(1)}, f32[1024,768]{1...) conditional(s32[]{:T(128)} %bitcast.60, () %tuple.140, ...), branch_computations={%region_21.22_spmd, %region_22.30_spmd} | conditional | flops 6332856320 | bytes 93014016 | solution.py:814
  447.4 10.7 %combine.2 = (f32[1024,768]{1,0:T(8,128)}, f32[1024,2]{1,0:T(8,128)}) custom-call(s32[1,2432]{1,0:T(1,128)} %select_n.166.refs_0_, s32[1024,2]{1,0:T(8,128)} %copy.94.refs_1_, f32[1024,768]{1,0:T(8,128)} %get-tuple-element.461.refs_2_, bf16[304,768]{1,0:T(8,128)(2,1)} %get-tuple-element.462.refs_3_, bf16[304,768]{1,0:T(8,128)(2,1)} %get-tuple-element.463.refs_4_, ...), custom_call_target="tpu_custom_call" | custom-call | flops 3825205248 | bytes 10027008 | tf_op jit(solution)/shard_map/cond/branch_1_fun/combine/pallas_call | solution.py:608
  469.8 4.0 convolution_convert_fusion
  477.6 4.1 collective-permute-done.36
  482.3 67.3 %conditional.18 = (bf16[1024,2304]{1,0:T(8,128)(2,1)}, bf16[4,384,768]{2,1,0:T(8,128)(2,1)}, bf16[288,768]{1,0:T(8,128)(2,1)}, bf16[288,768]{1,0:T(8,128)(2,1)},...) conditional(s32[]{:T(128)} %bitcast.60, () %tuple.139, ...), branch_computations={%region_30.31_spmd, %region_31.32_spmd} | conditional | flops 34639970304 | bytes 76874376 | solution.py:814
  493.4 42.5 %attend_back.1.refs_3_ = bf16[1024,2304]{1,0:T(8,128)(2,1)} custom-call(s32[4]{0:T(128)S(1)} %copy-done.45, bf16[1024,2304]{1,0:T(8,128)(2,1)} %get-tuple-element.487.q_ref.k_ref.v_ref, bf16[1024,2304]{1,0:T(8,128)(2,1)} %get-tuple-element.487.q_ref.k_ref.v_ref, bf16[1024,2304]{1,0:T(8,128)(2,1)} %get-tuple-element.487.q_ref.k_ref.v_ref, ...), custom_call_target="tpu_custom_call" | custom-call | flops 32212254720 | bytes 12582912 | tf_op jit(solution)/shard_map/cond/branch_1_fun/attend_back/pallas_call | solution.py:193
  542.0 7.6 %attention_outer.2 = bf16[4,384,768]{2,1,0:T(8,128)(2,1)} custom-call(s32[1]{0:T(128)} %bitcast.29.refs_0_, bf16[4,2,96,1024]{3,2,1,0:T(8,128)(2,1)} %bitcast.30.refs_1_, bf16[4,2,96,1024]{3,2,1,0:T(8,128)(2,1)} %bitcast.31.refs_2_, bf16[1024,2304]{1,0:T(8,128)(2,1)} %attend_back.1.refs_3_, bf16[1024,768]{1,0:T(8,128)(2,1)} %get-tuple-element.493.refs_4_), custom_call_target="tpu_custom_call" | custom-call | flops 2415919104 | bytes 14155776 | tf_op jit(solution)/shard_map/cond/branch_1_fun/attention_outer/pallas_call | solution.py:469
  549.7 44.7 %conditional.19 = (bf16[1024,768]{1,0:T(8,128)(2,1)}, f32[4,768]{1,0:T(4,128)S(1)}, f32[4,768]{1,0:T(4,128)S(1)}, bf16[4,384,768]{2,1,0:T(8,128)(2,1)}, f32[192,...) conditional(s32[]{:T(128)} %bitcast.60, () %tuple.145, ...), branch_computations={%region_32.33_spmd, %region_33.40_spmd} | conditional | flops 6063634432 | bytes 77820512 | solution.py:814
  555.4 7.2 %fusion.11 = (f32[1024]{0:T(1024)S(1)}, f32[1024]{0:T(1024)S(1)}, f32[1024,768]{1,0:T(8,128)S(1)}) fusion(f32[4,768]{1,0:T(4,128)S(1)} %slice_add_fusion, f32[1024]{0:T(1024)S(1)} %add_rsqrt_fusion, f32[1024]{0:T(1024)S(1)} %broadcast_multiply_fusion.2, bf16[1024,768]{1,0:T(8,128)(2,1)S(1)} %get-tuple-element.505, ...), kind=kOutput, calls=%fused_computation.31 | convolution fusion | flops 3629381632 | bytes 13004800 | tf_op jit(solution)/shard_map/cond/branch_1_fun/dot_general | solution.py:34
  565.2 4.3 fusion.9
  573.1 7.6 %collective-permute-done.42 = bf16[192,768]{1,0:T(8,128)(2,1)} collective-permute-done((bf16[192,768]{1,0:T(8,128)(2,1)S(1)}, bf16[192,768]{1,0:T(8,128)(2,1)}, u32[]{:S(2)}, u32[]{:S(2)}) %collective-permute-start.42) | collective-permute-done | bytes 294944 | tf_op jit(solution)/shard_map/cond/branch_1_fun/ppermute | solution.py:806
  586.0 8.3 %attention_outer.3 = bf16[4,384,768]{2,1,0:T(8,128)(2,1)} custom-call(s32[1]{0:T(128)} %bitcast.40.refs_0_, bf16[4,2,96,1024]{3,2,1,0:T(8,128)(2,1)} %bitcast.41.refs_1_, bf16[4,2,96,1024]{3,2,1,0:T(8,128)(2,1)} %bitcast.42.refs_2_, bf16[1024,2304]{1,0:T(8,128)(2,1)} %get-tuple-element.506.refs_3_, bf16[1024,768]{1,0:T(8,128)(2,1)} %get-tuple-element.511.refs_4_, ...), custom_call_target="tpu_custom_call" | custom-call | flops 2415919104 | bytes 14155776 | tf_op jit(solution)/shard_map/cond/branch_1_fun/attention_outer/pallas_call | solution.py:469
  594.4 35.7 %conditional.20 = (f32[2,384,768]{2,1,0:T(8,128)}, f32[2,96,3072]{2,1,0:T(8,128)}, bf16[1024,768]{1,0:T(8,128)(2,1)}, f32[4,768]{1,0:T(4,128)S(1)}, f32[384,768]...) conditional(s32[]{:T(128)} %bitcast.60, () %tuple.128, ...), branch_computations={%region_40.41_spmd, %region_41.43_spmd} | conditional | flops 3630368512 | bytes 77951240 | solution.py:814
  602.6 9.0 %combine.3 = (f32[1024,768]{1,0:T(8,128)}, f32[1024,2]{1,0:T(8,128)}) custom-call(s32[1,2304]{1,0:T(1,128)} %select_n.182.refs_0_, s32[1024,2]{1,0:T(8,128)} %copy.97.refs_1_, f32[1024,768]{1,0:T(8,128)} %get-tuple-element.528.refs_2_, bf16[288,768]{1,0:T(8,128)(2,1)} %get-tuple-element.529.refs_3_, bf16[288,768]{1,0:T(8,128)(2,1)} %get-tuple-element.530.refs_4_, ...), custom_call_target="tpu_custom_call" | custom-call | flops 3623878656 | bytes 9830400 | tf_op jit(solution)/shard_map/cond/branch_1_fun/combine/pallas_call | solution.py:608
  615.0 8.2 %expert_sums.1 = (f32[2,384,768]{2,1,0:T(8,128)}, f32[2,96,3072]{2,1,0:T(8,128)}) custom-call(bf16[1536,768]{1,0:T(8,128)(2,1)} %get-tuple-element.514.refs_0_, bf16[1536,768]{1,0:T(8,128)(2,1)} %get-tuple-element.515.refs_1_, bf16[1536,768]{1,0:T(8,128)(2,1)} %get-tuple-element.516.refs_2_, bf16[1536,768]{1,0:T(8,128)(2,1)} %get-tuple-element.517.refs_3_.refs_7_, ...), custom_call_target="tpu_custom_call" | custom-call | bytes 18874368 | tf_op jit(solution)/shard_map/cond/branch_1_fun/expert_sums/pallas_call | solution.py:660
  637.7 22.5 %conditional.21 = (f32[96,768]{1,0:T(8,128)S(1)}, f32[96,768]{1,0:T(8,128)S(1)}, f32[96,768]{1,0:T(8,128)S(1)}, f32[96,768]{1,0:T(8,128)}, f32[96,576]{1,0:T(8,128)S(1)}, /*index=5*/f32[96,192]{1,0:T(8,128)S(1)}) conditional(s32[]{:T(128)} %bitcast.60, () %tuple.148, bf16[4,96,768]{1,2,0:T(8,128)(2,1)S(1)} %maximum_bitcast_fusion), branch_computations={%region_43.44_spmd, %region_44.45_spmd} | conditional | flops 516113 | bytes 6488440 | solution.py:814
  642.1 4.5 collective-permute-done.24
  646.6 5.9 collective-permute-done.25
  652.5 5.0 collective-permute-done.26
  (366 shorter events, 190.0 us)
Async XLA Ops:
  7.2 148.6 %all-gather.3.cloned.1.call-start = ((), (), s32[]{:S(2)}) async-start(), calls=%async_computation.3 | async-start | bytes 11354112 | tf_op jit(solution)/shard_map/all_gather | solution.py:893
  17.1 17.8 %all-to-all-start = ((bf16[32,2,1800]{2,1,0:T(2,128)(2,1)}), bf16[32,2,1800]{2,1,0:T(2,128)(2,1)S(1)}, u32[]{:S(2)}, u32[]{:S(2)}) async-start(bf16[32,2,1800]{2,1,0:T(2,128)(2,1)} %reshape.854), calls=%async_computation | async-start | bytes 491520 | tf_op jit(solution)/shard_map/all_to_all | solution.py:794
  23.3 86.6 %copy-start.39 = (s32[4]{0:T(128)}, s32[4]{0:T(128)S(1)}, u32[]{:S(2)}) copy-start(s32[4]{0:T(128)S(1)} %get-tuple-element.1060) | copy-start | bytes 52
  38.6 60.0 %all-to-all-start.1 = ((f32[32,4,144]{2,1,0:T(4,128)}), f32[32,4,144]{2,1,0:T(4,128)S(1)}, u32[]{:S(2)}, u32[]{:S(2)}) async-start(f32[32,4,144]{2,1,0:T(4,128)} %reshape.817), calls=%async_computation.1 | async-start | bytes 262144 | tf_op jit(solution)/shard_map/all_to_all | solution.py:794
  111.1 37.8 %collective-permute-start.31 = (bf16[288,768]{1,0:T(8,128)(2,1)}, bf16[288,768]{1,0:T(8,128)(2,1)}, u32[]{:S(2)}, u32[]{:S(2)}) collective-permute-start(bf16[288,768]{1,0:T(8,128)(2,1)} %slice.235), channel_id=1, source_target_pairs={{0,1},{1,0},{2,3},{3,2},{4,5},{5,4},{6,7},{7,6},{8,9},{9,8},{10,11... | collective-permute-start | bytes 1327112 | tf_op jit(solution)/shard_map/cond/branch_1_fun/ppermute | solution.py:820
  111.8 37.0 %collective-permute-start.32 = (bf16[288,768]{1,0:T(8,128)(2,1)}, bf16[288,768]{1,0:T(8,128)(2,1)}, u32[]{:S(2)}, u32[]{:S(2)}) collective-permute-start(bf16[288,768]{1,0:T(8,128)(2,1)} %slice.236), channel_id=1, source_target_pairs={{0,2},{1,3},{2,0},{3,1},{4,6},{5,7},{6,4},{7,5},{8,10},{9,11},{10,... | collective-permute-start | bytes 1327112 | tf_op jit(solution)/shard_map/cond/branch_1_fun/ppermute | solution.py:820
  114.7 40.6 %collective-permute-start.33 = (bf16[288,768]{1,0:T(8,128)(2,1)}, bf16[288,768]{1,0:T(8,128)(2,1)}, u32[]{:S(2)}, u32[]{:S(2)}) collective-permute-start(bf16[288,768]{1,0:T(8,128)(2,1)} %slice.237), channel_id=1, source_target_pairs={{0,3},{1,2},{2,1},{3,0},{4,7},{5,6},{6,5},{7,4},{8,11},{9,10},{10,... | collective-permute-start | bytes 1327112 | tf_op jit(solution)/shard_map/cond/branch_1_fun/ppermute | solution.py:820
  184.0 44.2 %collective-permute-start = (bf16[304,768]{1,0:T(8,128)(2,1)}, bf16[304,768]{1,0:T(8,128)(2,1)}, u32[]{:S(2)}, u32[]{:S(2)}) collective-permute-start(bf16[304,768]{1,0:T(8,128)(2,1)} %get-tuple-element.373), channel_id=1, source_target_pairs={{0,1},{1,0},{2,3},{3,2},{4,5},{5,4},{6,7},{7,6},{8,9},{9,8},{10,11... | collective-permute-start | bytes 1400840 | tf_op jit(solution)/shard_map/cond/branch_1_fun/ppermute | solution.py:820
  184.0 44.2 %collective-permute-start.1 = (bf16[304,768]{1,0:T(8,128)(2,1)}, bf16[304,768]{1,0:T(8,128)(2,1)}, u32[]{:S(2)}, u32[]{:S(2)}) collective-permute-start(bf16[304,768]{1,0:T(8,128)(2,1)} %get-tuple-element.374), channel_id=1, source_target_pairs={{0,2},{1,3},{2,0},{3,1},{4,6},{5,7},{6,4},{7,5},{8,10},{9,11},{10,... | collective-permute-start | bytes 1400840 | tf_op jit(solution)/shard_map/cond/branch_1_fun/ppermute | solution.py:820
  186.1 42.1 %collective-permute-start.2 = (bf16[304,768]{1,0:T(8,128)(2,1)}, bf16[304,768]{1,0:T(8,128)(2,1)}, u32[]{:S(2)}, u32[]{:S(2)}) collective-permute-start(bf16[304,768]{1,0:T(8,128)(2,1)} %get-tuple-element.375), channel_id=1, source_target_pairs={{0,3},{1,2},{2,1},{3,0},{4,7},{5,6},{6,5},{7,4},{8,11},{9,10},{10,... | collective-permute-start | bytes 1400840 | tf_op jit(solution)/shard_map/cond/branch_1_fun/ppermute | solution.py:820
  228.5 51.5 %collective-permute-start.3 = (bf16[304,768]{1,0:T(8,128)(2,1)}, bf16[304,768]{1,0:T(8,128)(2,1)}, u32[]{:S(2)}, u32[]{:S(2)}) collective-permute-start(bf16[304,768]{1,0:T(8,128)(2,1)} %get-tuple-element.399), channel_id=1, source_target_pairs={{0,1},{1,0},{2,3},{3,2},{4,5},{5,4},{6,7},{7,6},{8,9},{9,8},{10,11... | collective-permute-start | bytes 1400840 | tf_op jit(solution)/shard_map/cond/branch_1_fun/ppermute | solution.py:820
  229.5 50.5 %collective-permute-start.4 = (bf16[304,768]{1,0:T(8,128)(2,1)}, bf16[304,768]{1,0:T(8,128)(2,1)}, u32[]{:S(2)}, u32[]{:S(2)}) collective-permute-start(bf16[304,768]{1,0:T(8,128)(2,1)} %get-tuple-element.400), channel_id=1, source_target_pairs={{0,2},{1,3},{2,0},{3,1},{4,6},{5,7},{6,4},{7,5},{8,10},{9,11},{10,... | collective-permute-start | bytes 1400840 | tf_op jit(solution)/shard_map/cond/branch_1_fun/ppermute | solution.py:820
  230.6 49.4 %collective-permute-start.5 = (bf16[304,768]{1,0:T(8,128)(2,1)}, bf16[304,768]{1,0:T(8,128)(2,1)}, u32[]{:S(2)}, u32[]{:S(2)}) collective-permute-start(bf16[304,768]{1,0:T(8,128)(2,1)} %get-tuple-element.401), channel_id=1, source_target_pairs={{0,3},{1,2},{2,1},{3,0},{4,7},{5,6},{6,5},{7,4},{8,11},{9,10},{10,... | collective-permute-start | bytes 1400840 | tf_op jit(solution)/shard_map/cond/branch_1_fun/ppermute | solution.py:820
  280.0 8.3 %collective-permute-start.6 = (bf16[4,768,768]{2,1,0:T(8,128)(2,1)}, bf16[4,768,768]{2,1,0:T(8,128)(2,1)}, u32[]{:S(2)}, u32[]{:S(2)}) collective-permute-start(bf16[4,768,768]{2,1,0:T(8,128)(2,1)} %get-tuple-element.406), channel_id=1, source_target_pairs={{0,4},{4,0},{8,12},{12,8},{16,20},{20,16},{24,28},{28,24},{1,5},{5... | collective-permute-start | bytes 14155784 | tf_op jit(solution)/shard_map/cond/branch_1_fun/ppermute | solution.py:574
  280.1 23.0 %collective-permute-start.7 = (bf16[4,768,768]{2,1,0:T(8,128)(2,1)}, bf16[4,768,768]{2,1,0:T(8,128)(2,1)}, u32[]{:S(2)}, u32[]{:S(2)}) collective-permute-start(bf16[4,768,768]{2,1,0:T(8,128)(2,1)} %get-tuple-element.411), channel_id=1, source_target_pairs={{0,4},{4,0},{8,12},{12,8},{16,20},{20,16},{24,28},{28,24},{1,5},{5... | collective-permute-start | bytes 14155784 | tf_op jit(solution)/shard_map/cond/branch_1_fun/ppermute | solution.py:574
  280.6 35.7 %collective-permute-start.10 = (bf16[288,768]{1,0:T(8,128)(2,1)}, bf16[288,768]{1,0:T(8,128)(2,1)}, u32[]{:S(2)}, u32[]{:S(2)}) collective-permute-start(bf16[288,768]{1,0:T(8,128)(2,1)} %get-tuple-element.415), channel_id=1, source_target_pairs={{0,3},{1,2},{2,1},{3,0},{4,7},{5,6},{6,5},{7,4},{8,11},{9,10},{10,... | collective-permute-start | bytes 1327112 | tf_op jit(solution)/shard_map/cond/branch_1_fun/ppermute | solution.py:820
  281.2 35.2 %collective-permute-start.8 = (bf16[288,768]{1,0:T(8,128)(2,1)}, bf16[288,768]{1,0:T(8,128)(2,1)}, u32[]{:S(2)}, u32[]{:S(2)}) collective-permute-start(bf16[288,768]{1,0:T(8,128)(2,1)} %get-tuple-element.413), channel_id=1, source_target_pairs={{0,1},{1,0},{2,3},{3,2},{4,5},{5,4},{6,7},{7,6},{8,9},{9,8},{10,11... | collective-permute-start | bytes 1327112 | tf_op jit(solution)/shard_map/cond/branch_1_fun/ppermute | solution.py:820
  283.9 35.6 %collective-permute-start.9 = (bf16[288,768]{1,0:T(8,128)(2,1)}, bf16[288,768]{1,0:T(8,128)(2,1)}, u32[]{:S(2)}, u32[]{:S(2)}) collective-permute-start(bf16[288,768]{1,0:T(8,128)(2,1)} %get-tuple-element.414), channel_id=1, source_target_pairs={{0,2},{1,3},{2,0},{3,1},{4,6},{5,7},{6,4},{7,5},{8,10},{9,11},{10,... | collective-permute-start | bytes 1327112 | tf_op jit(solution)/shard_map/cond/branch_1_fun/ppermute | solution.py:820
  326.1 57.8 %collective-permute-start.14 = (bf16[1536,768]{1,0:T(8,128)(2,1)}, bf16[1536,768]{1,0:T(8,128)(2,1)}, u32[]{:S(2)}, u32[]{:S(2)}) collective-permute-start(bf16[1536,768]{1,0:T(8,128)(2,1)} %pad_maximum_fusion.1), channel_id=1, source_target_pairs={{0,8},{4,12},{8,0},{12,4},{16,24},{20,28},{24,16},{28,20},{1,9},{5... | collective-permute-start | bytes 7077896 | tf_op jit(solution)/shard_map/cond/branch_1_fun/ppermute | solution.py:833
  328.8 55.1 %collective-permute-start.15 = (bf16[1536,768]{1,0:T(8,128)(2,1)}, bf16[1536,768]{1,0:T(8,128)(2,1)}, u32[]{:S(2)}, u32[]{:S(2)}) collective-permute-start(bf16[1536,768]{1,0:T(8,128)(2,1)} %pad_maximum_fusion.2), channel_id=1, source_target_pairs={{0,16},{4,20},{8,24},{12,28},{16,0},{20,4},{24,8},{28,12},{1,17},{... | collective-permute-start | bytes 7077896 | tf_op jit(solution)/shard_map/cond/branch_1_fun/ppermute | solution.py:833
  329.7 54.1 %collective-permute-start.11 = (bf16[304,768]{1,0:T(8,128)(2,1)}, bf16[304,768]{1,0:T(8,128)(2,1)}, u32[]{:S(2)}, u32[]{:S(2)}) collective-permute-start(bf16[304,768]{1,0:T(8,128)(2,1)} %get-tuple-element.439), channel_id=1, source_target_pairs={{0,1},{1,0},{2,3},{3,2},{4,5},{5,4},{6,7},{7,6},{8,9},{9,8},{10,11... | collective-permute-start | bytes 1400840 | tf_op jit(solution)/shard_map/cond/branch_1_fun/ppermute | solution.py:820
  333.0 50.9 %collective-permute-start.12 = (bf16[304,768]{1,0:T(8,128)(2,1)}, bf16[304,768]{1,0:T(8,128)(2,1)}, u32[]{:S(2)}, u32[]{:S(2)}) collective-permute-start(bf16[304,768]{1,0:T(8,128)(2,1)} %get-tuple-element.440), channel_id=1, source_target_pairs={{0,2},{1,3},{2,0},{3,1},{4,6},{5,7},{6,4},{7,5},{8,10},{9,11},{10,... | collective-permute-start | bytes 1400840 | tf_op jit(solution)/shard_map/cond/branch_1_fun/ppermute | solution.py:820
  333.1 50.8 %collective-permute-start.13 = (bf16[304,768]{1,0:T(8,128)(2,1)}, bf16[304,768]{1,0:T(8,128)(2,1)}, u32[]{:S(2)}, u32[]{:S(2)}) collective-permute-start(bf16[304,768]{1,0:T(8,128)(2,1)} %get-tuple-element.441), channel_id=1, source_target_pairs={{0,3},{1,2},{2,1},{3,0},{4,7},{5,6},{6,5},{7,4},{8,11},{9,10},{10,... | collective-permute-start | bytes 1400840 | tf_op jit(solution)/shard_map/cond/branch_1_fun/ppermute | solution.py:820
  385.5 16.3 %collective-permute-start.16 = (bf16[4,768,768]{2,1,0:T(8,128)(2,1)}, bf16[4,768,768]{2,1,0:T(8,128)(2,1)}, u32[]{:S(2)}, u32[]{:S(2)}) collective-permute-start(bf16[4,768,768]{2,1,0:T(8,128)(2,1)} %get-tuple-element.448), channel_id=1, source_target_pairs={{0,4},{4,0},{8,12},{12,8},{16,20},{20,16},{24,28},{28,24},{1,5},{5... | collective-permute-start | bytes 14155784 | tf_op jit(solution)/shard_map/cond/branch_1_fun/ppermute | solution.py:574
  388.1 46.8 %collective-permute-start.20 = (bf16[768,768]{1,0:T(8,128)(2,1)}, bf16[768,768]{1,0:T(8,128)(2,1)}, u32[]{:S(2)}, u32[]{:S(2)}) collective-permute-start(bf16[768,768]{1,0:T(8,128)(2,1)} %dynamic-slice_bitcast_fusion.6), channel_id=1, source_target_pairs={{0,24},{4,28},{8,16},{12,20},{16,8},{20,12},{24,0},{28,4},{1,25},{... | collective-permute-start | bytes 3538952 | tf_op jit(solution)/shard_map/cond/branch_1_fun/ppermute | solution.py:833
  389.6 26.9 %collective-permute-start.17 = (bf16[304,768]{1,0:T(8,128)(2,1)}, bf16[304,768]{1,0:T(8,128)(2,1)}, u32[]{:S(2)}, u32[]{:S(2)}) collective-permute-start(bf16[304,768]{1,0:T(8,128)(2,1)} %get-tuple-element.450), channel_id=1, source_target_pairs={{0,1},{1,0},{2,3},{3,2},{4,5},{5,4},{6,7},{7,6},{8,9},{9,8},{10,11... | collective-permute-start | bytes 1400840 | tf_op jit(solution)/shard_map/cond/branch_1_fun/ppermute | solution.py:820
  392.5 31.5 %collective-permute-start.18 = (bf16[304,768]{1,0:T(8,128)(2,1)}, bf16[304,768]{1,0:T(8,128)(2,1)}, u32[]{:S(2)}, u32[]{:S(2)}) collective-permute-start(bf16[304,768]{1,0:T(8,128)(2,1)} %get-tuple-element.451), channel_id=1, source_target_pairs={{0,2},{1,3},{2,0},{3,1},{4,6},{5,7},{6,4},{7,5},{8,10},{9,11},{10,... | collective-permute-start | bytes 1400840 | tf_op jit(solution)/shard_map/cond/branch_1_fun/ppermute | solution.py:820
  392.6 42.4 %collective-permute-start.19 = (bf16[304,768]{1,0:T(8,128)(2,1)}, bf16[304,768]{1,0:T(8,128)(2,1)}, u32[]{:S(2)}, u32[]{:S(2)}) collective-permute-start(bf16[304,768]{1,0:T(8,128)(2,1)} %get-tuple-element.452), channel_id=1, source_target_pairs={{0,3},{1,2},{2,1},{3,0},{4,7},{5,6},{6,5},{7,4},{8,11},{9,10},{10,... | collective-permute-start | bytes 1400840 | tf_op jit(solution)/shard_map/cond/branch_1_fun/ppermute | solution.py:820
  439.0 42.7 %collective-permute-start.37 = (bf16[768,768]{1,0:T(8,128)(2,1)}, bf16[768,768]{1,0:T(8,128)(2,1)}, u32[]{:S(2)}, u32[]{:S(2)}) collective-permute-start(bf16[768,768]{1,0:T(8,128)(2,1)} %get-tuple-element.1097), channel_id=1, source_target_pairs={{0,8},{4,12},{8,0},{12,4},{16,24},{20,28},{24,16},{28,20},{1,9},{5... | collective-permute-start | bytes 3538952 | tf_op jit(solution)/shard_map/cond/branch_1_fun/ppermute | solution.py:833
  440.2 41.5 %collective-permute-start.38 = (bf16[768,768]{1,0:T(8,128)(2,1)}, bf16[768,768]{1,0:T(8,128)(2,1)}, u32[]{:S(2)}, u32[]{:S(2)}) collective-permute-start(bf16[768,768]{1,0:T(8,128)(2,1)} %get-tuple-element.1096), channel_id=1, source_target_pairs={{0,16},{4,20},{8,24},{12,28},{16,0},{20,4},{24,8},{28,12},{1,17},{... | collective-permute-start | bytes 3538952 | tf_op jit(solution)/shard_map/cond/branch_1_fun/ppermute | solution.py:833
  441.0 36.6 %collective-permute-start.34 = (bf16[288,768]{1,0:T(8,128)(2,1)}, bf16[288,768]{1,0:T(8,128)(2,1)}, u32[]{:S(2)}, u32[]{:S(2)}) collective-permute-start(bf16[288,768]{1,0:T(8,128)(2,1)} %get-tuple-element.482), channel_id=1, source_target_pairs={{0,1},{1,0},{2,3},{3,2},{4,5},{5,4},{6,7},{7,6},{8,9},{9,8},{10,11... | collective-permute-start | bytes 1327112 | tf_op jit(solution)/shard_map/cond/branch_1_fun/ppermute | solution.py:820
  441.0 36.6 %collective-permute-start.35 = (bf16[288,768]{1,0:T(8,128)(2,1)}, bf16[288,768]{1,0:T(8,128)(2,1)}, u32[]{:S(2)}, u32[]{:S(2)}) collective-permute-start(bf16[288,768]{1,0:T(8,128)(2,1)} %get-tuple-element.483), channel_id=1, source_target_pairs={{0,2},{1,3},{2,0},{3,1},{4,6},{5,7},{6,4},{7,5},{8,10},{9,11},{10,... | collective-permute-start | bytes 1327112 | tf_op jit(solution)/shard_map/cond/branch_1_fun/ppermute | solution.py:820
  443.1 38.6 %collective-permute-start.36 = (bf16[288,768]{1,0:T(8,128)(2,1)}, bf16[288,768]{1,0:T(8,128)(2,1)}, u32[]{:S(2)}, u32[]{:S(2)}) collective-permute-start(bf16[288,768]{1,0:T(8,128)(2,1)} %get-tuple-element.484), channel_id=1, source_target_pairs={{0,3},{1,2},{2,1},{3,0},{4,7},{5,6},{6,5},{7,4},{8,11},{9,10},{10,... | collective-permute-start | bytes 1327112 | tf_op jit(solution)/shard_map/cond/branch_1_fun/ppermute | solution.py:820
  485.9 63.8 %collective-permute-start.30 = (bf16[1536,768]{1,0:T(8,128)(2,1)}, bf16[1536,768]{1,0:T(8,128)(2,1)}, u32[]{:S(2)}, u32[]{:S(2)}) collective-permute-start(bf16[1536,768]{1,0:T(8,128)(2,1)} %pad_maximum_fusion.3), channel_id=1, source_target_pairs={{0,24},{4,28},{8,16},{12,20},{16,8},{20,12},{24,0},{28,4},{1,25},{... | collective-permute-start | bytes 7077896 | tf_op jit(solution)/shard_map/cond/branch_1_fun/ppermute | solution.py:833
  487.3 62.3 %collective-permute-start.27 = (bf16[288,768]{1,0:T(8,128)(2,1)}, bf16[288,768]{1,0:T(8,128)(2,1)}, u32[]{:S(2)}, u32[]{:S(2)}) collective-permute-start(bf16[288,768]{1,0:T(8,128)(2,1)} %get-tuple-element.495), channel_id=1, source_target_pairs={{0,1},{1,0},{2,3},{3,2},{4,5},{5,4},{6,7},{7,6},{8,9},{9,8},{10,11... | collective-permute-start | bytes 1327112 | tf_op jit(solution)/shard_map/cond/branch_1_fun/ppermute | solution.py:820
  487.3 62.3 %collective-permute-start.28 = (bf16[288,768]{1,0:T(8,128)(2,1)}, bf16[288,768]{1,0:T(8,128)(2,1)}, u32[]{:S(2)}, u32[]{:S(2)}) collective-permute-start(bf16[288,768]{1,0:T(8,128)(2,1)} %get-tuple-element.496), channel_id=1, source_target_pairs={{0,2},{1,3},{2,0},{3,1},{4,6},{5,7},{6,4},{7,5},{8,10},{9,11},{10,... | collective-permute-start | bytes 1327112 | tf_op jit(solution)/shard_map/cond/branch_1_fun/ppermute | solution.py:820
  489.4 60.2 %collective-permute-start.29 = (bf16[288,768]{1,0:T(8,128)(2,1)}, bf16[288,768]{1,0:T(8,128)(2,1)}, u32[]{:S(2)}, u32[]{:S(2)}) collective-permute-start(bf16[288,768]{1,0:T(8,128)(2,1)} %get-tuple-element.497), channel_id=1, source_target_pairs={{0,3},{1,2},{2,1},{3,0},{4,7},{5,6},{6,5},{7,4},{8,11},{9,10},{10,... | collective-permute-start | bytes 1327112 | tf_op jit(solution)/shard_map/cond/branch_1_fun/ppermute | solution.py:820
  550.1 35.9 %collective-permute-start.39 = (bf16[4,384,768]{2,1,0:T(8,128)(2,1)}, bf16[4,384,768]{2,1,0:T(8,128)(2,1)}, u32[]{:S(2)}, u32[]{:S(2)}) collective-permute-start(bf16[4,384,768]{2,1,0:T(8,128)(2,1)} %get-tuple-element.512), channel_id=1, source_target_pairs={{0,4},{4,0},{8,12},{12,8},{16,20},{20,16},{24,28},{28,24},{1,5},{5... | collective-permute-start | bytes 7077896 | tf_op jit(solution)/shard_map/cond/branch_1_fun/ppermute | solution.py:574
  551.0 18.5 %collective-permute-start.40 = (bf16[192,768]{1,0:T(8,128)(2,1)}, bf16[192,768]{1,0:T(8,128)(2,1)}, u32[]{:S(2)}, u32[]{:S(2)}) collective-permute-start(bf16[192,768]{1,0:T(8,128)(2,1)} %get-tuple-element.1080), channel_id=1, source_target_pairs={{0,1},{1,0},{2,3},{3,2},{4,5},{5,4},{6,7},{7,6},{8,9},{9,8},{10,11... | collective-permute-start | bytes 884744 | tf_op jit(solution)/shard_map/cond/branch_1_fun/ppermute | solution.py:806
  551.9 21.2 %collective-permute-start.41 = (bf16[192,768]{1,0:T(8,128)(2,1)S(1)}, bf16[192,768]{1,0:T(8,128)(2,1)}, u32[]{:S(2)}, u32[]{:S(2)}) collective-permute-start(bf16[192,768]{1,0:T(8,128)(2,1)S(1)} %get-tuple-element.1082), channel_id=1, source_target_pairs={{0,2},{1,3},{2,0},{3,1},{4,6},{5,7},{6,4},{7,5},{8,10},{9,11},{10,... | collective-permute-start | bytes 884744 | tf_op jit(solution)/shard_map/cond/branch_1_fun/ppermute | solution.py:806
  553.0 27.6 %collective-permute-start.42 = (bf16[192,768]{1,0:T(8,128)(2,1)S(1)}, bf16[192,768]{1,0:T(8,128)(2,1)}, u32[]{:S(2)}, u32[]{:S(2)}) collective-permute-start(bf16[192,768]{1,0:T(8,128)(2,1)S(1)} %get-tuple-element.1081), channel_id=1, source_target_pairs={{0,3},{1,2},{2,1},{3,0},{4,7},{5,6},{6,5},{7,4},{8,11},{9,10},{10,... | collective-permute-start | bytes 884744 | tf_op jit(solution)/shard_map/cond/branch_1_fun/ppermute | solution.py:806
  597.2 29.4 %collective-permute-start.21 = (bf16[384,768]{1,0:T(8,128)(2,1)}, bf16[384,768]{1,0:T(8,128)(2,1)}, u32[]{:S(2)}, u32[]{:S(2)}) collective-permute-start(bf16[384,768]{1,0:T(8,128)(2,1)} %get-tuple-element.1090), channel_id=1, source_target_pairs={{0,8},{4,12},{8,0},{12,4},{16,24},{20,28},{24,16},{28,20},{1,9},{5... | collective-permute-start | bytes 1769480 | tf_op jit(solution)/shard_map/cond/branch_1_fun/ppermute | solution.py:833
  598.3 28.2 %collective-permute-start.22 = (bf16[384,768]{1,0:T(8,128)(2,1)}, bf16[384,768]{1,0:T(8,128)(2,1)}, u32[]{:S(2)}, u32[]{:S(2)}) collective-permute-start(bf16[384,768]{1,0:T(8,128)(2,1)} %get-tuple-element.1089), channel_id=1, source_target_pairs={{0,16},{4,20},{8,24},{12,28},{16,0},{20,4},{24,8},{28,12},{1,17},{... | collective-permute-start | bytes 1769480 | tf_op jit(solution)/shard_map/cond/branch_1_fun/ppermute | solution.py:833
  599.2 26.3 %collective-permute-start.23 = (bf16[384,768]{1,0:T(8,128)(2,1)}, bf16[384,768]{1,0:T(8,128)(2,1)S(1)}, u32[]{:S(2)}, u32[]{:S(2)}) collective-permute-start(bf16[384,768]{1,0:T(8,128)(2,1)} %get-tuple-element.1088), channel_id=1, source_target_pairs={{0,24},{4,28},{8,16},{12,20},{16,8},{20,12},{24,0},{28,4},{1,25},{... | collective-permute-start | bytes 1769480 | tf_op jit(solution)/shard_map/cond/branch_1_fun/ppermute | solution.py:833
  632.2 28.1 %all-to-all-start.2 = ((bf16[32,39,128]{2,1,0:T(8,128)(2,1)}), bf16[32,39,128]{2,1,0:T(8,128)(2,1)S(1)}, u32[]{:S(2)}, u32[]{:S(2)}) async-start(bf16[32,39,128]{2,1,0:T(8,128)(2,1)} %reshape.830), calls=%async_computation.2 | async-start | bytes 655360 | tf_op jit(solution)/shard_map/all_to_all | solution.py:794
  638.0 8.6 %collective-permute-start.24 = (bf16[96,768]{1,0:T(8,128)(2,1)S(1)}, bf16[96,768]{1,0:T(8,128)(2,1)S(1)}, u32[]{:S(2)}, u32[]{:S(2)}) collective-permute-start(bf16[96,768]{1,0:T(8,128)(2,1)S(1)} %bitcast.229), channel_id=1, source_target_pairs={{0,1},{1,0},{2,3},{3,2},{4,5},{5,4},{6,7},{7,6},{8,9},{9,8},{10,11... | collective-permute-start | bytes 442376 | tf_op jit(solution)/shard_map/cond/branch_1_fun/ppermute | solution.py:806
  638.5 14.1 %collective-permute-start.25 = (bf16[96,768]{1,0:T(8,128)(2,1)S(1)}, bf16[96,768]{1,0:T(8,128)(2,1)S(1)}, u32[]{:S(2)}, u32[]{:S(2)}) collective-permute-start(bf16[96,768]{1,0:T(8,128)(2,1)S(1)} %bitcast.230), channel_id=1, source_target_pairs={{0,2},{1,3},{2,0},{3,1},{4,6},{5,7},{6,4},{7,5},{8,10},{9,11},{10,... | collective-permute-start | bytes 442376 | tf_op jit(solution)/shard_map/cond/branch_1_fun/ppermute | solution.py:806
  641.3 16.2 %collective-permute-start.26 = (bf16[96,768]{1,0:T(8,128)(2,1)S(1)}, bf16[96,768]{1,0:T(8,128)(2,1)S(1)}, u32[]{:S(2)}, u32[]{:S(2)}) collective-permute-start(bf16[96,768]{1,0:T(8,128)(2,1)S(1)} %bitcast.231), channel_id=1, source_target_pairs={{0,3},{1,2},{2,1},{3,0},{4,7},{5,6},{6,5},{7,4},{8,11},{9,10},{10,... | collective-permute-start | bytes 442376 | tf_op jit(solution)/shard_map/cond/branch_1_fun/ppermute | solution.py:806
  (46 other events, 809.4 us)
Sparse Core Ops, SparseCore 0:
  13.8 115.0 all-gather.2

commit v3 on v2

--- a/solution.py
+++ b/solution.py
@@ -414,6 +414,7 @@
             pltpu.VMEM((count, D), jnp.float32),
             pltpu.VMEM((count, D), jnp.float32),
         ],
+        768 if count <= 4 * CAP else 512,
     )
     return (result[:senders], result[senders : 2 * senders]) + tuple(result[2 * senders :])
 

time: 682 us -> 681 us (level)
  no operation moved by 1% of the time
where the time goes in v3:
time: 681 us; the launch traced here: 670 us
  Pallas kernels  362 us (53%)
  local copies, waits for them, and re-layouts  71.1 us (10%)
  waiting for transfers between devices  68.7 us (10%)
  starting transfers between devices  64.1 us (9%)
  other arithmetic  51.4 us (8%)
  matrix products  34.2 us (5%)
  between operations  15.9 us (2%)
    pallas_call x8, Pallas kernels, outer_call(): pl.pallas_call(lambda *refs: kernel(came is not None, *refs), grid_spec=p...  98.9 us
    pallas_call x3, Pallas kernels, ffn_call(): pl.pallas_call(kernel, grid=(ff // width,), in_specs=specs + (w_specs or...  95.5 us
    pallas_call x1, Pallas kernels, gather(): pl.pallas_call(lambda *refs: gather_kernel(n_dp, n_ex, *refs), in_specs=[...  53.2 us
    pallas_call x1, Pallas kernels, attend_back(): pl.pallas_call(attend_back_kernel, grid=(PAIRS,), in_specs=[pl.BlockSpec(...  42.5 us
    ppermute x24, waiting for transfers between devices, to_expert(): lax.ppermute(blocks[distance], 'expert', [(i, i ^ distance) for i in rang...  32.4 us
    ppermute x24, starting transfers between devices, to_expert(): lax.ppermute(blocks[distance], 'expert', [(i, i ^ distance) for i in rang...  31.1 us
    pallas_call x1, Pallas kernels, attend(): pl.pallas_call(attend_kernel, grid=(PAIRS,), in_specs=[pl.BlockSpec(memor...  27 us
    ppermute x6, waiting for transfers between devices, from_expert(): lax.ppermute(at_place(parts, me ^ distance), 'expert', route)  26.6 us
  transfers between devices with their start and end apart: 47, of which 12 were waited for; matrix products, arithmetic and copies ran while one was open for 15% of the time, Pallas kernels for 51%

profile of v3, /device:TPU:8, one launch (start us, length us, event | category | flops | bytes accessed | tf_op | source)
XLA Modules:
  0.0 670.3 jit_solution(5128082649765596512)
XLA Ops:
  17.1 6.0 all-to-all-start
  28.7 6.3 all-to-all-done
  38.6 5.5 all-to-all-start.1
  45.4 53.2 %gather.1 = bf16[32,24,2304]{2,1,0:T(8,128)(2,1)} custom-call(bf16[24,2304]{1,0:T(8,128)(2,1)} %broadcast_add_fusion.refs_0_), custom_call_target="tpu_custom_call" | custom-call | bytes 3538944 | tf_op jit(solution)/shard_map/gather/pallas_call | solution.py:782
  104.5 5.4 convolution_convert_fusion.1
  109.9 45.9 %conditional.11 = (bf16[1024,768]{1,0:T(8,128)(2,1)}, f32[6,2,1024]{2,1,0:T(2,128)S(1)}, bf16[288,768]{1,0:T(8,128)(2,1)}, bf16[288,768]{1,0:T(8,128)(2,1)}, bf1...) conditional(s32[]{:T(128)} %bitcast.60, () %tuple.132, ...), branch_computations={%region_4.5_spmd, %region_5.6_spmd} | conditional | flops 14701266944 | bytes 29157716 | solution.py:815
  116.5 27.0 %attend.1 = (bf16[1024,768]{1,0:T(8,128)(2,1)}, f32[6,2,1024]{2,1,0:T(2,128)S(1)}) custom-call(s32[4]{0:T(128)S(1)} %get-tuple-element.350.length_ref, bf16[1024,2304]{1,0:T(8,128)(2,1)} %get-tuple-element.351.q_ref.k_ref.v_ref, bf16[1024,2304]{1,0:T(8,128)(2,1)} %get-tuple-element.351.q_ref.k_ref.v_ref, bf16[1024,2304]{1,0:T(8,128)(2,1)} %get-tuple-element.351.q_ref.k_ref.v_ref), custom_call_target="tpu_custom_call" | custom-call | flops 12884901888 | bytes 6291456 | tf_op jit(solution)/shard_map/cond/branch_1_fun/attend/pallas_call | solution.py:167
  148.8 6.5 collective-permute-done.33
  163.7 4.2 fusion.49
  174.8 9.0 %dispatch.1 = (bf16[304,768]{1,0:T(8,128)(2,1)}, bf16[304,768]{1,0:T(8,128)(2,1)}, bf16[304,768]{1,0:T(8,128)(2,1)}, bf16[304,768]{1,0:T(8,128)(2,1)}, bf16[304,...) custom-call(s32[2432,1]{1,0:T(8,128)} %select_n.208.refs_0_, ...), custom_call_target="tpu_custom_call" | custom-call | flops 3825205248 | bytes 5308416 | tf_op jit(solution)/shard_map/dispatch/pallas_call | solution.py:694
  183.8 44.4 %conditional.12 = (f32[1024,768]{1,0:T(8,128)}, f32[1024,768]{1,0:T(8,128)}, bf16[1024,3072]{1,0:T(8,128)(2,1)}, bf16[1024,3072]{1,0:T(8,128)(2,1)}, bf16[768,10...) conditional(s32[]{:T(128)} %bitcast.60, () %tuple.131, ...), branch_computations={%region_11.12_spmd, %region_12.13_spmd} | conditional | flops 24159191040 | bytes 52789596 | solution.py:815
  187.5 28.1 %shared_expert.1 = (f32[1024,768]{1,0:T(8,128)}, f32[1024,768]{1,0:T(8,128)}, bf16[1024,3072]{1,0:T(8,128)(2,1)}, bf16[1024,3072]{1,0:T(8,128)(2,1)}, bf16[768,1024]{1,0:T(8,128)(2,1)}) custom-call(bf16[1024,768]{1,0:T(8,128)(2,1)S(1)} %get-tuple-element.363.rows_ref, bf16[1024,768]{1,0:T(8,128)(2,1)S(1)} %get-tuple-element.364.grad_ref.refs_2_, ...), custom_call_target="tpu_custom_call" | custom-call | flops 19327352832 | bytes 22020096 | tf_op jit(solution)/shard_map/cond/branch_1_fun/shared_expert/pallas_call | solution.py:344
  215.7 12.5 %expert_outer.6 = bf16[4,768,768]{2,1,0:T(8,128)(2,1)} custom-call(s32[1]{0:T(128)} %bitcast.1.refs_0_, bf16[1024,3072]{1,0:T(8,128)(2,1)} %get-tuple-element.1161.refs_1_, bf16[1024,768]{1,0:T(8,128)(2,1)S(1)} %get-tuple-element.364.grad_ref.refs_2_, bf16[4,2,96,1024]{3,2,1,0:T(8,128)(2,1)} %bitcast.2.refs_3_, bf16[1024,3072]{1,0:T(8,128)(2,1)} %get-tuple-element.1162.refs_4_), custom_call_target="tpu_custom_call" | custom-call | flops 4831838208 | bytes 25165824 | tf_op jit(solution)/shard_map/cond/branch_1_fun/expert_outer/pallas_call | solution.py:470
  228.2 51.6 %conditional.13 = (bf16[288,768]{1,0:T(8,128)(2,1)}, bf16[288,768]{1,0:T(8,128)(2,1)}, bf16[288,768]{1,0:T(8,128)(2,1)}, bf16[288,768]{1,0:T(8,128)(2,1)}, bf16[...) conditional(s32[]{:T(128)} %bitcast.60, () %tuple.130, ...), branch_computations={%region_13.14_spmd, %region_14.15_spmd} | conditional | flops 27179089920 | bytes 56328596 | solution.py:815
  232.2 33.7 %routed_expert.2 = (bf16[288,768]{1,0:T(8,128)(2,1)}, bf16[288,768]{1,0:T(8,128)(2,1)}, bf16[288,768]{1,0:T(8,128)(2,1)}, bf16[288,768]{1,0:T(8,128)(2,1)}, bf16...) custom-call(bf16[304,768]{1,0:T(8,128)(2,1)} %get-tuple-element.376., ...), custom_call_target="tpu_custom_call" | custom-call | flops 21743271936 | bytes 23592960 | tf_op jit(solution)/shard_map/cond/branch_1_fun/routed_expert/pallas_call | solution.py:344
  265.9 13.9 %expert_outer.7 = bf16[4,768,768]{2,1,0:T(8,128)(2,1)} custom-call(s32[1]{0:T(128)} %bitcast.3.refs_0_, bf16[1152,3072]{1,0:T(8,128)(2,1)} %get-tuple-element.1194.refs_1_, bf16[1152,768]{1,0:T(8,128)(2,1)} %get-tuple-element.1196.refs_2_, bf16[4,2,96,1152]{3,2,1,0:T(8,128)(2,1)} %bitcast.4.refs_3_, bf16[1152,3072]{1,0:T(8,128)(2,1)} %get-tuple-element.1195.refs_4_), custom_call_target="tpu_custom_call" | custom-call | flops 5435817984 | bytes 27131904 | tf_op jit(solution)/shard_map/cond/branch_1_fun/expert_outer/pallas_call | solution.py:470
  279.8 39.7 %conditional.14 = (bf16[4,768,768]{2,1,0:T(8,128)(2,1)}, bf16[4,768,768]{2,1,0:T(8,128)(2,1)}, bf16[288,768]{1,0:T(8,128)(2,1)}, bf16[288,768]{1,0:T(8,128)(2,1)...) conditional(s32[]{:T(128)} %bitcast.60, () %tuple.136, (bf16[768,1152]{1,0:T(8,128)(2,1)}, ...), branch_computations={%region_15.16_spmd, %region_16.17_spmd} | conditional | flops 10267656192 | bytes 95355272 | solution.py:815
  288.1 14.7 %expert_outer.8.refs_7_ = bf16[4,768,768]{2,1,0:T(8,128)(2,1)} custom-call(s32[1]{0:T(128)} %bitcast.5.refs_0_, bf16[1152,3072]{1,0:T(8,128)(2,1)} %get-tuple-element.402.refs_1_, bf16[1152,768]{1,0:T(8,128)(2,1)} %get-tuple-element.403.refs_2_, bf16[4,2,96,1152]{3,2,1,0:T(8,128)(2,1)} %bitcast.6.refs_3_, bf16[1152,3072]{1,0:T(8,128)(2,1)} %get-tuple-element.405.refs_4_, ...), custom_call_target="tpu_custom_call" | custom-call | flops 5435817984 | bytes 27131904 | tf_op jit(solution)/shard_map/cond/branch_1_fun/expert_outer/pallas_call | solution.py:470
  302.8 13.3 %expert_outer.9 = bf16[4,768,768]{2,1,0:T(8,128)(2,1)} custom-call(s32[1]{0:T(128)} %bitcast.5.refs_0_, bf16[1024,3072]{1,0:T(8,128)(2,1)} %get-tuple-element.407.refs_1_, bf16[1024,768]{1,0:T(8,128)(2,1)S(1)} %get-tuple-element.408.refs_2_, bf16[4,2,96,1024]{3,2,1,0:T(8,128)(2,1)} %bitcast.7.refs_3_, bf16[1024,3072]{1,0:T(8,128)(2,1)} %get-tuple-element.410.refs_4_, ...), custom_call_target="tpu_custom_call" | custom-call | flops 4831838208 | bytes 25165824 | tf_op jit(solution)/shard_map/cond/branch_1_fun/expert_outer/pallas_call | solution.py:470
  319.4 63.7 %conditional.15 = (bf16[288,768]{1,0:T(8,128)(2,1)}, bf16[288,768]{1,0:T(8,128)(2,1)}, bf16[288,768]{1,0:T(8,128)(2,1)}, bf16[288,768]{1,0:T(8,128)(2,1)}, bf16[...) conditional(s32[]{:T(128)} %bitcast.60, () %tuple.129, ...), branch_computations={%region_17.18_spmd, %region_18.19_spmd} | conditional | flops 27193245696 | bytes 105382632 | solution.py:815
  319.6 4.5 dynamic-slice_bitcast_fusion
  335.5 33.7 %routed_expert.3 = (bf16[288,768]{1,0:T(8,128)(2,1)}, bf16[288,768]{1,0:T(8,128)(2,1)}, bf16[288,768]{1,0:T(8,128)(2,1)}, bf16[288,768]{1,0:T(8,128)(2,1)}, bf16...) custom-call(bf16[304,768]{1,0:T(8,128)(2,1)S(1)} %copy-done.46, ...), custom_call_target="tpu_custom_call" | custom-call | flops 21743271936 | bytes 23592960 | tf_op jit(solution)/shard_map/cond/branch_1_fun/routed_expert/pallas_call | solution.py:344
  369.2 13.8 %expert_outer.10 = bf16[4,768,768]{2,1,0:T(8,128)(2,1)} custom-call(s32[1]{0:T(128)} %bitcast.8.refs_0_, bf16[1152,3072]{1,0:T(8,128)(2,1)} %get-tuple-element.1243.refs_1_, bf16[1152,768]{1,0:T(8,128)(2,1)} %get-tuple-element.1245.refs_2_, bf16[4,2,96,1152]{3,2,1,0:T(8,128)(2,1)} %bitcast.9.refs_3_, bf16[1152,3072]{1,0:T(8,128)(2,1)} %get-tuple-element.1244.refs_4_), custom_call_target="tpu_custom_call" | custom-call | flops 5435817984 | bytes 27131904 | tf_op jit(solution)/shard_map/cond/branch_1_fun/expert_outer/pallas_call | solution.py:470
  384.5 49.7 %conditional.16 = (bf16[4,768,768]{2,1,0:T(8,128)(2,1)}, bf16[304,768]{1,0:T(8,128)(2,1)}, bf16[304,768]{1,0:T(8,128)(2,1)}, bf16[304,768]{1,0:T(8,128)(2,1)}, b...) conditional(s32[]{:T(128)} %bitcast.60, () %tuple.141, ...), branch_computations={%region_19.20_spmd, %region_20.21_spmd} | conditional | flops 5435817984 | bytes 64979472 | solution.py:815
  393.3 3.9 turn.2
  397.2 3.9 turn.3
  401.1 14.8 %expert_outer.11 = bf16[4,768,768]{2,1,0:T(8,128)(2,1)} custom-call(s32[1]{0:T(128)} %bitcast.16.refs_0_, bf16[1152,3072]{1,0:T(8,128)(2,1)} %get-tuple-element.444.refs_1_, bf16[1152,768]{1,0:T(8,128)(2,1)} %get-tuple-element.445.refs_2_, bf16[4,2,96,1152]{3,2,1,0:T(8,128)(2,1)} %bitcast.17.refs_3_, bf16[1152,3072]{1,0:T(8,128)(2,1)} %get-tuple-element.447.refs_4_, ...), custom_call_target="tpu_custom_call" | custom-call | flops 5435817984 | bytes 27131904 | tf_op jit(solution)/shard_map/cond/branch_1_fun/expert_outer/pallas_call | solution.py:470
  415.8 7.5 %collective-permute-done.18 = bf16[304,768]{1,0:T(8,128)(2,1)} collective-permute-done((bf16[304,768]{1,0:T(8,128)(2,1)}, bf16[304,768]{1,0:T(8,128)(2,1)}, u32[]{:S(2)}, u32[]{:S(2)}) %collective-permute-start.18) | collective-permute-done | bytes 466976 | tf_op jit(solution)/shard_map/cond/branch_1_fun/ppermute | solution.py:821
  423.4 10.9 %collective-permute-done.19 = bf16[304,768]{1,0:T(8,128)(2,1)} collective-permute-done((bf16[304,768]{1,0:T(8,128)(2,1)}, bf16[304,768]{1,0:T(8,128)(2,1)}, u32[]{:S(2)}, u32[]{:S(2)}) %collective-permute-start.19) | collective-permute-done | bytes 466976 | tf_op jit(solution)/shard_map/cond/branch_1_fun/ppermute | solution.py:821
  434.3 46.6 %conditional.17 = (bf16[768,8]{0,1:T(8,128)(2,1)S(1)}, f32[4,768]{1,0:T(4,128)S(1)}, f32[4,768]{1,0:T(4,128)S(1)}, f32[4,768]{1,0:T(4,128)S(1)}, f32[1024,768]{1...) conditional(s32[]{:T(128)} %bitcast.60, () %tuple.140, ...), branch_computations={%region_21.22_spmd, %region_22.30_spmd} | conditional | flops 6332856320 | bytes 93014016 | solution.py:815
  446.7 10.7 %combine.2 = (f32[1024,768]{1,0:T(8,128)}, f32[1024,2]{1,0:T(8,128)}) custom-call(s32[1,2432]{1,0:T(1,128)} %select_n.166.refs_0_, s32[1024,2]{1,0:T(8,128)} %copy.94.refs_1_, f32[1024,768]{1,0:T(8,128)} %get-tuple-element.461.refs_2_, bf16[304,768]{1,0:T(8,128)(2,1)} %get-tuple-element.462.refs_3_, bf16[304,768]{1,0:T(8,128)(2,1)} %get-tuple-element.463.refs_4_, ...), custom_call_target="tpu_custom_call" | custom-call | flops 3825205248 | bytes 10027008 | tf_op jit(solution)/shard_map/cond/branch_1_fun/combine/pallas_call | solution.py:609
  469.1 4.0 convolution_convert_fusion
  476.8 4.1 collective-permute-done.36
  481.5 67.5 %conditional.18 = (bf16[1024,2304]{1,0:T(8,128)(2,1)}, bf16[4,384,768]{2,1,0:T(8,128)(2,1)}, bf16[288,768]{1,0:T(8,128)(2,1)}, bf16[288,768]{1,0:T(8,128)(2,1)},...) conditional(s32[]{:T(128)} %bitcast.60, () %tuple.139, ...), branch_computations={%region_30.31_spmd, %region_31.32_spmd} | conditional | flops 34639970304 | bytes 76874376 | solution.py:815
  492.8 42.5 %attend_back.1.refs_3_ = bf16[1024,2304]{1,0:T(8,128)(2,1)} custom-call(s32[4]{0:T(128)S(1)} %copy-done.45, bf16[1024,2304]{1,0:T(8,128)(2,1)} %get-tuple-element.487.q_ref.k_ref.v_ref, bf16[1024,2304]{1,0:T(8,128)(2,1)} %get-tuple-element.487.q_ref.k_ref.v_ref, bf16[1024,2304]{1,0:T(8,128)(2,1)} %get-tuple-element.487.q_ref.k_ref.v_ref, ...), custom_call_target="tpu_custom_call" | custom-call | flops 32212254720 | bytes 12582912 | tf_op jit(solution)/shard_map/cond/branch_1_fun/attend_back/pallas_call | solution.py:193
  541.4 7.6 %attention_outer.2 = bf16[4,384,768]{2,1,0:T(8,128)(2,1)} custom-call(s32[1]{0:T(128)} %bitcast.29.refs_0_, bf16[4,2,96,1024]{3,2,1,0:T(8,128)(2,1)} %bitcast.30.refs_1_, bf16[4,2,96,1024]{3,2,1,0:T(8,128)(2,1)} %bitcast.31.refs_2_, bf16[1024,2304]{1,0:T(8,128)(2,1)} %attend_back.1.refs_3_, bf16[1024,768]{1,0:T(8,128)(2,1)} %get-tuple-element.493.refs_4_), custom_call_target="tpu_custom_call" | custom-call | flops 2415919104 | bytes 14155776 | tf_op jit(solution)/shard_map/cond/branch_1_fun/attention_outer/pallas_call | solution.py:470
  549.1 44.5 %conditional.19 = (bf16[1024,768]{1,0:T(8,128)(2,1)}, f32[4,768]{1,0:T(4,128)S(1)}, f32[4,768]{1,0:T(4,128)S(1)}, bf16[4,384,768]{2,1,0:T(8,128)(2,1)}, f32[192,...) conditional(s32[]{:T(128)} %bitcast.60, () %tuple.145, ...), branch_computations={%region_32.33_spmd, %region_33.40_spmd} | conditional | flops 6063634432 | bytes 77820512 | solution.py:815
  554.6 7.2 %fusion.11 = (f32[1024]{0:T(1024)S(1)}, f32[1024]{0:T(1024)S(1)}, f32[1024,768]{1,0:T(8,128)S(1)}) fusion(f32[4,768]{1,0:T(4,128)S(1)} %slice_add_fusion, f32[1024]{0:T(1024)S(1)} %add_rsqrt_fusion, f32[1024]{0:T(1024)S(1)} %broadcast_multiply_fusion.2, bf16[1024,768]{1,0:T(8,128)(2,1)S(1)} %get-tuple-element.505, ...), kind=kOutput, calls=%fused_computation.31 | convolution fusion | flops 3629381632 | bytes 13004800 | tf_op jit(solution)/shard_map/cond/branch_1_fun/dot_general | solution.py:34
  564.4 4.3 fusion.9
  572.3 7.5 %collective-permute-done.42 = bf16[192,768]{1,0:T(8,128)(2,1)} collective-permute-done((bf16[192,768]{1,0:T(8,128)(2,1)S(1)}, bf16[192,768]{1,0:T(8,128)(2,1)}, u32[]{:S(2)}, u32[]{:S(2)}) %collective-permute-start.42) | collective-permute-done | bytes 294944 | tf_op jit(solution)/shard_map/cond/branch_1_fun/ppermute | solution.py:807
  585.2 8.3 %attention_outer.3 = bf16[4,384,768]{2,1,0:T(8,128)(2,1)} custom-call(s32[1]{0:T(128)} %bitcast.40.refs_0_, bf16[4,2,96,1024]{3,2,1,0:T(8,128)(2,1)} %bitcast.41.refs_1_, bf16[4,2,96,1024]{3,2,1,0:T(8,128)(2,1)} %bitcast.42.refs_2_, bf16[1024,2304]{1,0:T(8,128)(2,1)} %get-tuple-element.506.refs_3_, bf16[1024,768]{1,0:T(8,128)(2,1)} %get-tuple-element.511.refs_4_, ...), custom_call_target="tpu_custom_call" | custom-call | flops 2415919104 | bytes 14155776 | tf_op jit(solution)/shard_map/cond/branch_1_fun/attention_outer/pallas_call | solution.py:470
  593.6 35.8 %conditional.20 = (f32[2,384,768]{2,1,0:T(8,128)}, f32[2,96,3072]{2,1,0:T(8,128)}, bf16[1024,768]{1,0:T(8,128)(2,1)}, f32[4,768]{1,0:T(4,128)S(1)}, f32[384,768]...) conditional(s32[]{:T(128)} %bitcast.60, () %tuple.128, ...), branch_computations={%region_40.41_spmd, %region_41.43_spmd} | conditional | flops 3630368512 | bytes 77951240 | solution.py:815
  601.8 9.0 %combine.3 = (f32[1024,768]{1,0:T(8,128)}, f32[1024,2]{1,0:T(8,128)}) custom-call(s32[1,2304]{1,0:T(1,128)} %select_n.182.refs_0_, s32[1024,2]{1,0:T(8,128)} %copy.97.refs_1_, f32[1024,768]{1,0:T(8,128)} %get-tuple-element.528.refs_2_, bf16[288,768]{1,0:T(8,128)(2,1)} %get-tuple-element.529.refs_3_, bf16[288,768]{1,0:T(8,128)(2,1)} %get-tuple-element.530.refs_4_, ...), custom_call_target="tpu_custom_call" | custom-call | flops 3623878656 | bytes 9830400 | tf_op jit(solution)/shard_map/cond/branch_1_fun/combine/pallas_call | solution.py:609
  614.2 8.2 %expert_sums.1 = (f32[2,384,768]{2,1,0:T(8,128)}, f32[2,96,3072]{2,1,0:T(8,128)}) custom-call(bf16[1536,768]{1,0:T(8,128)(2,1)} %get-tuple-element.514.refs_0_, bf16[1536,768]{1,0:T(8,128)(2,1)} %get-tuple-element.515.refs_1_, bf16[1536,768]{1,0:T(8,128)(2,1)} %get-tuple-element.516.refs_2_, bf16[1536,768]{1,0:T(8,128)(2,1)} %get-tuple-element.517.refs_3_.refs_7_, ...), custom_call_target="tpu_custom_call" | custom-call | bytes 18874368 | tf_op jit(solution)/shard_map/cond/branch_1_fun/expert_sums/pallas_call | solution.py:661
  637.0 22.5 %conditional.21 = (f32[96,768]{1,0:T(8,128)S(1)}, f32[96,768]{1,0:T(8,128)S(1)}, f32[96,768]{1,0:T(8,128)S(1)}, f32[96,768]{1,0:T(8,128)}, f32[96,576]{1,0:T(8,128)S(1)}, /*index=5*/f32[96,192]{1,0:T(8,128)S(1)}) conditional(s32[]{:T(128)} %bitcast.60, () %tuple.148, bf16[4,96,768]{1,2,0:T(8,128)(2,1)S(1)} %maximum_bitcast_fusion), branch_computations={%region_43.44_spmd, %region_44.45_spmd} | conditional | flops 516113 | bytes 6488440 | solution.py:815
  641.3 4.5 collective-permute-done.24
  645.9 5.9 collective-permute-done.25
  651.8 5.0 collective-permute-done.26
  (366 shorter events, 190.1 us)
Async XLA Ops:
  7.2 148.6 %all-gather.3.cloned.1.call-start = ((), (), s32[]{:S(2)}) async-start(), calls=%async_computation.3 | async-start | bytes 11354112 | tf_op jit(solution)/shard_map/all_gather | solution.py:894
  17.1 17.8 %all-to-all-start = ((bf16[32,2,1800]{2,1,0:T(2,128)(2,1)}), bf16[32,2,1800]{2,1,0:T(2,128)(2,1)S(1)}, u32[]{:S(2)}, u32[]{:S(2)}) async-start(bf16[32,2,1800]{2,1,0:T(2,128)(2,1)} %reshape.854), calls=%async_computation | async-start | bytes 491520 | tf_op jit(solution)/shard_map/all_to_all | solution.py:795
  23.3 86.6 %copy-start.39 = (s32[4]{0:T(128)}, s32[4]{0:T(128)S(1)}, u32[]{:S(2)}) copy-start(s32[4]{0:T(128)S(1)} %get-tuple-element.1060) | copy-start | bytes 52
  38.6 60.0 %all-to-all-start.1 = ((f32[32,4,144]{2,1,0:T(4,128)}), f32[32,4,144]{2,1,0:T(4,128)S(1)}, u32[]{:S(2)}, u32[]{:S(2)}) async-start(f32[32,4,144]{2,1,0:T(4,128)} %reshape.817), calls=%async_computation.1 | async-start | bytes 262144 | tf_op jit(solution)/shard_map/all_to_all | solution.py:795
  111.0 37.8 %collective-permute-start.31 = (bf16[288,768]{1,0:T(8,128)(2,1)}, bf16[288,768]{1,0:T(8,128)(2,1)}, u32[]{:S(2)}, u32[]{:S(2)}) collective-permute-start(bf16[288,768]{1,0:T(8,128)(2,1)} %slice.235), channel_id=1, source_target_pairs={{0,1},{1,0},{2,3},{3,2},{4,5},{5,4},{6,7},{7,6},{8,9},{9,8},{10,11... | collective-permute-start | bytes 1327112 | tf_op jit(solution)/shard_map/cond/branch_1_fun/ppermute | solution.py:821
  111.8 37.0 %collective-permute-start.32 = (bf16[288,768]{1,0:T(8,128)(2,1)}, bf16[288,768]{1,0:T(8,128)(2,1)}, u32[]{:S(2)}, u32[]{:S(2)}) collective-permute-start(bf16[288,768]{1,0:T(8,128)(2,1)} %slice.236), channel_id=1, source_target_pairs={{0,2},{1,3},{2,0},{3,1},{4,6},{5,7},{6,4},{7,5},{8,10},{9,11},{10,... | collective-permute-start | bytes 1327112 | tf_op jit(solution)/shard_map/cond/branch_1_fun/ppermute | solution.py:821
  114.7 40.6 %collective-permute-start.33 = (bf16[288,768]{1,0:T(8,128)(2,1)}, bf16[288,768]{1,0:T(8,128)(2,1)}, u32[]{:S(2)}, u32[]{:S(2)}) collective-permute-start(bf16[288,768]{1,0:T(8,128)(2,1)} %slice.237), channel_id=1, source_target_pairs={{0,3},{1,2},{2,1},{3,0},{4,7},{5,6},{6,5},{7,4},{8,11},{9,10},{10,... | collective-permute-start | bytes 1327112 | tf_op jit(solution)/shard_map/cond/branch_1_fun/ppermute | solution.py:821
  184.0 44.2 %collective-permute-start = (bf16[304,768]{1,0:T(8,128)(2,1)}, bf16[304,768]{1,0:T(8,128)(2,1)}, u32[]{:S(2)}, u32[]{:S(2)}) collective-permute-start(bf16[304,768]{1,0:T(8,128)(2,1)} %get-tuple-element.373), channel_id=1, source_target_pairs={{0,1},{1,0},{2,3},{3,2},{4,5},{5,4},{6,7},{7,6},{8,9},{9,8},{10,11... | collective-permute-start | bytes 1400840 | tf_op jit(solution)/shard_map/cond/branch_1_fun/ppermute | solution.py:821
  184.1 44.1 %collective-permute-start.1 = (bf16[304,768]{1,0:T(8,128)(2,1)}, bf16[304,768]{1,0:T(8,128)(2,1)}, u32[]{:S(2)}, u32[]{:S(2)}) collective-permute-start(bf16[304,768]{1,0:T(8,128)(2,1)} %get-tuple-element.374), channel_id=1, source_target_pairs={{0,2},{1,3},{2,0},{3,1},{4,6},{5,7},{6,4},{7,5},{8,10},{9,11},{10,... | collective-permute-start | bytes 1400840 | tf_op jit(solution)/shard_map/cond/branch_1_fun/ppermute | solution.py:821
  186.1 42.1 %collective-permute-start.2 = (bf16[304,768]{1,0:T(8,128)(2,1)}, bf16[304,768]{1,0:T(8,128)(2,1)}, u32[]{:S(2)}, u32[]{:S(2)}) collective-permute-start(bf16[304,768]{1,0:T(8,128)(2,1)} %get-tuple-element.375), channel_id=1, source_target_pairs={{0,3},{1,2},{2,1},{3,0},{4,7},{5,6},{6,5},{7,4},{8,11},{9,10},{10,... | collective-permute-start | bytes 1400840 | tf_op jit(solution)/shard_map/cond/branch_1_fun/ppermute | solution.py:821
  228.6 51.2 %collective-permute-start.3 = (bf16[304,768]{1,0:T(8,128)(2,1)}, bf16[304,768]{1,0:T(8,128)(2,1)}, u32[]{:S(2)}, u32[]{:S(2)}) collective-permute-start(bf16[304,768]{1,0:T(8,128)(2,1)} %get-tuple-element.399), channel_id=1, source_target_pairs={{0,1},{1,0},{2,3},{3,2},{4,5},{5,4},{6,7},{7,6},{8,9},{9,8},{10,11... | collective-permute-start | bytes 1400840 | tf_op jit(solution)/shard_map/cond/branch_1_fun/ppermute | solution.py:821
  229.6 50.1 %collective-permute-start.4 = (bf16[304,768]{1,0:T(8,128)(2,1)}, bf16[304,768]{1,0:T(8,128)(2,1)}, u32[]{:S(2)}, u32[]{:S(2)}) collective-permute-start(bf16[304,768]{1,0:T(8,128)(2,1)} %get-tuple-element.400), channel_id=1, source_target_pairs={{0,2},{1,3},{2,0},{3,1},{4,6},{5,7},{6,4},{7,5},{8,10},{9,11},{10,... | collective-permute-start | bytes 1400840 | tf_op jit(solution)/shard_map/cond/branch_1_fun/ppermute | solution.py:821
  230.7 49.0 %collective-permute-start.5 = (bf16[304,768]{1,0:T(8,128)(2,1)}, bf16[304,768]{1,0:T(8,128)(2,1)}, u32[]{:S(2)}, u32[]{:S(2)}) collective-permute-start(bf16[304,768]{1,0:T(8,128)(2,1)} %get-tuple-element.401), channel_id=1, source_target_pairs={{0,3},{1,2},{2,1},{3,0},{4,7},{5,6},{6,5},{7,4},{8,11},{9,10},{10,... | collective-permute-start | bytes 1400840 | tf_op jit(solution)/shard_map/cond/branch_1_fun/ppermute | solution.py:821
  279.8 8.3 %collective-permute-start.6 = (bf16[4,768,768]{2,1,0:T(8,128)(2,1)}, bf16[4,768,768]{2,1,0:T(8,128)(2,1)}, u32[]{:S(2)}, u32[]{:S(2)}) collective-permute-start(bf16[4,768,768]{2,1,0:T(8,128)(2,1)} %get-tuple-element.406), channel_id=1, source_target_pairs={{0,4},{4,0},{8,12},{12,8},{16,20},{20,16},{24,28},{28,24},{1,5},{5... | collective-permute-start | bytes 14155784 | tf_op jit(solution)/shard_map/cond/branch_1_fun/ppermute | solution.py:575
  279.9 23.0 %collective-permute-start.7 = (bf16[4,768,768]{2,1,0:T(8,128)(2,1)}, bf16[4,768,768]{2,1,0:T(8,128)(2,1)}, u32[]{:S(2)}, u32[]{:S(2)}) collective-permute-start(bf16[4,768,768]{2,1,0:T(8,128)(2,1)} %get-tuple-element.411), channel_id=1, source_target_pairs={{0,4},{4,0},{8,12},{12,8},{16,20},{20,16},{24,28},{28,24},{1,5},{5... | collective-permute-start | bytes 14155784 | tf_op jit(solution)/shard_map/cond/branch_1_fun/ppermute | solution.py:575
  280.4 35.7 %collective-permute-start.10 = (bf16[288,768]{1,0:T(8,128)(2,1)}, bf16[288,768]{1,0:T(8,128)(2,1)}, u32[]{:S(2)}, u32[]{:S(2)}) collective-permute-start(bf16[288,768]{1,0:T(8,128)(2,1)} %get-tuple-element.415), channel_id=1, source_target_pairs={{0,3},{1,2},{2,1},{3,0},{4,7},{5,6},{6,5},{7,4},{8,11},{9,10},{10,... | collective-permute-start | bytes 1327112 | tf_op jit(solution)/shard_map/cond/branch_1_fun/ppermute | solution.py:821
  281.0 35.1 %collective-permute-start.8 = (bf16[288,768]{1,0:T(8,128)(2,1)}, bf16[288,768]{1,0:T(8,128)(2,1)}, u32[]{:S(2)}, u32[]{:S(2)}) collective-permute-start(bf16[288,768]{1,0:T(8,128)(2,1)} %get-tuple-element.413), channel_id=1, source_target_pairs={{0,1},{1,0},{2,3},{3,2},{4,5},{5,4},{6,7},{7,6},{8,9},{9,8},{10,11... | collective-permute-start | bytes 1327112 | tf_op jit(solution)/shard_map/cond/branch_1_fun/ppermute | solution.py:821
  283.8 35.6 %collective-permute-start.9 = (bf16[288,768]{1,0:T(8,128)(2,1)}, bf16[288,768]{1,0:T(8,128)(2,1)}, u32[]{:S(2)}, u32[]{:S(2)}) collective-permute-start(bf16[288,768]{1,0:T(8,128)(2,1)} %get-tuple-element.414), channel_id=1, source_target_pairs={{0,2},{1,3},{2,0},{3,1},{4,6},{5,7},{6,4},{7,5},{8,10},{9,11},{10,... | collective-permute-start | bytes 1327112 | tf_op jit(solution)/shard_map/cond/branch_1_fun/ppermute | solution.py:821
  325.7 57.4 %collective-permute-start.14 = (bf16[1536,768]{1,0:T(8,128)(2,1)}, bf16[1536,768]{1,0:T(8,128)(2,1)}, u32[]{:S(2)}, u32[]{:S(2)}) collective-permute-start(bf16[1536,768]{1,0:T(8,128)(2,1)} %pad_maximum_fusion.1), channel_id=1, source_target_pairs={{0,8},{4,12},{8,0},{12,4},{16,24},{20,28},{24,16},{28,20},{1,9},{5... | collective-permute-start | bytes 7077896 | tf_op jit(solution)/shard_map/cond/branch_1_fun/ppermute | solution.py:834
  328.4 54.7 %collective-permute-start.15 = (bf16[1536,768]{1,0:T(8,128)(2,1)}, bf16[1536,768]{1,0:T(8,128)(2,1)}, u32[]{:S(2)}, u32[]{:S(2)}) collective-permute-start(bf16[1536,768]{1,0:T(8,128)(2,1)} %pad_maximum_fusion.2), channel_id=1, source_target_pairs={{0,16},{4,20},{8,24},{12,28},{16,0},{20,4},{24,8},{28,12},{1,17},{... | collective-permute-start | bytes 7077896 | tf_op jit(solution)/shard_map/cond/branch_1_fun/ppermute | solution.py:834
  329.3 53.8 %collective-permute-start.11 = (bf16[304,768]{1,0:T(8,128)(2,1)}, bf16[304,768]{1,0:T(8,128)(2,1)}, u32[]{:S(2)}, u32[]{:S(2)}) collective-permute-start(bf16[304,768]{1,0:T(8,128)(2,1)} %get-tuple-element.439), channel_id=1, source_target_pairs={{0,1},{1,0},{2,3},{3,2},{4,5},{5,4},{6,7},{7,6},{8,9},{9,8},{10,11... | collective-permute-start | bytes 1400840 | tf_op jit(solution)/shard_map/cond/branch_1_fun/ppermute | solution.py:821
  332.6 50.5 %collective-permute-start.12 = (bf16[304,768]{1,0:T(8,128)(2,1)}, bf16[304,768]{1,0:T(8,128)(2,1)}, u32[]{:S(2)}, u32[]{:S(2)}) collective-permute-start(bf16[304,768]{1,0:T(8,128)(2,1)} %get-tuple-element.440), channel_id=1, source_target_pairs={{0,2},{1,3},{2,0},{3,1},{4,6},{5,7},{6,4},{7,5},{8,10},{9,11},{10,... | collective-permute-start | bytes 1400840 | tf_op jit(solution)/shard_map/cond/branch_1_fun/ppermute | solution.py:821
  332.7 50.4 %collective-permute-start.13 = (bf16[304,768]{1,0:T(8,128)(2,1)}, bf16[304,768]{1,0:T(8,128)(2,1)}, u32[]{:S(2)}, u32[]{:S(2)}) collective-permute-start(bf16[304,768]{1,0:T(8,128)(2,1)} %get-tuple-element.441), channel_id=1, source_target_pairs={{0,3},{1,2},{2,1},{3,0},{4,7},{5,6},{6,5},{7,4},{8,11},{9,10},{10,... | collective-permute-start | bytes 1400840 | tf_op jit(solution)/shard_map/cond/branch_1_fun/ppermute | solution.py:821
  384.8 16.3 %collective-permute-start.16 = (bf16[4,768,768]{2,1,0:T(8,128)(2,1)}, bf16[4,768,768]{2,1,0:T(8,128)(2,1)}, u32[]{:S(2)}, u32[]{:S(2)}) collective-permute-start(bf16[4,768,768]{2,1,0:T(8,128)(2,1)} %get-tuple-element.448), channel_id=1, source_target_pairs={{0,4},{4,0},{8,12},{12,8},{16,20},{20,16},{24,28},{28,24},{1,5},{5... | collective-permute-start | bytes 14155784 | tf_op jit(solution)/shard_map/cond/branch_1_fun/ppermute | solution.py:575
  387.4 46.8 %collective-permute-start.20 = (bf16[768,768]{1,0:T(8,128)(2,1)}, bf16[768,768]{1,0:T(8,128)(2,1)}, u32[]{:S(2)}, u32[]{:S(2)}) collective-permute-start(bf16[768,768]{1,0:T(8,128)(2,1)} %dynamic-slice_bitcast_fusion.6), channel_id=1, source_target_pairs={{0,24},{4,28},{8,16},{12,20},{16,8},{20,12},{24,0},{28,4},{1,25},{... | collective-permute-start | bytes 3538952 | tf_op jit(solution)/shard_map/cond/branch_1_fun/ppermute | solution.py:834
  388.9 27.0 %collective-permute-start.17 = (bf16[304,768]{1,0:T(8,128)(2,1)}, bf16[304,768]{1,0:T(8,128)(2,1)}, u32[]{:S(2)}, u32[]{:S(2)}) collective-permute-start(bf16[304,768]{1,0:T(8,128)(2,1)} %get-tuple-element.450), channel_id=1, source_target_pairs={{0,1},{1,0},{2,3},{3,2},{4,5},{5,4},{6,7},{7,6},{8,9},{9,8},{10,11... | collective-permute-start | bytes 1400840 | tf_op jit(solution)/shard_map/cond/branch_1_fun/ppermute | solution.py:821
  391.8 31.5 %collective-permute-start.18 = (bf16[304,768]{1,0:T(8,128)(2,1)}, bf16[304,768]{1,0:T(8,128)(2,1)}, u32[]{:S(2)}, u32[]{:S(2)}) collective-permute-start(bf16[304,768]{1,0:T(8,128)(2,1)} %get-tuple-element.451), channel_id=1, source_target_pairs={{0,2},{1,3},{2,0},{3,1},{4,6},{5,7},{6,4},{7,5},{8,10},{9,11},{10,... | collective-permute-start | bytes 1400840 | tf_op jit(solution)/shard_map/cond/branch_1_fun/ppermute | solution.py:821
  391.9 42.3 %collective-permute-start.19 = (bf16[304,768]{1,0:T(8,128)(2,1)}, bf16[304,768]{1,0:T(8,128)(2,1)}, u32[]{:S(2)}, u32[]{:S(2)}) collective-permute-start(bf16[304,768]{1,0:T(8,128)(2,1)} %get-tuple-element.452), channel_id=1, source_target_pairs={{0,3},{1,2},{2,1},{3,0},{4,7},{5,6},{6,5},{7,4},{8,11},{9,10},{10,... | collective-permute-start | bytes 1400840 | tf_op jit(solution)/shard_map/cond/branch_1_fun/ppermute | solution.py:821
  438.3 42.7 %collective-permute-start.37 = (bf16[768,768]{1,0:T(8,128)(2,1)}, bf16[768,768]{1,0:T(8,128)(2,1)}, u32[]{:S(2)}, u32[]{:S(2)}) collective-permute-start(bf16[768,768]{1,0:T(8,128)(2,1)} %get-tuple-element.1097), channel_id=1, source_target_pairs={{0,8},{4,12},{8,0},{12,4},{16,24},{20,28},{24,16},{28,20},{1,9},{5... | collective-permute-start | bytes 3538952 | tf_op jit(solution)/shard_map/cond/branch_1_fun/ppermute | solution.py:834
  439.4 41.5 %collective-permute-start.38 = (bf16[768,768]{1,0:T(8,128)(2,1)}, bf16[768,768]{1,0:T(8,128)(2,1)}, u32[]{:S(2)}, u32[]{:S(2)}) collective-permute-start(bf16[768,768]{1,0:T(8,128)(2,1)} %get-tuple-element.1096), channel_id=1, source_target_pairs={{0,16},{4,20},{8,24},{12,28},{16,0},{20,4},{24,8},{28,12},{1,17},{... | collective-permute-start | bytes 3538952 | tf_op jit(solution)/shard_map/cond/branch_1_fun/ppermute | solution.py:834
  440.3 36.6 %collective-permute-start.34 = (bf16[288,768]{1,0:T(8,128)(2,1)}, bf16[288,768]{1,0:T(8,128)(2,1)}, u32[]{:S(2)}, u32[]{:S(2)}) collective-permute-start(bf16[288,768]{1,0:T(8,128)(2,1)} %get-tuple-element.482), channel_id=1, source_target_pairs={{0,1},{1,0},{2,3},{3,2},{4,5},{5,4},{6,7},{7,6},{8,9},{9,8},{10,11... | collective-permute-start | bytes 1327112 | tf_op jit(solution)/shard_map/cond/branch_1_fun/ppermute | solution.py:821
  440.3 36.6 %collective-permute-start.35 = (bf16[288,768]{1,0:T(8,128)(2,1)}, bf16[288,768]{1,0:T(8,128)(2,1)}, u32[]{:S(2)}, u32[]{:S(2)}) collective-permute-start(bf16[288,768]{1,0:T(8,128)(2,1)} %get-tuple-element.483), channel_id=1, source_target_pairs={{0,2},{1,3},{2,0},{3,1},{4,6},{5,7},{6,4},{7,5},{8,10},{9,11},{10,... | collective-permute-start | bytes 1327112 | tf_op jit(solution)/shard_map/cond/branch_1_fun/ppermute | solution.py:821
  442.4 38.5 %collective-permute-start.36 = (bf16[288,768]{1,0:T(8,128)(2,1)}, bf16[288,768]{1,0:T(8,128)(2,1)}, u32[]{:S(2)}, u32[]{:S(2)}) collective-permute-start(bf16[288,768]{1,0:T(8,128)(2,1)} %get-tuple-element.484), channel_id=1, source_target_pairs={{0,3},{1,2},{2,1},{3,0},{4,7},{5,6},{6,5},{7,4},{8,11},{9,10},{10,... | collective-permute-start | bytes 1327112 | tf_op jit(solution)/shard_map/cond/branch_1_fun/ppermute | solution.py:821
  485.3 63.8 %collective-permute-start.30 = (bf16[1536,768]{1,0:T(8,128)(2,1)}, bf16[1536,768]{1,0:T(8,128)(2,1)}, u32[]{:S(2)}, u32[]{:S(2)}) collective-permute-start(bf16[1536,768]{1,0:T(8,128)(2,1)} %pad_maximum_fusion.3), channel_id=1, source_target_pairs={{0,24},{4,28},{8,16},{12,20},{16,8},{20,12},{24,0},{28,4},{1,25},{... | collective-permute-start | bytes 7077896 | tf_op jit(solution)/shard_map/cond/branch_1_fun/ppermute | solution.py:834
  486.8 62.3 %collective-permute-start.27 = (bf16[288,768]{1,0:T(8,128)(2,1)}, bf16[288,768]{1,0:T(8,128)(2,1)}, u32[]{:S(2)}, u32[]{:S(2)}) collective-permute-start(bf16[288,768]{1,0:T(8,128)(2,1)} %get-tuple-element.495), channel_id=1, source_target_pairs={{0,1},{1,0},{2,3},{3,2},{4,5},{5,4},{6,7},{7,6},{8,9},{9,8},{10,11... | collective-permute-start | bytes 1327112 | tf_op jit(solution)/shard_map/cond/branch_1_fun/ppermute | solution.py:821
  486.8 62.3 %collective-permute-start.28 = (bf16[288,768]{1,0:T(8,128)(2,1)}, bf16[288,768]{1,0:T(8,128)(2,1)}, u32[]{:S(2)}, u32[]{:S(2)}) collective-permute-start(bf16[288,768]{1,0:T(8,128)(2,1)} %get-tuple-element.496), channel_id=1, source_target_pairs={{0,2},{1,3},{2,0},{3,1},{4,6},{5,7},{6,4},{7,5},{8,10},{9,11},{10,... | collective-permute-start | bytes 1327112 | tf_op jit(solution)/shard_map/cond/branch_1_fun/ppermute | solution.py:821
  488.9 60.2 %collective-permute-start.29 = (bf16[288,768]{1,0:T(8,128)(2,1)}, bf16[288,768]{1,0:T(8,128)(2,1)}, u32[]{:S(2)}, u32[]{:S(2)}) collective-permute-start(bf16[288,768]{1,0:T(8,128)(2,1)} %get-tuple-element.497), channel_id=1, source_target_pairs={{0,3},{1,2},{2,1},{3,0},{4,7},{5,6},{6,5},{7,4},{8,11},{9,10},{10,... | collective-permute-start | bytes 1327112 | tf_op jit(solution)/shard_map/cond/branch_1_fun/ppermute | solution.py:821
  549.3 35.9 %collective-permute-start.39 = (bf16[4,384,768]{2,1,0:T(8,128)(2,1)}, bf16[4,384,768]{2,1,0:T(8,128)(2,1)}, u32[]{:S(2)}, u32[]{:S(2)}) collective-permute-start(bf16[4,384,768]{2,1,0:T(8,128)(2,1)} %get-tuple-element.512), channel_id=1, source_target_pairs={{0,4},{4,0},{8,12},{12,8},{16,20},{20,16},{24,28},{28,24},{1,5},{5... | collective-permute-start | bytes 7077896 | tf_op jit(solution)/shard_map/cond/branch_1_fun/ppermute | solution.py:575
  550.2 18.5 %collective-permute-start.40 = (bf16[192,768]{1,0:T(8,128)(2,1)}, bf16[192,768]{1,0:T(8,128)(2,1)}, u32[]{:S(2)}, u32[]{:S(2)}) collective-permute-start(bf16[192,768]{1,0:T(8,128)(2,1)} %get-tuple-element.1080), channel_id=1, source_target_pairs={{0,1},{1,0},{2,3},{3,2},{4,5},{5,4},{6,7},{7,6},{8,9},{9,8},{10,11... | collective-permute-start | bytes 884744 | tf_op jit(solution)/shard_map/cond/branch_1_fun/ppermute | solution.py:807
  551.1 21.3 %collective-permute-start.41 = (bf16[192,768]{1,0:T(8,128)(2,1)S(1)}, bf16[192,768]{1,0:T(8,128)(2,1)}, u32[]{:S(2)}, u32[]{:S(2)}) collective-permute-start(bf16[192,768]{1,0:T(8,128)(2,1)S(1)} %get-tuple-element.1082), channel_id=1, source_target_pairs={{0,2},{1,3},{2,0},{3,1},{4,6},{5,7},{6,4},{7,5},{8,10},{9,11},{10,... | collective-permute-start | bytes 884744 | tf_op jit(solution)/shard_map/cond/branch_1_fun/ppermute | solution.py:807
  552.3 27.6 %collective-permute-start.42 = (bf16[192,768]{1,0:T(8,128)(2,1)S(1)}, bf16[192,768]{1,0:T(8,128)(2,1)}, u32[]{:S(2)}, u32[]{:S(2)}) collective-permute-start(bf16[192,768]{1,0:T(8,128)(2,1)S(1)} %get-tuple-element.1081), channel_id=1, source_target_pairs={{0,3},{1,2},{2,1},{3,0},{4,7},{5,6},{6,5},{7,4},{8,11},{9,10},{10,... | collective-permute-start | bytes 884744 | tf_op jit(solution)/shard_map/cond/branch_1_fun/ppermute | solution.py:807
  596.4 29.4 %collective-permute-start.21 = (bf16[384,768]{1,0:T(8,128)(2,1)}, bf16[384,768]{1,0:T(8,128)(2,1)}, u32[]{:S(2)}, u32[]{:S(2)}) collective-permute-start(bf16[384,768]{1,0:T(8,128)(2,1)} %get-tuple-element.1090), channel_id=1, source_target_pairs={{0,8},{4,12},{8,0},{12,4},{16,24},{20,28},{24,16},{28,20},{1,9},{5... | collective-permute-start | bytes 1769480 | tf_op jit(solution)/shard_map/cond/branch_1_fun/ppermute | solution.py:834
  597.6 28.2 %collective-permute-start.22 = (bf16[384,768]{1,0:T(8,128)(2,1)}, bf16[384,768]{1,0:T(8,128)(2,1)}, u32[]{:S(2)}, u32[]{:S(2)}) collective-permute-start(bf16[384,768]{1,0:T(8,128)(2,1)} %get-tuple-element.1089), channel_id=1, source_target_pairs={{0,16},{4,20},{8,24},{12,28},{16,0},{20,4},{24,8},{28,12},{1,17},{... | collective-permute-start | bytes 1769480 | tf_op jit(solution)/shard_map/cond/branch_1_fun/ppermute | solution.py:834
  598.4 26.3 %collective-permute-start.23 = (bf16[384,768]{1,0:T(8,128)(2,1)}, bf16[384,768]{1,0:T(8,128)(2,1)S(1)}, u32[]{:S(2)}, u32[]{:S(2)}) collective-permute-start(bf16[384,768]{1,0:T(8,128)(2,1)} %get-tuple-element.1088), channel_id=1, source_target_pairs={{0,24},{4,28},{8,16},{12,20},{16,8},{20,12},{24,0},{28,4},{1,25},{... | collective-permute-start | bytes 1769480 | tf_op jit(solution)/shard_map/cond/branch_1_fun/ppermute | solution.py:834
  631.4 28.1 %all-to-all-start.2 = ((bf16[32,39,128]{2,1,0:T(8,128)(2,1)}), bf16[32,39,128]{2,1,0:T(8,128)(2,1)S(1)}, u32[]{:S(2)}, u32[]{:S(2)}) async-start(bf16[32,39,128]{2,1,0:T(8,128)(2,1)} %reshape.830), calls=%async_computation.2 | async-start | bytes 655360 | tf_op jit(solution)/shard_map/all_to_all | solution.py:795
  637.2 8.6 %collective-permute-start.24 = (bf16[96,768]{1,0:T(8,128)(2,1)S(1)}, bf16[96,768]{1,0:T(8,128)(2,1)S(1)}, u32[]{:S(2)}, u32[]{:S(2)}) collective-permute-start(bf16[96,768]{1,0:T(8,128)(2,1)S(1)} %bitcast.229), channel_id=1, source_target_pairs={{0,1},{1,0},{2,3},{3,2},{4,5},{5,4},{6,7},{7,6},{8,9},{9,8},{10,11... | collective-permute-start | bytes 442376 | tf_op jit(solution)/shard_map/cond/branch_1_fun/ppermute | solution.py:807
  637.7 14.1 %collective-permute-start.25 = (bf16[96,768]{1,0:T(8,128)(2,1)S(1)}, bf16[96,768]{1,0:T(8,128)(2,1)S(1)}, u32[]{:S(2)}, u32[]{:S(2)}) collective-permute-start(bf16[96,768]{1,0:T(8,128)(2,1)S(1)} %bitcast.230), channel_id=1, source_target_pairs={{0,2},{1,3},{2,0},{3,1},{4,6},{5,7},{6,4},{7,5},{8,10},{9,11},{10,... | collective-permute-start | bytes 442376 | tf_op jit(solution)/shard_map/cond/branch_1_fun/ppermute | solution.py:807
  640.6 16.2 %collective-permute-start.26 = (bf16[96,768]{1,0:T(8,128)(2,1)S(1)}, bf16[96,768]{1,0:T(8,128)(2,1)S(1)}, u32[]{:S(2)}, u32[]{:S(2)}) collective-permute-start(bf16[96,768]{1,0:T(8,128)(2,1)S(1)} %bitcast.231), channel_id=1, source_target_pairs={{0,3},{1,2},{2,1},{3,0},{4,7},{5,6},{6,5},{7,4},{8,11},{9,10},{10,... | collective-permute-start | bytes 442376 | tf_op jit(solution)/shard_map/cond/branch_1_fun/ppermute | solution.py:807
  (46 other events, 809.5 us)
Sparse Core Ops, SparseCore 0:
  13.8 115.0 all-gather.2
